TPU v7x, 32 devices: a whole 2x2x4 slice. The times are simulated.
32 devices in a mesh: expert: 8 (over z, x), tensor: 4 (over y, core).
Axes of the slice: x: 2, y: 2, z: 4, core: 2. Of those that a mesh axis runs over, the one named last changes fastest.
Arguments:
- tokens: bfloat16 [2048, 4096], P('expert'), may hold values from -6 to 6
- cotangent: bfloat16 [2048, 4096], P('expert'), may hold values from -1.5 to 1.5
- w_in: bfloat16 [4096, 16384], P(None, ('expert', 'tensor')), may hold values from -0.09375 to 0.09375
- w_out: bfloat16 [16384, 4096], P(('expert', 'tensor')), may hold values from -0.09375 to 0.09375
- router: bfloat16 [4096, 4], replicated, may hold values from -0.09375 to 0.09375
- chosen: int32 [4, 512], replicated, may hold values from 0 to 2047, as said below
Outputs:
- grad_tokens: bfloat16 [2048, 4096], P('expert', 'tensor')
- grad_in: bfloat16 [4096, 16384], P(None, ('expert', 'tensor'))
- grad_out: bfloat16 [16384, 4096], P(('expert', 'tensor'))
- grad_router: float32 [4096, 4], replicated
Inputs may be any that keep to these rules, and one draw needn't show every extreme that they name: Row e lists, in increasing order, 512 distinct tokens chosen by expert e; at most 128 of them lie among one device's 256 consecutive tokens, and in every row some device's tokens hold exactly 128 of them.
All inputs are finite; a program needn't handle non-finite values.
Results may differ from a plain program's by a relative error of at most 0.005.
Values may be sent and summed in bfloat16 or wider, within the bound.
No kernel may reach another device: no remote copies, remote signals or barrier semaphores. Data moves between devices by JAX's collectives and lax.ppermute only.
A program may use at most 128 MiB of HBM per device.

v0:
```python
import jax
import jax.numpy as jnp
from jax import lax
from jax.sharding import PartitionSpec as P


def body(tokens, cotangent, w_in, w_out, router, chosen):
    tok_dev, features = tokens.shape
    n_expert = lax.axis_size("expert")
    bucket = 4 * tok_dev // n_expert
    capacity = chosen.shape[1]
    expert_total = router.shape[1]
    device_index = lax.axis_index("expert")
    expert = device_index // 2
    slot_range = jnp.arange(bucket, dtype=jnp.int32)
    first_token = device_index * tok_dev
    starts = jnp.sum((chosen < first_token).astype(jnp.int32), axis=1)
    run_ends = jnp.sum((chosen < first_token + tok_dev).astype(jnp.int32), axis=1)
    counts = run_ends - starts
    positions = jnp.minimum(starts[:, None] + slot_range[None, :], capacity - 1)
    picked = jnp.take_along_axis(chosen, positions, axis=1) - first_token
    filled = slot_range[None, :] < counts[:, None]
    local_rows = jnp.where(filled, picked, 0)
    owner_expert = jnp.arange(n_expert, dtype=jnp.int32) // 2
    send_rows = local_rows[owner_expert].reshape(-1)
    send_filled = filled[owner_expert].reshape(-1)

    def pack(source):
        gathered = jnp.where(send_filled[:, None], source[send_rows], jnp.zeros((), source.dtype))
        return gathered.reshape(n_expert, bucket, source.shape[1])

    got_x, got_y = (
        lax.all_to_all(pack(tokens), "expert", split_axis=0, concat_axis=0, tiled=True),
        lax.all_to_all(pack(cotangent), "expert", split_axis=0, concat_axis=0, tiled=True),
    )
    my_chosen = lax.dynamic_index_in_dim(chosen, expert, 0, keepdims=False)
    home_index = my_chosen // tok_dev
    bounds = jnp.arange(n_expert, dtype=jnp.int32) * tok_dev
    run_start = jnp.sum((my_chosen[None, :] < bounds[:, None]).astype(jnp.int32), axis=1)
    slot_index = home_index * bucket + jnp.arange(capacity, dtype=jnp.int32) - run_start[home_index]
    x_rows = got_x.reshape(-1, features)[slot_index]
    grad_rows = got_y.reshape(-1, features)[slot_index]
    r_col = lax.dynamic_slice_in_dim(router, expert, 1, 1)
    gate = jax.nn.sigmoid(jnp.dot(x_rows, r_col, preferred_element_type=jnp.float32)[:, 0])
    pre_act = jnp.dot(x_rows, w_in, preferred_element_type=jnp.float32)
    sig_act = jax.nn.sigmoid(pre_act)
    hidden = pre_act * sig_act
    upstream = jnp.dot(grad_rows, w_out.T, preferred_element_type=jnp.float32)
    gated_hidden = (gate[:, None] * hidden).astype(jnp.bfloat16)
    gate_grad = jnp.sum(hidden * upstream, axis=1)
    pre_grad = (gate[:, None] * upstream * sig_act * (1.0 + pre_act * (1.0 - sig_act))).astype(
        jnp.bfloat16
    )
    grad_out = jnp.dot(gated_hidden.T, grad_rows, preferred_element_type=jnp.float32).astype(
        jnp.bfloat16
    )
    grad_in = jnp.dot(x_rows.T, pre_grad, preferred_element_type=jnp.float32).astype(jnp.bfloat16)
    score_grad = gate_grad * gate * (1.0 - gate)
    router_col = jnp.dot(score_grad, x_rows.astype(jnp.float32), precision=lax.Precision.HIGHEST)
    router_term = (
        router_col[:, None] * (jnp.arange(expert_total) == expert).astype(jnp.float32)[None, :]
    )
    grad_router = lax.psum(router_term, ("expert", "tensor"))
    router_rows = r_col.astype(jnp.float32)
    summed = lax.psum_scatter(
        jnp.dot(w_in, pre_grad.T, preferred_element_type=jnp.float32)
        + router_rows * score_grad[None, :],
        "tensor",
        scatter_dimension=0,
        tiled=True,
    )
    share = summed.shape[0]
    outgoing = jnp.zeros((share, n_expert * bucket), jnp.float32).at[:, slot_index].set(summed)
    returned = lax.all_to_all(
        outgoing.reshape(share, n_expert, bucket), "expert", split_axis=1, concat_axis=1, tiled=True
    )
    returned = jnp.where(send_filled[None, :], returned.reshape(share, -1), 0.0)
    combined = jnp.zeros((share, tok_dev), jnp.float32).at[:, send_rows].add(returned)
    grad_tokens = combined.T.astype(jnp.bfloat16)
    return (grad_tokens, grad_in, grad_out, grad_router)


def solution(mesh):
    placed = (
        P("expert", None),
        P("expert", None),
        P(None, ("expert", "tensor")),
        P(("expert", "tensor"), None),
        P(),
        P(),
    )
    return jax.shard_map(
        body,
        mesh=mesh,
        in_specs=placed,
        out_specs=(
            P("expert", "tensor"),
            P(None, ("expert", "tensor")),
            P(("expert", "tensor"), None),
            P(),
        ),
        check_vma=False,
    )
```

profile of v0, /device:TPU:0, one launch (start us, length us, event | category | flops | bytes accessed | tf_op | source)
XLA Modules:
  0.0 724.6 jit_solution(17618018877152200852)
XLA Ops:
  9.1 5.0 gather_fusion.6
  14.9 7.7 %gather_fusion.2 = bf16[1024,4096]{1,0:T(8,128)(2,1)} fusion(bf16[256,4096]{1,0:T(8,128)(2,1)S(1)} %copy-done, s32[1024]{0:T(1024)S(1)} %broadcast_clamp_fusion), kind=kCustom, calls=%fused_computation.2 | custom fusion | bytes 16781312 | tf_op jit(solution)/shard_map/gather | solution.py:29
  22.6 16.9 %gather_fusion.4 = bf16[1024,4096]{1,0:T(8,128)(2,1)} fusion(bf16[256,4096]{1,0:T(8,128)(2,1)} %param.7, s32[1024]{0:T(1024)S(1)} %broadcast_clamp_fusion), kind=kCustom, calls=%fused_computation.4 | custom fusion | bytes 16781312 | tf_op jit(solution)/shard_map/gather | solution.py:29
  40.2 9.2 %broadcast_select_fusion = (bf16[8,128,4096]{2,1,0:T(8,128)(2,1)}, bf16[8,128,4096]{2,1,0:T(8,128)(2,1)S(1)}) fusion(bf16[8,128,4096]{2,1,0:T(8,128)(2,1)} %bitcast.68, pred[8,128]{1,0:T(8,128)(4,1)S(1)} %gather_fusion.1, bf16[8,128,4096]{2,1,0:T(8,128)(2,1)} %bitcast.67), kind=kLoop, calls=%fused_computation.10 | loop fusion | flops 8388608 | bytes 33555456 | tf_op jit(solution)/shard_map/jit(_where)/select_n | solution.py:29
  49.4 190.2 %all_to_all.15 = bf16[8,128,4096]{2,1,0:T(8,128)(2,1)} all-to-all(bf16[8,128,4096]{2,1,0:T(8,128)(2,1)S(1)} %get-tuple-element.11), channel_id=1, replica_groups=mesh['expert'=8,'tensor'=4] {'expert'}, dimensions={0} | all-to-all | bytes 16777216 | tf_op jit(solution)/shard_map/all_to_all | solution.py:33
  239.6 5.2 all-to-all-start.1
  245.8 4.4 compare_select_fusion.3
  250.8 13.2 %gather_fusion.3 = bf16[512,4096]{1,0:T(8,128)(2,1)} fusion(bf16[1024,4096]{1,0:T(8,128)(2,1)} %bitcast.66, s32[1024]{0:T(1024)S(1)} %pad_clamp_fusion), kind=kCustom, calls=%fused_computation.3 | custom fusion | bytes 8390656 | tf_op jit(solution)/shard_map/gather | solution.py:41
  264.1 3.5 fusion.9
  267.6 4.6 fusion.21
  272.2 154.8 %all-to-all-done.1 = bf16[8,128,4096]{2,1,0:T(8,128)(2,1)} async-done(((bf16[8,128,4096]{2,1,0:T(8,128)(2,1)}), bf16[8,128,4096]{2,1,0:T(8,128)(2,1)}, u32[]{:S(2)}, u32[]{:S(2)}) %all-to-all-start.1) | async-done | bytes 8388640 | tf_op jit(solution)/shard_map/all_to_all | solution.py:34
  427.0 13.0 %gather_fusion.5 = bf16[512,4096]{1,0:T(8,128)(2,1)} fusion(bf16[1024,4096]{1,0:T(8,128)(2,1)} %bitcast.23, s32[1024]{0:T(1024)S(1)} %pad_clamp_fusion), kind=kCustom, calls=%fused_computation.5 | custom fusion | bytes 8390656 | tf_op jit(solution)/shard_map/gather | solution.py:42
  440.0 6.3 multiply_reduce_fusion
  446.3 6.3 bitcast_add_fusion
  452.6 71.0 %reduce-scatter.2.cloned.1.call-done = f32[1024,512]{0,1:T(8,128)} async-done(((f32[4096,512]{0,1:T(8,128)}), f32[1024,512]{0,1:T(8,128)}) %reduce-scatter.2.cloned.1.call-update) | async-done | bytes 2097168 | tf_op jit(solution)/shard_map/reduce_scatter | solution.py:65
  523.5 5.6 scatter_custom_fusion
  529.2 5.5 all-to-all-start.2
  535.0 3.9 fusion.22
  539.7 6.8 convolution_convert_fusion.1
  546.4 4.4 convolution_convert_fusion
  550.8 77.8 %all-to-all-done.2 = f32[1024,8,128]{0,2,1:T(8,128)} async-done(((f32[1024,8,128]{0,2,1:T(8,128)}), f32[1024,8,128]{0,2,1:T(8,128)}, u32[]{:S(2)}, u32[]{:S(2)}) %all-to-all-start.2) | async-done | bytes 4194336 | tf_op jit(solution)/shard_map/all_to_all | solution.py:74
  628.6 4.7 bitcast_select_fusion
  633.3 10.3 %scatter_custom_fusion.1 = f32[1024,256]{0,1:T(8,128)S(1)} fusion(s32[1024]{0:T(1024)S(1)} %bitcast.75, f32[1024,1024]{0,1:T(8,128)} %bitcast_select_fusion, f32[]{:T(128)} %constant.47.clone.1), kind=kCustom, calls=%fused_computation.14 | custom fusion | flops 1048576 | bytes 5242884 | tf_op jit(solution)/shard_map/scatter-add | solution.py:78
  644.4 71.2 %all-reduce.2.cloned.1.call-done = f32[4096,4]{0,1:T(4,128)} async-done(((f32[4096,4]{0,1:T(4,128)}), f32[4096,4]{0,1:T(4,128)}) %all-reduce.2.cloned.1.call-update) | async-done | bytes 65552 | tf_op jit(solution)/shard_map/psum | solution.py:63
  (45 shorter events, 7.4 us)
Async XLA Ops:
  8.0 6.9 copy-start
  239.6 5.3 copy-start.5
  239.6 5.3 copy-start.2
  239.6 187.4 %all-to-all-start.1 = ((bf16[8,128,4096]{2,1,0:T(8,128)(2,1)}), bf16[8,128,4096]{2,1,0:T(8,128)(2,1)}, u32[]{:S(2)}, u32[]{:S(2)}) async-start(bf16[8,128,4096]{2,1,0:T(8,128)(2,1)} %get-tuple-element.10), calls=%async_computation.1 | async-start | bytes 16777216 | tf_op jit(solution)/shard_map/all_to_all | solution.py:34
  244.8 278.8 %reduce-scatter.2.cloned.1.call-start = ((), (), s32[]{:S(2)}) async-start(), calls=%async_computation.4 | async-start | bytes 10485760 | tf_op jit(solution)/shard_map/reduce_scatter | solution.py:65
  264.1 3.5 copy-start.3
  440.0 6.3 copy-start.6
  529.2 99.4 %all-to-all-start.2 = ((f32[1024,8,128]{0,2,1:T(8,128)}), f32[1024,8,128]{0,2,1:T(8,128)}, u32[]{:S(2)}, u32[]{:S(2)}) async-start(f32[1024,8,128]{0,2,1:T(8,128)} %bitcast.69), calls=%async_computation.3 | async-start | bytes 8388608 | tf_op jit(solution)/shard_map/all_to_all | solution.py:74
  534.7 181.0 %all-reduce.2.cloned.1.call-start = ((), (), s32[]{:S(2)}) async-start(), calls=%async_computation.5 | async-start | bytes 131072 | tf_op jit(solution)/shard_map/psum | solution.py:63
  539.7 6.8 copy-start.4
  628.6 88.6 %copy-start.1 = (bf16[256,4096]{1,0:T(8,128)(2,1)S(1)}, bf16[256,4096]{1,0:T(8,128)(2,1)}, u32[]{:S(2)}) copy-start(bf16[256,4096]{1,0:T(8,128)(2,1)} %param.6) | copy-start | bytes 6291460
Sparse Core Ops, SparseCore 0:
  452.7 70.7 reduce-scatter.1
Sparse Core Ops, SparseCore 1:
  542.2 173.4 all-reduce.1
where the time goes:
time: 727 us; the launch traced here: 725 us
  waiting for transfers between devices  375 us (52%)
  blocking collectives  190 us (26%)
  local copies, waits for them, and re-layouts  64.9 us (9%)
  matrix products  35.8 us (5%)
  other arithmetic  32.3 us (4%)
  between operations  15.7 us (2%)
  starting transfers between devices  11 us (2%)
    all_to_all x1, blocking collectives, body(): lax.all_to_all(pack(tokens), 'expert', split_axis=0, concat_axis=0, tiled...  190 us
    all_to_all x1, waiting for transfers between devices, body(): lax.all_to_all(pack(cotangent), 'expert', split_axis=0, concat_axis=0, ti...  155 us
    all_to_all x1, waiting for transfers between devices, body(): lax.all_to_all(outgoing.reshape(share, n_expert, bucket), 'expert', split...  77.8 us
    psum x1, waiting for transfers between devices, body(): grad_router = lax.psum(router_term, ('expert', 'tensor'))  71.2 us
    reduce_scatter x1, waiting for transfers between devices, body(): lax.psum_scatter(jnp.dot(w_in, pre_grad.T, preferred_element_type=jnp.flo...  71 us
    gather x2, local copies, waits for them, and re-layouts, pack(): source[send_rows]  24.7 us
  transfers between devices with their start and end apart: 4, of which 4 were waited for; matrix products, arithmetic and copies ran while one was open for 8% of the time, Pallas kernels for 0%

commit v1 on v0

v1 whole, which is shorter than its diff:
```python
import functools

import jax
import jax.numpy as jnp
from jax import lax
from jax.experimental import pallas as pl
from jax.experimental.pallas import tpu as pltpu
from jax.sharding import Mesh
from jax.sharding import PartitionSpec as P

BF = jnp.bfloat16
F32 = jnp.float32
CORE = 2
VMEM_LIMIT = 40 * 1024 * 1024


def params():
    return pltpu.CompilerParams(vmem_limit_bytes=VMEM_LIMIT)


def full(shape):
    return pl.BlockSpec(shape, lambda *_: (0,) * len(shape))


def cost(flops, moved):
    return pl.CostEstimate(flops=int(flops), bytes_accessed=int(moved), transcendentals=0)


def dot(a, b, da, db):
    return lax.dot_general(a, b, (((da,), (db,)), ((), ())), preferred_element_type=F32)


def flip(x, bit):
    if bit == 1:
        return lax.ppermute(x, "half", [(0, 1), (1, 0)])
    n = lax.axis_size("tensor")
    return lax.ppermute(x, "tensor", [(i, i ^ (bit >> 1)) for i in range(n)])


def shift(x, step):
    n = lax.axis_size("plane")
    return lax.ppermute(x, "plane", [(i, (i + step) % n) for i in range(n)])


def chip_masks(slots):
    return sorted((m for m in range(slots) if not m & CORE), key=lambda m: (m.bit_count(), m))


def top_bit(m):
    return 1 << (m.bit_length() - 1)


def plane_gather(own, slots):
    half = own.shape[0] // 2
    blocks = {0: own}
    for m in chip_masks(slots)[1:]:
        low, high = m & -m, top_bit(m)
        if low == high:
            blocks[m] = flip(own, m)
        else:
            blocks[m] = jnp.concatenate(
                [flip(blocks[m ^ low][:half], low), flip(blocks[m ^ high][half:], high)]
            )
    for m in chip_masks(slots):
        blocks[m | CORE] = flip(blocks[m], CORE)
    return blocks


def ring_gather(x, n):
    rows = x.shape[0]
    half = rows // 2
    pieces = [(0, 0, x)]
    up, down = x, x
    for k in range(1, (n + 1) // 2):
        up, down = shift(up, 1), shift(down, -1)
        pieces += [(k, 0, up), (n - k, 0, down)]
    pieces += [(n // 2, 0, shift(up[:half], 1)), (n // 2, half, shift(down[half:], -1))]
    return pieces


def compact(chosen_col, starts, pieces):
    cap = chosen_col.shape[0]
    width = pieces[0].shape[1]

    def kernel(starts_ref, chosen_ref, *refs):
        out = refs[-1]
        acc = None
        for i, piece in enumerate(refs[:-1]):
            rows = piece.shape[0]
            place = chosen_ref[...] - starts_ref[i]
            hot = lax.broadcasted_iota(jnp.int32, (cap, rows), 1) == place
            term = dot(hot.astype(F32).astype(BF), piece[...], 1, 0)
            acc = term if acc is None else acc + term
        out[...] = acc.astype(BF)

    total = sum(p.shape[0] for p in pieces)
    return pl.pallas_call(
        kernel,
        grid_spec=pltpu.PrefetchScalarGridSpec(
            num_scalar_prefetch=1,
            grid=(1,),
            in_specs=[full(chosen_col.shape)] + [full(p.shape) for p in pieces],
            out_specs=full((cap, width)),
        ),
        out_shape=jax.ShapeDtypeStruct((cap, width), BF),
        compiler_params=params(),
        cost_estimate=cost(2 * cap * total * width, 2 * (cap + total) * width),
        name="compact_rows",
    )(starts, chosen_col, *pieces)


def place(chosen_row, starts, sizes, terms):
    cap, width = terms[0].shape

    def kernel(starts_ref, chosen_ref, *refs):
        ins, outs = refs[: len(terms)], refs[len(terms) :]
        total = ins[0][...].astype(F32)
        for r in ins[1:]:
            total = total + r[...].astype(F32)
        rows = total.astype(BF)
        for i, out in enumerate(outs):
            n = out.shape[0]
            spot = chosen_ref[...] - starts_ref[i]
            hot = lax.broadcasted_iota(jnp.int32, (n, cap), 0) == spot
            out[...] = dot(hot.astype(F32).astype(BF), rows, 1, 0).astype(BF)

    total = sum(sizes)
    return pl.pallas_call(
        kernel,
        grid_spec=pltpu.PrefetchScalarGridSpec(
            num_scalar_prefetch=1,
            grid=(1,),
            in_specs=[full(chosen_row.shape)] + [full(t.shape) for t in terms],
            out_specs=[full((n, width)) for n in sizes],
        ),
        out_shape=[jax.ShapeDtypeStruct((n, width), BF) for n in sizes],
        compiler_params=params(),
        cost_estimate=cost(2 * cap * total * width, 2 * (cap + total) * width),
        name="place_rows",
    )(starts, chosen_row, *terms)


def project_in(order, expert, xs, w_in, router):
    cap, width = xs[0].shape
    hidden = w_in.shape[1]
    experts = router.shape[1]
    count = len(xs)

    def kernel(order_ref, expert_ref, *refs):
        ins = refs[:count]
        w_ref, r_ref, a_ref, gate_ref, score = refs[count:]
        j = pl.program_id(0)

        @pl.when(j == 0)
        def _():
            a_ref[...] = jnp.zeros_like(a_ref)
            score[...] = jnp.zeros_like(score)

        for k in range(count):

            @pl.when(j == k)
            def _():
                a_ref[...] += dot(ins[k][...], w_ref[...], 1, 0)
                score[...] += dot(ins[k][...], r_ref[...], 1, 0)

        @pl.when(j == count - 1)
        def _():
            mine = lax.broadcasted_iota(jnp.int32, (cap, experts), 1) == expert_ref[0]
            picked = jnp.sum(jnp.where(mine, score[...], 0.0), axis=1, keepdims=True)
            gate_ref[...] = jax.nn.sigmoid(picked)

    return pl.pallas_call(
        kernel,
        grid_spec=pltpu.PrefetchScalarGridSpec(
            num_scalar_prefetch=2,
            grid=(count,),
            in_specs=[full((cap, width))] * count
            + [
                pl.BlockSpec((width, hidden), lambda j, order, _: (order[j], 0)),
                pl.BlockSpec((width, experts), lambda j, order, _: (order[j], 0)),
            ],
            out_specs=[full((cap, hidden)), full((cap, 1))],
            scratch_shapes=[pltpu.VMEM((cap, experts), F32)],
        ),
        out_shape=[jax.ShapeDtypeStruct((cap, hidden), F32), jax.ShapeDtypeStruct((cap, 1), F32)],
        compiler_params=params(),
        cost_estimate=cost(2 * cap * width * count * hidden, 2 * width * count * (cap + hidden)),
        name="project_in",
    )(order, expert, *xs, w_in, router)


def project_out(order, ys, w_out, pre_act, gate):
    cap, width = ys[0].shape
    hidden = w_out.shape[0]
    count = len(ys)

    def kernel(order_ref, *refs):
        ins = refs[:count]
        w_ref, a_ref, gate_ref, hg_ref, da_ref, ds_ref, up = refs[count:]
        j = pl.program_id(0)

        @pl.when(j == 0)
        def _():
            up[...] = jnp.zeros_like(up)

        for k in range(count):

            @pl.when(j == k)
            def _():
                up[...] += dot(ins[k][...], w_ref[...], 1, 1)

        @pl.when(j == count - 1)
        def _():
            a = a_ref[...]
            u = up[...]
            gate = gate_ref[...]
            sig = jax.nn.sigmoid(a)
            act = a * sig
            hg_ref[...] = (gate * act).astype(BF)
            gate_grad = jnp.sum(act * u, axis=1, keepdims=True)
            ds_ref[...] = gate_grad * gate * (1.0 - gate)
            da_ref[...] = (gate * u * sig * (1.0 + a * (1.0 - sig))).astype(BF)

    return pl.pallas_call(
        kernel,
        grid_spec=pltpu.PrefetchScalarGridSpec(
            num_scalar_prefetch=1,
            grid=(count,),
            in_specs=[full((cap, width))] * count
            + [
                pl.BlockSpec((hidden, width), lambda j, order: (0, order[j])),
                full((cap, hidden)),
                full((cap, 1)),
            ],
            out_specs=[full((cap, hidden)), full((cap, hidden)), full((cap, 1))],
            scratch_shapes=[pltpu.VMEM((cap, hidden), F32)],
        ),
        out_shape=[
            jax.ShapeDtypeStruct((cap, hidden), BF),
            jax.ShapeDtypeStruct((cap, hidden), BF),
            jax.ShapeDtypeStruct((cap, 1), F32),
        ],
        compiler_params=params(),
        cost_estimate=cost(2 * cap * width * count * hidden, 2 * width * count * (cap + hidden)),
        name="project_out",
    )(order, *ys, w_out, pre_act, gate)


def row_grads(order, pre_grad, score_grad, w_in, router_row, arrived, kinds):
    cap, hidden = pre_grad.shape
    count = len(kinds)
    width = w_in.shape[0] // (2 * lax.axis_size("tensor"))
    extra = [] if arrived is None else [arrived]

    def kernel(order_ref, da_ref, ds_ref, w_ref, r_ref, *refs):
        outs = refs[len(extra) :]
        j = pl.program_id(0)
        block = dot(da_ref[...], w_ref[...], 1, 1) + ds_ref[...] * r_ref[...]
        if extra:
            block = block + refs[0][0].astype(F32)
        for k in range(count):

            @pl.when(j == k)
            def _():
                outs[k][...] = block.astype(kinds[k])

    return pl.pallas_call(
        kernel,
        grid_spec=pltpu.PrefetchScalarGridSpec(
            num_scalar_prefetch=1,
            grid=(count,),
            in_specs=[
                full((cap, hidden)),
                full((cap, 1)),
                pl.BlockSpec((width, hidden), lambda j, order: (order[j], 0)),
                pl.BlockSpec((1, width), lambda j, order: (0, order[j])),
            ]
            + [pl.BlockSpec((1, cap, width), lambda j, order: (j, 0, 0)) for _ in extra],
            out_specs=[full((cap, width)) for _ in kinds],
        ),
        out_shape=[jax.ShapeDtypeStruct((cap, width), kind) for kind in kinds],
        compiler_params=params(),
        cost_estimate=cost(2 * cap * width * count * hidden, 4 * width * count * (cap + hidden)),
        name="row_grads",
    )(order, pre_grad, score_grad, w_in, router_row, *extra)


def grads_in(order, xs, pre_grad, score_grad):
    cap, width = xs[0].shape
    hidden = pre_grad.shape[1]
    count = len(xs)

    def kernel(order_ref, *refs):
        ins = refs[:count]
        da_ref, ds_ref, out, col = refs[count:]
        j = pl.program_id(0)
        for k in range(count):

            @pl.when(j == k)
            def _():
                x = ins[k][...]
                out[...] = dot(x, da_ref[...], 0, 0).astype(BF)
                col[...] = jnp.sum(x.astype(F32) * ds_ref[...], axis=0, keepdims=True)

    return pl.pallas_call(
        kernel,
        grid_spec=pltpu.PrefetchScalarGridSpec(
            num_scalar_prefetch=1,
            grid=(count,),
            in_specs=[full((cap, width))] * count + [full((cap, hidden)), full((cap, 1))],
            out_specs=[
                pl.BlockSpec((width, hidden), lambda j, order: (order[j], 0)),
                pl.BlockSpec((1, width), lambda j, order: (0, order[j])),
            ],
        ),
        out_shape=[
            jax.ShapeDtypeStruct((width * count, hidden), BF),
            jax.ShapeDtypeStruct((1, width * count), F32),
        ],
        compiler_params=params(),
        cost_estimate=cost(2 * cap * width * count * hidden, 2 * width * count * (cap + hidden)),
        name="grads_in",
    )(order, *xs, pre_grad, score_grad)


def grads_out(order, ys, gated):
    cap, width = ys[0].shape
    hidden = gated.shape[1]
    count = len(ys)

    def kernel(order_ref, *refs):
        ins = refs[:count]
        hg_ref, out = refs[count:]
        j = pl.program_id(0)
        for k in range(count):

            @pl.when(j == k)
            def _():
                out[...] = dot(hg_ref[...], ins[k][...], 0, 0).astype(BF)

    return pl.pallas_call(
        kernel,
        grid_spec=pltpu.PrefetchScalarGridSpec(
            num_scalar_prefetch=1,
            grid=(count,),
            in_specs=[full((cap, width))] * count + [full((cap, hidden))],
            out_specs=pl.BlockSpec((hidden, width), lambda j, order: (0, order[j])),
        ),
        out_shape=jax.ShapeDtypeStruct((hidden, width * count), BF),
        compiler_params=params(),
        cost_estimate=cost(2 * cap * width * count * hidden, 2 * width * count * (cap + hidden)),
        name="grads_out",
    )(order, *ys, gated)


def body(tokens, cotangent, w_in, w_out, router, chosen):
    planes = lax.axis_size("plane")
    slots = 2 * lax.axis_size("tensor")
    tok_dev, features = tokens.shape
    width = features // slots
    cap = chosen.shape[1]
    plane = lax.axis_index("plane")
    half = lax.axis_index("half")
    slot = lax.axis_index("tensor") * 2 + half
    expert = plane.astype(jnp.int32)[None]
    chosen_col = lax.dynamic_slice_in_dim(chosen.T, plane, 1, 1)
    chosen_row = lax.dynamic_slice_in_dim(chosen, plane, 1, 0)
    router_row = lax.dynamic_slice_in_dim(router.T, plane, 1, 0).astype(F32)
    masks = chip_masks(slots)

    def fetch(source):
        own = lax.dynamic_slice_in_dim(source, slot * width, width, 1)
        away = flip(lax.dynamic_slice_in_dim(source, (slot ^ 1) * width, width, 1), 1)
        pieces = [(0, p) for p in ring_gather(own, planes)] + [(1, p) for p in ring_gather(away, planes)]
        starts = jnp.stack(
            [
                (((plane - back) % planes) * 2 + (half ^ other)) * tok_dev + offset
                for other, (back, offset, _) in pieces
            ]
        ).astype(jnp.int32)
        return plane_gather(compact(chosen_col, starts, [x for _, (_, _, x) in pieces]), slots)

    xs = fetch(tokens)
    ys = fetch(cotangent)
    keys = masks + [m | CORE for m in masks]
    order = jnp.stack([slot ^ m for m in keys]).astype(jnp.int32)
    x_list = [xs[m] for m in keys]
    y_list = [ys[m] for m in keys]
    pre_act, gate = project_in(order, expert, x_list, w_in, router)
    gated, pre_grad, score_grad = project_out(order, y_list, w_out, pre_act, gate)

    back = masks[::-1]
    far = jnp.stack([slot ^ m ^ CORE for m in back]).astype(jnp.int32)
    near = jnp.stack([slot ^ m for m in back]).astype(jnp.int32)
    sent = row_grads(far, pre_grad, score_grad, w_in, router_row, None, [BF] * len(back))
    arrived = flip(jnp.stack(sent), CORE)
    kinds = [BF if i == 0 else F32 for i in range(len(back))]
    sums = dict(zip(back, row_grads(near, pre_grad, score_grad, w_in, router_row, arrived, kinds)))
    mid = cap // 2
    last = [sums[0]]
    for m in back[:-1]:
        low, high = m & -m, top_bit(m)
        block = sums[m].astype(BF)
        if low == high:
            last.append(flip(block, m))
            continue
        a, b = flip(block[:mid], low), flip(block[mid:], high)
        for key, piece, first in ((m ^ low, a, True), (m ^ high, b, False)):
            old = sums[key].astype(F32)
            parts = [old[:mid], old[mid:]]
            parts[0 if first else 1] = parts[0 if first else 1] + piece.astype(F32)
            sums[key] = jnp.concatenate(parts)

    shape = [(1, n, o, r) for n, o, r in ring_shape(planes, tok_dev)]
    shape += [(0, n, o, r) for n, o, r in ring_shape(planes, tok_dev)]
    starts = jnp.stack(
        [(((plane + n) % planes) * 2 + (half ^ other)) * tok_dev + o for other, n, o, _ in shape]
    ).astype(jnp.int32)
    placed = place(chosen_row, starts, [r for *_, r in shape], last)
    count = len(shape) // 2
    away = ring_scatter(placed[:count], planes)
    away = flip(away, 1)
    own = ring_scatter(placed[count:], planes)
    grad_tokens = jnp.where(
        half == 0, jnp.concatenate([own, away], axis=1), jnp.concatenate([away, own], axis=1)
    )

    grad_in, router_col = grads_in(order, x_list, pre_grad, score_grad)
    grad_out = grads_out(order, y_list, gated)
    total = jnp.where(jnp.arange(planes)[:, None] == plane, router_col, 0.0)
    bit = 1
    while bit < slots:
        total = total + flip(total, bit)
        bit *= 2
    bit = 1
    while bit < planes:
        total = total + lax.ppermute(total, "plane", [(i, i ^ bit) for i in range(planes)])
        bit *= 2
    return (grad_tokens, grad_in, grad_out, total.T)


def ring_shape(n, rows):
    half = rows // 2
    return [(0, 0, rows), (n // 2, 0, half), (n // 2, half, half)] + [
        piece for k in range(n // 2 - 1, 0, -1) for piece in ((k, 0, rows), (n - k, 0, rows))
    ]


def ring_scatter(pieces, n):
    own, up, down = pieces[:3]
    half = own.shape[0] // 2
    up, down = shift(up, 1).astype(F32), shift(down, -1).astype(F32)
    rest = pieces[3:]
    for k in range(0, len(rest), 2):
        ahead, behind = rest[k].astype(F32), rest[k + 1].astype(F32)
        if up.shape[0] == half:
            ahead = jnp.concatenate([ahead[:half] + up, ahead[half:]])
            behind = jnp.concatenate([behind[:half], behind[half:] + down])
        else:
            ahead, behind = ahead + up, behind + down
        up, down = shift(ahead.astype(BF), 1).astype(F32), shift(behind.astype(BF), -1).astype(F32)
    own = own.astype(F32)
    if up.shape[0] == half:
        return (own + jnp.concatenate([up, down])).astype(BF)
    return (own + up + down).astype(BF)


def solution(mesh):
    planes = mesh.shape["expert"] // 2
    inner = Mesh(mesh.devices.reshape(planes, 2, mesh.shape["tensor"]), ("plane", "half", "tensor"))
    home = ("plane", "half")
    every = ("plane", "half", "tensor")
    return jax.shard_map(
        body,
        mesh=inner,
        in_specs=(P(home, None), P(home, None), P(None, every), P(every, None), P(), P()),
        out_specs=(P(home, "tensor"), P(None, every), P(every, None), P()),
        check_vma=False,
    )
```

time: 727 us -> 237 us (0.33)
  waiting for transfers between devices: 375 us -> 98.5 us
  blocking collectives: 190 us -> 0 us
  starting transfers between devices: 11 us -> 65.1 us
  Pallas kernels: 0 us -> 44.4 us
  local copies, waits for them, and re-layouts: 64.9 us -> 22.3 us
  matrix products: 35.8 us -> 0 us
  other arithmetic: 32.3 us -> 4.27 us
  between operations: 15.7 us -> 1.39 us
    all_to_all x2 -> x0, waiting for transfers between devices: 233 us -> none  [the longest x1 155 us: body(): lax.all_to_all(pack(cotangent), 'expert', split_axis=0, concat_axis=0, ti...]
    all_to_all x1 -> x0, blocking collectives: 190 us -> none  [body(): lax.all_to_all(pack(tokens), 'expert', split_axis=0, concat_axis=0, tiled...]
    ppermute x0 -> x53, waiting for transfers between devices: none -> 98.5 us  [the longest x24 48.6 us: shift(): return lax.ppermute(x, 'plane', [(i, (i + step) % n) for i in range(n)])]
    psum x1 -> x0, waiting for transfers between devices: 71.2 us -> none  [body(): grad_router = lax.psum(router_term, ('expert', 'tensor'))]
    reduce_scatter x1 -> x0, waiting for transfers between devices: 71 us -> none  [body(): lax.psum_scatter(jnp.dot(w_in, pre_grad.T, preferred_element_type=jnp.flo...]
    ppermute x0 -> x53, starting transfers between devices: none -> 65.1 us  [the longest x24 40.1 us: shift(): return lax.ppermute(x, 'plane', [(i, (i + step) % n) for i in range(n)])]
    gather x8 -> x0, local copies, waits for them, and re-layouts: 57.7 us -> none  [the longest x2 24.7 us: pack(): source[send_rows]]
    pallas_call x0 -> x9, Pallas kernels: none -> 44.4 us  [the longest x1 8.37 us: grads_in(): pl.pallas_call(kernel, grid_spec=pltpu.PrefetchScalarGridSpec(num_scalar_...]
  transfers between devices with their start and end apart: 4 -> 53, of which waited for: 4 -> 28; matrix products, arithmetic and copies ran while one was open for 8% -> 6% of each run, Pallas kernels for 0% -> 15%
where the time goes in v1:
time: 237 us; the launch traced here: 236 us
  waiting for transfers between devices  98.5 us (42%)
  starting transfers between devices  65.1 us (27%)
  Pallas kernels  44.4 us (19%)
  local copies, waits for them, and re-layouts  22.3 us (9%)
  other arithmetic  4.27 us (2%)
    ppermute x24, waiting for transfers between devices, shift(): return lax.ppermute(x, 'plane', [(i, (i + step) % n) for i in range(n)])  48.6 us
    ppermute x24, starting transfers between devices, shift(): return lax.ppermute(x, 'plane', [(i, (i + step) % n) for i in range(n)])  40.1 us
    ppermute x17, waiting for transfers between devices, flip(): return lax.ppermute(x, 'tensor', [(i, i ^ bit >> 1) for i in range(n)])  25 us
    ppermute x10, waiting for transfers between devices, flip(): return lax.ppermute(x, 'half', [(0, 1), (1, 0)])  24.9 us
    ppermute x10, starting transfers between devices, flip(): return lax.ppermute(x, 'half', [(0, 1), (1, 0)])  13.6 us
    unnamed x63, local copies, waits for them, and re-layouts  10.7 us
    pallas_call x1, Pallas kernels, grads_in(): pl.pallas_call(kernel, grid_spec=pltpu.PrefetchScalarGridSpec(num_scalar_...  8.37 us
    pallas_call x1, Pallas kernels, project_in(): pl.pallas_call(kernel, grid_spec=pltpu.PrefetchScalarGridSpec(num_scalar_...  8.11 us
  transfers between devices with their start and end apart: 53, of which 28 were waited for; matrix products, arithmetic and copies ran while one was open for 6% of the time, Pallas kernels for 15%

profile of v1, /device:TPU:0, one launch (start us, length us, event | category | flops | bytes accessed | tf_op | source)
XLA Modules:
  0.0 235.9 jit_solution(14443921584470423951)
XLA Ops:
  5.9 4.1 %collective-permute-start.1 = (bf16[256,512]{1,0:T(8,128)(2,1)S(1)}, bf16[256,512]{1,0:T(8,128)(2,1)S(1)}, u32[]{:S(2)}, u32[]{:S(2)}) collective-permute-start(bf16[256,512]{1,0:T(8,128)(2,1)S(1)} %get-tuple-element.57.refs_0_), channel_id=1, source_target_pairs={{0,24},{8,0},{16,8},{24,16},{1,25},{9,1},{17,9},{25,17},{2,26},{10... | collective-permute-start | bytes 786440 | tf_op jit(solution)/shard_map/ppermute | solution.py:42
  11.9 4.2 %collective-permute-start.6 = (bf16[256,512]{1,0:T(8,128)(2,1)S(1)}, bf16[256,512]{1,0:T(8,128)(2,1)S(1)}, u32[]{:S(2)}, u32[]{:S(2)}) collective-permute-start(bf16[256,512]{1,0:T(8,128)(2,1)S(1)} %collective-permute-done.4.refs_5_), channel_id=1, source_target_pairs={{0,24},{8,0},{16,8},{24,16},{1,25},{9,1},{17,9},{25,17},{2,26},{10... | collective-permute-start | bytes 786440 | tf_op jit(solution)/shard_map/ppermute | solution.py:42
  20.1 3.3 %collective-permute-done.refs_1_ = bf16[256,512]{1,0:T(8,128)(2,1)S(1)} collective-permute-done((bf16[256,512]{1,0:T(8,128)(2,1)S(1)}, bf16[256,512]{1,0:T(8,128)(2,1)S(1)}, u32[]{:S(2)}, u32[]{:S(2)}) %collective-permute-start) | collective-permute-done | bytes 262176 | tf_op jit(solution)/shard_map/ppermute | solution.py:42
  30.0 3.6 %collective-permute-done.18.refs_2_ = bf16[256,512]{1,0:T(8,128)(2,1)S(1)} collective-permute-done((bf16[256,512]{1,0:T(8,128)(2,1)S(1)}, bf16[256,512]{1,0:T(8,128)(2,1)S(1)}, u32[]{:S(2)}, u32[]{:S(2)}) %collective-permute-start.18) | collective-permute-done | bytes 262176 | tf_op jit(solution)/shard_map/ppermute | solution.py:42
  33.7 4.3 %collective-permute-start.3 = (bf16[128,512]{1,0:T(8,128)(2,1)}, bf16[128,512]{1,0:T(8,128)(2,1)S(1)}, u32[]{:S(2)}, u32[]{:S(2)}) collective-permute-start(bf16[128,512]{1,0:T(8,128)(2,1)} %slice.127), channel_id=1, source_target_pairs={{0,24},{8,0},{16,8},{24,16},{1,25},{9,1},{17,9},{25,17},{2,26},{10... | collective-permute-start | bytes 393224 | tf_op jit(solution)/shard_map/ppermute | solution.py:42
  41.8 4.1 %collective-permute-done.5.refs_6_ = bf16[256,512]{1,0:T(8,128)(2,1)S(1)} collective-permute-done((bf16[256,512]{1,0:T(8,128)(2,1)S(1)}, bf16[256,512]{1,0:T(8,128)(2,1)S(1)}, u32[]{:S(2)}, u32[]{:S(2)}) %collective-permute-start.5) | collective-permute-done | bytes 262176 | tf_op jit(solution)/shard_map/ppermute | solution.py:42
  53.8 3.4 %collective-permute-done.22.refs_6_ = bf16[256,512]{1,0:T(8,128)(2,1)S(1)} collective-permute-done((bf16[256,512]{1,0:T(8,128)(2,1)S(1)}, bf16[256,512]{1,0:T(8,128)(2,1)S(1)}, u32[]{:S(2)}, u32[]{:S(2)}) %collective-permute-start.22) | collective-permute-done | bytes 262176 | tf_op jit(solution)/shard_map/ppermute | solution.py:42
  78.0 4.0 %compact_rows.3.refs_0_ = bf16[512,512]{1,0:T(8,128)(2,1)} custom-call(s32[10]{0:T(128)S(1)} %stack.164.starts_ref, s32[512,1]{1,0:T(8,128)S(1)} %copy.11.chosen_ref, bf16[256,512]{1,0:T(8,128)(2,1)S(1)} %get-tuple-element.55.refs_0_, bf16[256,512]{1,0:T(8,128)(2,1)S(1)} %collective-permute-done.17.refs_1_, ...), custom_call_target="tpu_custom_call" | custom-call | flops 1073741824 | bytes 2621440 | tf_op jit(solution)/shard_map/compact_rows/pallas_call | solution.py:97
  87.6 8.2 %collective-permute-done.27.refs_2_ = bf16[512,512]{1,0:T(8,128)(2,1)} collective-permute-done((bf16[512,512]{1,0:T(8,128)(2,1)}, bf16[512,512]{1,0:T(8,128)(2,1)}, u32[]{:S(2)}, u32[]{:S(2)}) %collective-permute-start.27) | collective-permute-done | bytes 524320 | tf_op jit(solution)/shard_map/ppermute | solution.py:37
  101.5 8.3 %collective-permute-done.9.refs_1_ = bf16[512,512]{1,0:T(8,128)(2,1)S(1)} collective-permute-done((bf16[512,512]{1,0:T(8,128)(2,1)S(1)}, bf16[512,512]{1,0:T(8,128)(2,1)S(1)}, u32[]{:S(2)}, u32[]{:S(2)}) %collective-permute-start.9) | collective-permute-done | bytes 524320 | tf_op jit(solution)/shard_map/ppermute | solution.py:35
  109.8 5.2 %collective-permute-done.11 = bf16[256,512]{1,0:T(8,128)(2,1)S(1)} collective-permute-done((bf16[256,512]{1,0:T(8,128)(2,1)S(1)}, bf16[256,512]{1,0:T(8,128)(2,1)S(1)}, u32[]{:S(2)}, u32[]{:S(2)}) %collective-permute-start.11) | collective-permute-done | bytes 262176 | tf_op jit(solution)/shard_map/ppermute | solution.py:35
  120.5 4.0 %collective-permute-done.12 = bf16[256,512]{1,0:T(8,128)(2,1)S(1)} collective-permute-done((bf16[256,512]{1,0:T(8,128)(2,1)S(1)}, bf16[256,512]{1,0:T(8,128)(2,1)S(1)}, u32[]{:S(2)}, u32[]{:S(2)}) %collective-permute-start.12) | collective-permute-done | bytes 262176 | tf_op jit(solution)/shard_map/ppermute | solution.py:37
  128.8 8.1 %project_in.1 = (f32[512,512]{1,0:T(8,128)S(1)}, f32[512,1]{1,0:T(8,128)S(1)}) custom-call(s32[8]{0:T(128)S(1)} %stack.155.order_ref, s32[1]{0:T(128)} %bitcast.27.expert_ref, bf16[512,512]{1,0:T(8,128)(2,1)} %compact_rows.3.refs_0_, bf16[512,512]{1,0:T(8,128)(2,1)} %collective-permute-done.26.refs_1_, bf16[512,512]{1,0:T(8,128)(2,1)} %collective-permute-done.27.refs_2_, ...), custom_call_target="tpu_custom_call" | custom-call | flops 2147483648 | bytes 8388608 | tf_op jit(solution)/shard_map/project_in/pallas_call | solution.py:172
  139.9 5.4 %project_out.1 = (bf16[512,512]{1,0:T(8,128)(2,1)S(1)}, bf16[512,512]{1,0:T(8,128)(2,1)S(1)}, f32[512,1]{1,0:T(8,128)S(1)}) custom-call(s32[8]{0:T(128)S(1)} %stack.155.order_ref, bf16[512,512]{1,0:T(8,128)(2,1)S(1)} %compact_rows.2.refs_0_, bf16[512,512]{1,0:T(8,128)(2,1)S(1)} %collective-permute-done.9.refs_1_, ...), custom_call_target="tpu_custom_call" | custom-call | flops 2147483648 | bytes 8388608 | tf_op jit(solution)/shard_map/project_out/pallas_call | solution.py:224
  151.0 8.4 %grads_in.1 = (bf16[4096,512]{1,0:T(8,128)(2,1)}, f32[1,4096]{1,0:T(1,128)S(1)}) custom-call(s32[8]{0:T(128)S(1)} %stack.155.order_ref, bf16[512,512]{1,0:T(8,128)(2,1)} %compact_rows.3.refs_0_, bf16[512,512]{1,0:T(8,128)(2,1)} %collective-permute-done.26.refs_1_, bf16[512,512]{1,0:T(8,128)(2,1)} %collective-permute-done.27.refs_2_, ...), custom_call_target="tpu_custom_call" | custom-call | flops 2147483648 | bytes 8388608 | tf_op jit(solution)/shard_map/grads_in/pallas_call | solution.py:305
  161.1 4.6 %row_grads.3 = (bf16[512,512]{1,0:T(8,128)(2,1)S(1)}, f32[512,512]{1,0:T(8,128)S(1)}, f32[512,512]{1,0:T(8,128)S(1)}, f32[512,512]{1,0:T(8,128)S(1)}) custom-call(s32[4]{0:T(128)S(1)} %pad_add_fusion.order_ref, bf16[512,512]{1,0:T(8,128)(2,1)S(1)} %get-tuple-element.31.da_ref.refs_8_, f32[512,1]{1,0:T(8,128)S(1)} %get-tuple-element.32.ds_ref.refs_9_, ...), custom_call_target="tpu_custom_call" | custom-call | flops 1073741824 | bytes 8388608 | tf_op jit(solution)/shard_map/row_grads/pallas_call | solution.py:267
  167.2 6.9 %collective-permute-done.35 = bf16[256,512]{1,0:T(8,128)(2,1)S(1)} collective-permute-done((bf16[256,512]{1,0:T(8,128)(2,1)S(1)}, bf16[256,512]{1,0:T(8,128)(2,1)S(1)}, u32[]{:S(2)}, u32[]{:S(2)}) %collective-permute-start.35) | collective-permute-done | bytes 262176 | tf_op jit(solution)/shard_map/ppermute | solution.py:35
  177.9 10.9 %collective-permute-done.50 = f32[4,4096]{1,0:T(4,128)S(1)} collective-permute-done((f32[4,4096]{1,0:T(4,128)S(1)}, f32[4,4096]{1,0:T(4,128)S(1)}, u32[]{:S(2)}, u32[]{:S(2)}) %collective-permute-start.50) | collective-permute-done | bytes 65568 | tf_op jit(solution)/shard_map/ppermute | solution.py:37
  192.5 6.2 %grads_out.1 = bf16[512,4096]{1,0:T(8,128)(2,1)} custom-call(s32[8]{0:T(128)S(1)} %stack.155.order_ref, bf16[512,512]{1,0:T(8,128)(2,1)S(1)} %compact_rows.2.refs_0_, bf16[512,512]{1,0:T(8,128)(2,1)S(1)} %collective-permute-done.9.refs_1_, bf16[512,512]{1,0:T(8,128)(2,1)S(1)} %collective-permute-done.10.refs_2_, ...), custom_call_target="tpu_custom_call" | custom-call | flops 2147483648 | bytes 8388608 | tf_op jit(solution)/shard_map/grads_out/pallas_call | solution.py:341
  200.9 3.6 %collective-permute-start.41 = (bf16[128,512]{1,0:T(8,128)(2,1)S(1)}, bf16[128,512]{1,0:T(8,128)(2,1)S(1)}, u32[]{:S(2)}, u32[]{:S(2)}) collective-permute-start(bf16[128,512]{1,0:T(8,128)(2,1)S(1)} %get-tuple-element.45), channel_id=1, source_target_pairs={{0,24},{8,0},{16,8},{24,16},{1,25},{9,1},{17,9},{25,17},{2,26},{10... | collective-permute-start | bytes 393224 | tf_op jit(solution)/shard_map/ppermute | solution.py:42
  204.6 3.9 %collective-permute-start.46 = (bf16[256,512]{1,0:T(8,128)(2,1)S(1)}, bf16[256,512]{1,0:T(8,128)(2,1)S(1)}, u32[]{:S(2)}, u32[]{:S(2)}) collective-permute-start(bf16[256,512]{1,0:T(8,128)(2,1)S(1)} %pad_maximum_fusion.6), channel_id=1, source_target_pairs={{0,24},{8,0},{16,8},{24,16},{1,25},{9,1},{17,9},{25,17},{2,26},{10... | collective-permute-start | bytes 786440 | tf_op jit(solution)/shard_map/ppermute | solution.py:42
  208.5 6.0 %collective-permute-done.43 = bf16[128,512]{1,0:T(8,128)(2,1)S(1)} collective-permute-done((bf16[128,512]{1,0:T(8,128)(2,1)S(1)}, bf16[128,512]{1,0:T(8,128)(2,1)S(1)}, u32[]{:S(2)}, u32[]{:S(2)}) %collective-permute-start.43) | collective-permute-done | bytes 131104 | tf_op jit(solution)/shard_map/ppermute | solution.py:42
  220.1 5.7 %collective-permute-done.44 = bf16[256,512]{1,0:T(8,128)(2,1)S(1)} collective-permute-done((bf16[256,512]{1,0:T(8,128)(2,1)S(1)}, bf16[256,512]{1,0:T(8,128)(2,1)S(1)}, u32[]{:S(2)}, u32[]{:S(2)}) %collective-permute-start.44) | collective-permute-done | bytes 262176 | tf_op jit(solution)/shard_map/ppermute | solution.py:42
  228.6 6.3 %collective-permute-done.40 = bf16[256,512]{1,0:T(8,128)(2,1)S(1)} collective-permute-done((bf16[256,512]{1,0:T(8,128)(2,1)S(1)}, bf16[256,512]{1,0:T(8,128)(2,1)S(1)}, u32[]{:S(2)}, u32[]{:S(2)}) %collective-permute-start.40) | collective-permute-done | bytes 262176 | tf_op jit(solution)/shard_map/ppermute | solution.py:42
  (209 shorter events, 101.9 us)
Async XLA Ops:
  11.9 16.2 %collective-permute-start.6 = (bf16[256,512]{1,0:T(8,128)(2,1)S(1)}, bf16[256,512]{1,0:T(8,128)(2,1)S(1)}, u32[]{:S(2)}, u32[]{:S(2)}) collective-permute-start(bf16[256,512]{1,0:T(8,128)(2,1)S(1)} %collective-permute-done.4.refs_5_), channel_id=1, source_target_pairs={{0,24},{8,0},{16,8},{24,16},{1,25},{9,1},{17,9},{25,17},{2,26},{10... | collective-permute-start | bytes 786440 | tf_op jit(solution)/shard_map/ppermute | solution.py:42
  16.0 17.6 %collective-permute-start.18 = (bf16[256,512]{1,0:T(8,128)(2,1)S(1)}, bf16[256,512]{1,0:T(8,128)(2,1)S(1)}, u32[]{:S(2)}, u32[]{:S(2)}) collective-permute-start(bf16[256,512]{1,0:T(8,128)(2,1)S(1)} %get-tuple-element.55.refs_0_), channel_id=1, source_target_pairs={{0,24},{8,0},{16,8},{24,16},{1,25},{9,1},{17,9},{25,17},{2,26},{10... | collective-permute-start | bytes 786440 | tf_op jit(solution)/shard_map/ppermute | solution.py:42
  16.7 23.7 %collective-permute-start.17 = (bf16[256,512]{1,0:T(8,128)(2,1)S(1)}, bf16[256,512]{1,0:T(8,128)(2,1)S(1)}, u32[]{:S(2)}, u32[]{:S(2)}) collective-permute-start(bf16[256,512]{1,0:T(8,128)(2,1)S(1)} %get-tuple-element.55.refs_0_), channel_id=1, source_target_pairs={{0,8},{8,16},{16,24},{24,0},{1,9},{9,17},{17,25},{25,1},{2,10},{10... | collective-permute-start | bytes 786440 | tf_op jit(solution)/shard_map/ppermute | solution.py:42
  18.5 27.4 %collective-permute-start.5 = (bf16[256,512]{1,0:T(8,128)(2,1)S(1)}, bf16[256,512]{1,0:T(8,128)(2,1)S(1)}, u32[]{:S(2)}, u32[]{:S(2)}) collective-permute-start(bf16[256,512]{1,0:T(8,128)(2,1)S(1)} %collective-permute-done.4.refs_5_), channel_id=1, source_target_pairs={{0,8},{8,16},{16,24},{24,0},{1,9},{9,17},{17,25},{25,1},{2,10},{10... | collective-permute-start | bytes 786440 | tf_op jit(solution)/shard_map/ppermute | solution.py:42
  23.3 27.2 %collective-permute-start.23 = (bf16[256,512]{1,0:T(8,128)(2,1)S(1)}, bf16[256,512]{1,0:T(8,128)(2,1)S(1)}, u32[]{:S(2)}, u32[]{:S(2)}) collective-permute-start(bf16[256,512]{1,0:T(8,128)(2,1)S(1)} %collective-permute-done.21.refs_5_), channel_id=1, source_target_pairs={{0,24},{8,0},{16,8},{24,16},{1,25},{9,1},{17,9},{25,17},{2,26},{10... | collective-permute-start | bytes 786440 | tf_op jit(solution)/shard_map/ppermute | solution.py:42
  28.1 29.2 %collective-permute-start.22 = (bf16[256,512]{1,0:T(8,128)(2,1)S(1)}, bf16[256,512]{1,0:T(8,128)(2,1)S(1)}, u32[]{:S(2)}, u32[]{:S(2)}) collective-permute-start(bf16[256,512]{1,0:T(8,128)(2,1)S(1)} %collective-permute-done.21.refs_5_), channel_id=1, source_target_pairs={{0,8},{8,16},{16,24},{24,0},{1,9},{9,17},{17,25},{25,1},{2,10},{10... | collective-permute-start | bytes 786440 | tf_op jit(solution)/shard_map/ppermute | solution.py:42
  33.7 26.2 %collective-permute-start.3 = (bf16[128,512]{1,0:T(8,128)(2,1)}, bf16[128,512]{1,0:T(8,128)(2,1)S(1)}, u32[]{:S(2)}, u32[]{:S(2)}) collective-permute-start(bf16[128,512]{1,0:T(8,128)(2,1)} %slice.127), channel_id=1, source_target_pairs={{0,24},{8,0},{16,8},{24,16},{1,25},{9,1},{17,9},{25,17},{2,26},{10... | collective-permute-start | bytes 393224 | tf_op jit(solution)/shard_map/ppermute | solution.py:42
  40.3 22.6 %collective-permute-start.2 = (bf16[128,512]{1,0:T(8,128)(2,1)}, bf16[128,512]{1,0:T(8,128)(2,1)S(1)}, u32[]{:S(2)}, u32[]{:S(2)}) collective-permute-start(bf16[128,512]{1,0:T(8,128)(2,1)} %slice.126), channel_id=1, source_target_pairs={{0,8},{8,16},{16,24},{24,0},{1,9},{9,17},{17,25},{25,1},{2,10},{10... | collective-permute-start | bytes 393224 | tf_op jit(solution)/shard_map/ppermute | solution.py:42
  45.9 19.0 %collective-permute-start.8 = (bf16[128,512]{1,0:T(8,128)(2,1)}, bf16[128,512]{1,0:T(8,128)(2,1)S(1)}, u32[]{:S(2)}, u32[]{:S(2)}) collective-permute-start(bf16[128,512]{1,0:T(8,128)(2,1)} %slice.129), channel_id=1, source_target_pairs={{0,24},{8,0},{16,8},{24,16},{1,25},{9,1},{17,9},{25,17},{2,26},{10... | collective-permute-start | bytes 393224 | tf_op jit(solution)/shard_map/ppermute | solution.py:42
  50.6 18.1 %collective-permute-start.7 = (bf16[128,512]{1,0:T(8,128)(2,1)}, bf16[128,512]{1,0:T(8,128)(2,1)}, u32[]{:S(2)}, u32[]{:S(2)}) collective-permute-start(bf16[128,512]{1,0:T(8,128)(2,1)} %slice.128), channel_id=1, source_target_pairs={{0,8},{8,16},{16,24},{24,0},{1,9},{9,17},{17,25},{25,1},{2,10},{10... | collective-permute-start | bytes 393224 | tf_op jit(solution)/shard_map/ppermute | solution.py:42
  57.2 18.8 %collective-permute-start.20 = (bf16[128,512]{1,0:T(8,128)(2,1)}, bf16[128,512]{1,0:T(8,128)(2,1)}, u32[]{:S(2)}, u32[]{:S(2)}) collective-permute-start(bf16[128,512]{1,0:T(8,128)(2,1)} %slice.133), channel_id=1, source_target_pairs={{0,24},{8,0},{16,8},{24,16},{1,25},{9,1},{17,9},{25,17},{2,26},{10... | collective-permute-start | bytes 393224 | tf_op jit(solution)/shard_map/ppermute | solution.py:42
  59.9 16.2 %collective-permute-start.19 = (bf16[128,512]{1,0:T(8,128)(2,1)}, bf16[128,512]{1,0:T(8,128)(2,1)}, u32[]{:S(2)}, u32[]{:S(2)}) collective-permute-start(bf16[128,512]{1,0:T(8,128)(2,1)} %slice.132), channel_id=1, source_target_pairs={{0,8},{8,16},{16,24},{24,0},{1,9},{9,17},{17,25},{25,1},{2,10},{10... | collective-permute-start | bytes 393224 | tf_op jit(solution)/shard_map/ppermute | solution.py:42
  85.0 24.8 %collective-permute-start.9 = (bf16[512,512]{1,0:T(8,128)(2,1)S(1)}, bf16[512,512]{1,0:T(8,128)(2,1)S(1)}, u32[]{:S(2)}, u32[]{:S(2)}) collective-permute-start(bf16[512,512]{1,0:T(8,128)(2,1)S(1)} %compact_rows.2.refs_0_), channel_id=1, source_target_pairs={{0,4},{4,0},{1,5},{5,1},{2,6},{6,2},{3,7},{7,3},{8,12},{12,8},{9,1... | collective-permute-start | bytes 1572872 | tf_op jit(solution)/shard_map/ppermute | solution.py:35
  86.1 28.9 %collective-permute-start.11 = (bf16[256,512]{1,0:T(8,128)(2,1)S(1)}, bf16[256,512]{1,0:T(8,128)(2,1)S(1)}, u32[]{:S(2)}, u32[]{:S(2)}) collective-permute-start(bf16[256,512]{1,0:T(8,128)(2,1)S(1)} %slice.130), channel_id=1, source_target_pairs={{0,4},{4,0},{1,5},{5,1},{2,6},{6,2},{3,7},{7,3},{8,12},{12,8},{9,1... | collective-permute-start | bytes 786440 | tf_op jit(solution)/shard_map/ppermute | solution.py:35
  96.8 21.1 %collective-permute-start.28 = (bf16[256,512]{1,0:T(8,128)(2,1)S(1)}, bf16[256,512]{1,0:T(8,128)(2,1)}, u32[]{:S(2)}, u32[]{:S(2)}) collective-permute-start(bf16[256,512]{1,0:T(8,128)(2,1)S(1)} %slice.136), channel_id=1, source_target_pairs={{0,4},{4,0},{1,5},{5,1},{2,6},{6,2},{3,7},{7,3},{8,12},{12,8},{9,1... | collective-permute-start | bytes 786440 | tf_op jit(solution)/shard_map/ppermute | solution.py:35
  98.3 26.2 %collective-permute-start.30 = (bf16[512,512]{1,0:T(8,128)(2,1)}, bf16[512,512]{1,0:T(8,128)(2,1)}, u32[]{:S(2)}, u32[]{:S(2)}) collective-permute-start(bf16[512,512]{1,0:T(8,128)(2,1)} %compact_rows.3.refs_0_), channel_id=1, source_target_pairs={{0,1},{1,0},{2,3},{3,2},{4,5},{5,4},{6,7},{7,6},{8,9},{9,8},{10,11... | collective-permute-start | bytes 1572872 | tf_op jit(solution)/shard_map/ppermute | solution.py:37
  100.3 19.1 %collective-permute-start.29 = (bf16[256,512]{1,0:T(8,128)(2,1)}, bf16[256,512]{1,0:T(8,128)(2,1)}, u32[]{:S(2)}, u32[]{:S(2)}) collective-permute-start(bf16[256,512]{1,0:T(8,128)(2,1)} %slice.137), channel_id=1, source_target_pairs={{0,2},{1,3},{2,0},{3,1},{4,6},{5,7},{6,4},{7,5},{8,10},{9,11},{10,... | collective-permute-start | bytes 786440 | tf_op jit(solution)/shard_map/ppermute | solution.py:37
  109.8 15.3 %collective-permute-start.32 = (bf16[512,512]{1,0:T(8,128)(2,1)}, bf16[512,512]{1,0:T(8,128)(2,1)}, u32[]{:S(2)}, u32[]{:S(2)}) collective-permute-start(bf16[512,512]{1,0:T(8,128)(2,1)} %collective-permute-done.27.refs_2_), channel_id=1, source_target_pairs={{0,1},{1,0},{2,3},{3,2},{4,5},{5,4},{6,7},{7,6},{8,9},{9,8},{10,11... | collective-permute-start | bytes 1572872 | tf_op jit(solution)/shard_map/ppermute | solution.py:37
  119.4 18.5 %collective-permute-start.13 = (bf16[512,512]{1,0:T(8,128)(2,1)S(1)}, bf16[512,512]{1,0:T(8,128)(2,1)S(1)}, u32[]{:S(2)}, u32[]{:S(2)}) collective-permute-start(bf16[512,512]{1,0:T(8,128)(2,1)S(1)} %compact_rows.2.refs_0_), channel_id=1, source_target_pairs={{0,1},{1,0},{2,3},{3,2},{4,5},{5,4},{6,7},{7,6},{8,9},{9,8},{10,11... | collective-permute-start | bytes 1572872 | tf_op jit(solution)/shard_map/ppermute | solution.py:37
  174.2 16.2 %collective-permute-start.36 = (bf16[512,512]{1,0:T(8,128)(2,1)S(1)}, bf16[512,512]{1,0:T(8,128)(2,1)S(1)}, u32[]{:S(2)}, u32[]{:S(2)}) collective-permute-start(bf16[512,512]{1,0:T(8,128)(2,1)S(1)} %pad_maximum_fusion.1), channel_id=1, source_target_pairs={{0,2},{1,3},{2,0},{3,1},{4,6},{5,7},{6,4},{7,5},{8,10},{9,11},{10,... | collective-permute-start | bytes 1572872 | tf_op jit(solution)/shard_map/ppermute | solution.py:37
  198.7 28.7 %collective-permute-start.52 = (f32[4,4096]{1,0:T(4,128)S(1)}, f32[4,4096]{1,0:T(4,128)S(1)}, u32[]{:S(2)}, u32[]{:S(2)}) collective-permute-start(f32[4,4096]{1,0:T(4,128)S(1)} %add.240), channel_id=1, source_target_pairs={{0,16},{8,24},{16,0},{24,8},{1,17},{9,25},{17,1},{25,9},{2,18},{10... | collective-permute-start | bytes 196616 | tf_op jit(solution)/shard_map/ppermute | solution.py:437
  200.7 17.9 %collective-permute-start.39 = (bf16[128,512]{1,0:T(8,128)(2,1)S(1)}, bf16[128,512]{1,0:T(8,128)(2,1)S(1)}, u32[]{:S(2)}, u32[]{:S(2)}) collective-permute-start(bf16[128,512]{1,0:T(8,128)(2,1)S(1)} %get-tuple-element.43), channel_id=1, source_target_pairs={{0,8},{8,16},{16,24},{24,0},{1,9},{9,17},{17,25},{25,1},{2,10},{10... | collective-permute-start | bytes 393224 | tf_op jit(solution)/shard_map/ppermute | solution.py:42
  204.6 15.5 %collective-permute-start.46 = (bf16[256,512]{1,0:T(8,128)(2,1)S(1)}, bf16[256,512]{1,0:T(8,128)(2,1)S(1)}, u32[]{:S(2)}, u32[]{:S(2)}) collective-permute-start(bf16[256,512]{1,0:T(8,128)(2,1)S(1)} %pad_maximum_fusion.6), channel_id=1, source_target_pairs={{0,24},{8,0},{16,8},{24,16},{1,25},{9,1},{17,9},{25,17},{2,26},{10... | collective-permute-start | bytes 786440 | tf_op jit(solution)/shard_map/ppermute | solution.py:42
  218.7 16.2 %collective-permute-start.40 = (bf16[256,512]{1,0:T(8,128)(2,1)S(1)}, bf16[256,512]{1,0:T(8,128)(2,1)S(1)}, u32[]{:S(2)}, u32[]{:S(2)}) collective-permute-start(bf16[256,512]{1,0:T(8,128)(2,1)S(1)} %pad_maximum_fusion.3), channel_id=1, source_target_pairs={{0,8},{8,16},{16,24},{24,0},{1,9},{9,17},{17,25},{25,1},{2,10},{10... | collective-permute-start | bytes 786440 | tf_op jit(solution)/shard_map/ppermute | solution.py:42
  (59 other events, 719.5 us)

commit v2 on v0

v2 whole, which is shorter than its diff:
```python
import functools
import math

import jax
import jax.numpy as jnp
from jax import lax
from jax.experimental import pallas as pl
from jax.experimental.pallas import tpu as pltpu
from jax.sharding import Mesh
from jax.sharding import PartitionSpec as P

BF = jnp.bfloat16
F32 = jnp.float32
CORE = 2
VMEM_LIMIT = 24 * 1024 * 1024


def dot(a, b, da, db):
    return lax.dot_general(a, b, (((da,), (db,)), ((), ())), preferred_element_type=F32)


def flip(x, bit):
    if bit == 1:
        return lax.ppermute(x, "half", [(0, 1), (1, 0)])
    n = lax.axis_size("tensor")
    return lax.ppermute(x, "tensor", [(i, i ^ (bit >> 1)) for i in range(n)])


def chip_masks(slots):
    return sorted((m for m in range(slots) if not m & CORE), key=lambda m: (m.bit_count(), m))


def top_bit(m):
    return 1 << (m.bit_length() - 1)


def plane_gather(own, slots, *before):
    half = own.shape[0] // 2
    blocks = {0: [(0, own)]}
    for m in chip_masks(slots)[1:]:
        low, high = m & -m, top_bit(m)
        if low == high:
            blocks[m] = [(0, flip(own, m))]
        else:
            first = rows_of(blocks[m ^ low], 0, half)
            second = rows_of(blocks[m ^ high], half, half)
            if before:
                first, second = after(first, *before), after(second, *before)
            blocks[m] = [(0, flip(first, low)), (half, flip(second, high))]
    for m in chip_masks(slots):
        blocks[m | CORE] = [(at, flip(x, CORE)) for at, x in blocks[m]]
    return blocks


def rows_of(pieces, start, count):
    for at, x in pieces:
        if at == start and x.shape[0] == count:
            return x
        if at <= start and start + count <= at + x.shape[0]:
            return x[start - at : start - at + count]
    raise ValueError("rows split")


def after(x, *others):
    return lax.optimization_barrier((x, *others))[0]


def join(*arrays):
    return lax.optimization_barrier(arrays)


class Tiles:
    def __init__(self, x, axis, count, first=0):
        self.x, self.axis, self.count, self.first = x, axis, count, first
        self.size = x.shape[axis] // (2 * lax.axis_size("tensor"))

    def at(self, ref, order_ref, j):
        here = block_at(order_ref[self.first + j], self.size)
        return ref.at[here, :] if self.axis == 0 else ref.at[:, here]


def call(kernel, name, flops, outs, smem, *args):
    flat_args = list(smem)
    for x in args:
        if isinstance(x, Tiles):
            x = x.x
        elif isinstance(x, list):
            x = pltpu.with_memory_space_constraint(x[0], pltpu.HBM)
        flat_args.append(x)

    def run(*refs):
        scalars, refs = refs[: len(smem)], list(refs[len(smem) :])
        for i, x in enumerate(args):
            if isinstance(x, Tiles):
                refs[i] = [x.at(refs[i], scalars[0], j) for j in range(x.count)]
        kernel(*scalars, *refs)

    moved = sum(a.size * a.dtype.itemsize for a in flat_args) + 4 * sum(math.prod(o.shape) for o in outs)
    return pl.pallas_call(
        run,
        in_specs=[pl.BlockSpec(memory_space=pltpu.SMEM)] * len(smem)
        + [pl.BlockSpec(memory_space=pltpu.VMEM)] * len(args),
        out_specs=[pl.BlockSpec(memory_space=pltpu.VMEM)] * len(outs),
        out_shape=outs,
        compiler_params=pltpu.CompilerParams(vmem_limit_bytes=VMEM_LIMIT),
        cost_estimate=pl.CostEstimate(flops=int(flops), bytes_accessed=int(moved), transcendentals=0),
        name=name,
    )(*flat_args)


def shaped(*shape, dtype=F32):
    return jax.ShapeDtypeStruct(shape, dtype)


def block_at(start, size):
    return pl.ds(pl.multiple_of(start * size, size), size)


def stage(*arrays):
    def kernel(*refs):
        sources, results, ready = refs[: len(arrays)], refs[len(arrays) : -1], refs[-1]
        copies = [
            pltpu.make_async_copy(x, y, ready.at[i]) for i, (x, y) in enumerate(zip(sources, results))
        ]
        for copy in copies:
            copy.start()
        for copy in copies:
            copy.wait()

    return pl.pallas_call(
        kernel,
        in_specs=[pl.BlockSpec(memory_space=pltpu.HBM)] * len(arrays),
        out_specs=[pl.BlockSpec(memory_space=pltpu.VMEM)] * len(arrays),
        out_shape=[pltpu.VMEM(x.shape, x.dtype) for x in arrays],
        scratch_shapes=[pltpu.SemaphoreType.DMA((len(arrays),))],
        compiler_params=pltpu.CompilerParams(vmem_limit_bytes=VMEM_LIMIT),
        cost_estimate=pl.CostEstimate(
            flops=0, bytes_accessed=sum(2 * x.size * x.dtype.itemsize for x in arrays), transcendentals=0
        ),
        name="stage_weights",
    )(*arrays)


def pack(firsts, chosen_cols, source, bucket):
    experts = chosen_cols.shape[1]
    rows, features = source.shape
    width = features // 2

    def kernel(firsts_ref, chosen_ref, source_ref, out, hot_out):
        for e in range(experts):
            picked = chosen_ref[pl.ds(firsts_ref[e + 1], bucket), :][:, e : e + 1] - firsts_ref[0]
            hot = lax.broadcasted_iota(jnp.int32, (bucket, rows), 1) == picked
            hot = hot.astype(F32).astype(BF)
            hot_out[e] = hot
            got = dot(hot, source_ref[...], 1, 0).astype(BF)
            out[2 * e], out[2 * e + 1] = got[:, :width], got[:, width:]

    flops = 2 * experts * bucket * rows * features
    outs = [
        shaped(2 * experts, bucket, width, dtype=BF),
        shaped(experts, bucket, rows, dtype=BF),
    ]
    return call(kernel, "pack_rows", flops, outs, [firsts], chosen_cols, source)


def compact(reach, buckets, cap):
    homes, bucket, width = buckets.shape

    def kernel(reach_ref, buckets_ref, out):
        acc = None
        for s in range(homes):
            at = lax.broadcasted_iota(jnp.int32, (cap, bucket), 0) - reach_ref[s]
            hot = lax.broadcasted_iota(jnp.int32, (cap, bucket), 1) == at
            term = dot(hot.astype(F32).astype(BF), buckets_ref[s], 1, 0)
            acc = term if acc is None else acc + term
        out[...] = acc.astype(BF)

    flops = 2 * cap * homes * bucket * width
    outs = [shaped(cap, width, dtype=BF)]
    return call(kernel, "compact_rows", flops, outs, [reach], buckets)[0]


def place(reach, homes, bucket, terms):
    cap, width = terms[0].shape

    def kernel(reach_ref, *refs):
        total = refs[0][...].astype(F32)
        for r in refs[1:-1]:
            total = total + r[...].astype(F32)
        rows = total.astype(BF)
        for s in range(homes):
            at = lax.broadcasted_iota(jnp.int32, (bucket, cap), 1) - reach_ref[s]
            hot = lax.broadcasted_iota(jnp.int32, (bucket, cap), 0) == at
            refs[-1][s] = dot(hot.astype(F32).astype(BF), rows, 1, 0).astype(BF)

    flops = 2 * cap * homes * bucket * width
    outs = [shaped(homes, bucket, width, dtype=BF)]
    return call(kernel, "place_rows", flops, outs, [reach], *terms)[0]


def combine(hots, returned):
    experts, bucket, rows = hots.shape
    width = returned.shape[2]

    def kernel(hots_ref, returned_ref, out):
        for h in range(2):
            acc = None
            for e in range(experts):
                term = dot(hots_ref[e], returned_ref[2 * e + h], 0, 0)
                acc = term if acc is None else acc + term
            out[:, h * width : (h + 1) * width] = acc.astype(BF)

    flops = 4 * experts * bucket * rows * width
    outs = [shaped(rows, 2 * width, dtype=BF)]
    return call(kernel, "combine_rows", flops, outs, [], hots, returned)[0]


def flat(blocks, keys):
    spots = [(j, at, x.shape[0]) for j, m in enumerate(keys) for at, x in blocks[m]]
    return spots, [x for m in keys for _, x in blocks[m]]


def add_rows(total, at, rows, values):
    done = []
    for start, old in total:
        size = old.shape[0]
        if at <= start and start + size <= at + rows:
            done.append((start, old + values[start - at : start - at + size]))
        elif start <= at and at + rows <= start + size:
            cuts = [(start, old[: at - start]), (at, old[at - start : at - start + rows] + values)]
            cuts.append((at + rows, old[at - start + rows :]))
            done += [c for c in cuts if c[1].shape[0]]
        else:
            done.append((start, old))
    return done


def product(spots, ins, tiles, side):
    total = None
    for (j, at, rows), x in zip(spots, ins):
        term = dot(x[...], tiles[j][...], 1, side)
        total = [(at, term)] if total is None else add_rows(total, at, rows, term)
    return total


def project_in(order, expert, blocks, keys, w_in, router):
    spots, xs = flat(blocks, keys)
    cap, width = blocks[0][0][1].shape
    hidden = w_in.shape[1]
    experts = router.shape[1]

    def kernel(order_ref, expert_ref, *refs):
        ins, (tiles, r_ref, a_ref, gate_ref) = refs[: len(xs)], refs[len(xs) :]
        scores = None
        for (j, at, rows), x in zip(spots, ins):
            s = dot(x[...], r_ref[block_at(order_ref[j], width), :], 1, 0)
            scores = [(at, s)] if scores is None else add_rows(scores, at, rows, s)
            a = dot(x[...], tiles[j][...], 1, 0)
            if j == 0:
                a_ref[at : at + rows, :] = a
            else:
                a_ref[at : at + rows, :] += a
        for at, s in scores:
            mine = lax.broadcasted_iota(jnp.int32, s.shape, 1) == expert_ref[0]
            picked = jnp.sum(jnp.where(mine, s, 0.0), axis=1, keepdims=True)
            gate_ref[at : at + s.shape[0], :] = jax.nn.sigmoid(picked)

    flops = 2 * cap * width * len(keys) * hidden
    outs = [shaped(cap, hidden), shaped(cap, 1)]
    tiles = Tiles(w_in, 0, len(keys))
    return call(kernel, "project_in", flops, outs, [order, expert], *[[x] for x in xs], tiles, router)


def project_out(order, blocks, keys, w_out):
    spots, ys = flat(blocks, keys)
    cap, width = blocks[0][0][1].shape
    hidden = w_out.shape[0]

    def kernel(order_ref, *refs):
        ins, (tiles, up) = refs[: len(ys)], refs[len(ys) :]
        for (j, at, rows), y in zip(spots, ins):
            u = dot(y[...], tiles[j][...], 1, 1)
            if j == 0:
                up[at : at + rows, :] = u
            else:
                up[at : at + rows, :] += u

    flops = 2 * cap * width * len(keys) * hidden
    tiles = Tiles(w_out, 1, len(keys))
    return call(kernel, "project_out", flops, [shaped(cap, hidden)], [order], *ys, tiles)[0]


def activation(order, blocks, keys, far, near, w_out, w_in, router_row, upstream, pre_act, gate):
    spots, ys = flat(blocks, keys)
    width = blocks[0][0][1].shape[1]
    cap, hidden = pre_act.shape
    count = sum(far) + sum(near)

    def kernel(order_ref, *refs):
        ins, refs = refs[: len(ys)], refs[len(ys) :]
        tiles, back, r_ref, u_ref, a_ref, gate_ref, hg_ref, da_ref, ds_ref, *outs = refs
        up = [(0, u_ref[...])]
        for (j, at, rows), y in zip(spots, ins):
            up = add_rows(up, at, rows, dot(y[...], tiles[j][...], 1, 1))
        for at, u in up:
            place = slice(at, at + u.shape[0])
            a = a_ref[place, :]
            gate = gate_ref[place, :]
            sig = jax.nn.sigmoid(a)
            act = a * sig
            hg_ref[place, :] = (gate * act).astype(BF)
            gate_grad = jnp.sum(act * u, axis=1, keepdims=True)
            ds_ref[place, :] = gate_grad * gate * (1.0 - gate)
            da_ref[place, :] = (gate * u * sig * (1.0 + a * (1.0 - sig))).astype(BF)
        places = [(out, k) for out, n in zip(outs, far + near) for k in range(n)]
        for k, (out, spot) in enumerate(places):
            here = block_at(order_ref[len(keys) + k], width)
            block = dot(da_ref[...], back[k][...], 1, 1) + ds_ref[...] * r_ref[:, here]
            out[spot] = block.astype(out.dtype)

    flops = 2 * cap * width * (len(keys) + count) * hidden
    outs = [shaped(cap, hidden, dtype=BF), shaped(cap, hidden, dtype=BF), shaped(cap, 1)]
    outs += [shaped(n, cap, width, dtype=BF) for n in far] + [shaped(n, cap, width) for n in near]
    tiles, back = Tiles(w_out, 1, len(keys)), Tiles(w_in, 0, count, len(keys))
    more = (tiles, back, router_row, upstream, pre_act, gate)
    return call(kernel, "activation", flops, outs, [order], *ys, *more)


def router_column(order, blocks, keys, score_grad):
    spots, xs = flat(blocks, keys)
    width = blocks[0][0][1].shape[1]

    def kernel(order_ref, *refs):
        ins, (ds_ref, col) = refs[: len(xs)], refs[len(xs) :]
        for j in range(len(keys)):
            line = None
            for (k, at, rows), x in zip(spots, ins):
                if k == j:
                    c = jnp.sum(x[...].astype(F32) * ds_ref[at : at + rows, :], axis=0, keepdims=True)
                    line = c if line is None else line + c
            col[:, block_at(order_ref[j], width)] = line

    flops = 2 * score_grad.shape[0] * width * len(keys)
    outs = [shaped(1, width * len(keys))]
    return call(kernel, "router_column", flops, outs, [order], *[[x] for x in xs], score_grad)[0]


def grads_in(order, blocks, keys, pre_grad):
    spots, xs = flat(blocks, keys)
    cap, width = blocks[0][0][1].shape
    hidden = pre_grad.shape[1]

    def kernel(order_ref, *refs):
        ins, (da_ref, out) = refs[: len(xs)], refs[len(xs) :]
        for j in range(len(keys)):
            grad = None
            for (k, at, rows), x in zip(spots, ins):
                if k == j:
                    g = dot(x[...], da_ref[at : at + rows, :], 0, 0)
                    grad = g if grad is None else grad + g
            out[block_at(order_ref[j], width), :] = grad.astype(BF)

    flops = 2 * cap * width * len(keys) * hidden
    outs = [shaped(width * len(keys), hidden, dtype=BF)]
    return call(kernel, "grads_in", flops, outs, [order], *[[x] for x in xs], pre_grad)[0]


def grads_out(order, blocks, keys, gated):
    spots, ys = flat(blocks, keys)
    cap, width = blocks[0][0][1].shape
    hidden = gated.shape[1]

    def kernel(order_ref, *refs):
        ins, (hg_ref, out) = refs[: len(ys)], refs[len(ys) :]
        for j in range(len(keys)):
            grad = None
            for (k, at, rows), y in zip(spots, ins):
                if k == j:
                    g = dot(hg_ref[at : at + rows, :], y[...], 0, 0)
                    grad = g if grad is None else grad + g
            out[:, block_at(order_ref[j], width)] = grad.astype(BF)

    flops = 2 * cap * width * len(keys) * hidden
    outs = [shaped(hidden, width * len(keys), dtype=BF)]
    return call(kernel, "grads_out", flops, outs, [order], *ys, gated)[0]


def numbers(values):
    return jnp.stack(values).astype(jnp.int32)


def body(tokens, cotangent, w_in, w_out, router, chosen):
    planes = lax.axis_size("plane")
    slots = 2 * lax.axis_size("tensor")
    tok_dev, features = tokens.shape
    width = features // slots
    cap = chosen.shape[1]
    plane = lax.axis_index("plane")
    half = lax.axis_index("half")
    slot = lax.axis_index("tensor") * 2 + half
    homes = 2 * planes
    bucket = 4 * tok_dev // homes
    expert = plane.astype(jnp.int32)[None]
    router_row = lax.dynamic_slice_in_dim(router.T, plane, 1, 0).astype(F32)
    masks = chip_masks(slots)
    first = ((plane * 2 + half) * tok_dev).astype(jnp.int32)
    before_me = jnp.sum((chosen < first).astype(jnp.int32), axis=1)
    firsts = jnp.concatenate([first[None], before_me])
    chosen_cols = jnp.pad(chosen.T, ((0, bucket), (0, 0)), constant_values=-1)
    mine = lax.dynamic_slice_in_dim(chosen, plane, 1, 0)
    edges = jnp.arange(homes, dtype=jnp.int32)[:, None] * tok_dev
    reach = jnp.sum((mine < edges).astype(jnp.int32), axis=1)

    def tensor_slice(source):
        return lax.dynamic_slice_in_dim(source, (slot // 2) * 2 * width, 2 * width, 1)

    def exchange(x):
        return lax.all_to_all(x, ("plane", "half"), split_axis=0, concat_axis=0, tiled=True)

    def order_of(*keys):
        return numbers([slot ^ m for m in keys])

    x_sent, hots = pack(firsts, chosen_cols, tensor_slice(tokens), bucket)
    x_got = exchange(x_sent)
    w_in, w_out, _ = join(w_in, w_out, x_sent)
    w_in, w_out = stage(w_in, w_out)
    y_sent, _ = pack(firsts, chosen_cols, tensor_slice(cotangent), bucket)
    x_got, y_sent, w_in, w_out = join(x_got, y_sent, w_in, w_out)
    y_got = exchange(y_sent)
    xs = plane_gather(compact(reach, x_got, cap), slots)
    pieces = [x for m in xs for _, x in xs[m]]
    y_got, *pieces = join(y_got, *pieces)
    xs = {m: [(at, pieces.pop(0)) for at, _ in xs[m]] for m in xs}
    late = [m for m in masks if m.bit_count() > 1]
    late += [m | CORE for m in late]
    early = [m for m in xs if m not in late]
    keys = early + late
    order = order_of(*keys)
    pre_act, gate = project_in(order, expert, xs, keys, w_in, router)
    ys = plane_gather(compact(reach, y_got, cap), slots, pre_act)
    upstream = project_out(order_of(*early), ys, early, w_out)

    groups = [[m for m in masks if m.bit_count() > 1], [m for m in masks if m.bit_count() <= 1]]
    groups = [g[::-1] for g in groups]
    sizes = [len(g) for g in groups]
    near = [m for g in groups for m in g]
    gated, pre_grad, score_grad, far1, far2, near1, near2 = activation(
        order_of(*late, *[m | CORE for m in near], *near),
        ys,
        late,
        sizes,
        sizes,
        w_out,
        w_in,
        router_row,
        upstream,
        pre_act,
        gate,
    )
    hops = [
        lambda x, step=1 << i: lax.ppermute(x, "plane", [(e, e ^ step) for e in range(planes)])
        for i in range(planes.bit_length() - 1)
    ]
    hops += [functools.partial(flip, bit=1 << i) for i in reversed(range(slots.bit_length() - 1))]

    def hop(total):
        return total + hops.pop(0)(total) if hops else total

    mid = cap // 2
    got1, got2 = flip(far1, CORE), flip(far2, CORE)
    column = router_column(order, xs, keys, score_grad)
    got1, got2, column = join(got1, got2, column)
    total = jnp.where(jnp.arange(planes)[:, None] == plane, column, 0.0)
    sums = {m: near1[k] + got1[k].astype(F32) for k, m in enumerate(groups[0])}
    sums.update({m: near2[k] + got2[k].astype(F32) for k, m in enumerate(groups[1])})
    total = hop(total)
    for m in groups[0]:
        low, high = m & -m, top_bit(m)
        a, b = flip(sums[m][:mid].astype(BF), low), flip(sums[m][mid:].astype(BF), high)
        a, b, total, *rest = join(a, b, total, *[sums[k] for k in groups[1]])
        sums.update(zip(groups[1], rest))
        pad = jnp.zeros((cap - mid, width), F32)
        sums[m ^ low] = sums[m ^ low] + jnp.concatenate([a.astype(F32), pad])
        sums[m ^ high] = sums[m ^ high] + jnp.concatenate([pad, b.astype(F32)])
    sent = [sums[m].astype(BF) for m in groups[1] if m]
    *sent, total, pre_grad = join(*sent, total, pre_grad)
    came = [flip(x, m) for x, m in zip(sent, groups[1])]
    grad_in = grads_in(order, xs, keys, pre_grad)
    total = hop(total)
    *terms, grad_in, total = join(sums[0], *came, grad_in, total)

    back = place(reach, homes, bucket, terms)
    returned = exchange(back)
    grad_out = grads_out(order, ys, keys, after(gated, back))
    total = after(total, grad_out)
    while hops:
        total = hop(total)
    returned, grad_out, total = join(returned, grad_out, total)
    return (combine(hots, returned), grad_in, grad_out, total.T)


def solution(mesh):
    planes = mesh.shape["expert"] // 2
    inner = Mesh(mesh.devices.reshape(planes, 2, mesh.shape["tensor"]), ("plane", "half", "tensor"))
    home = ("plane", "half")
    every = ("plane", "half", "tensor")
    return jax.shard_map(
        body,
        mesh=inner,
        in_specs=(P(home, None), P(home, None), P(None, every), P(every, None), P(), P()),
        out_specs=(P(home, "tensor"), P(None, every), P(every, None), P()),
        check_vma=False,
    )
```

time: 727 us -> 177 us (0.24)
  waiting for transfers between devices: 375 us -> 69.7 us
  blocking collectives: 190 us -> 0 us
  local copies, waits for them, and re-layouts: 64.9 us -> 24.5 us
  Pallas kernels: 0 us -> 39.6 us
  matrix products: 35.8 us -> 0 us
  other arithmetic: 32.3 us -> 2.92 us
  starting transfers between devices: 11 us -> 38.3 us
  between operations: 15.7 us -> 1.05 us
    all_to_all x2 -> x3, waiting for transfers between devices: 233 us -> 17.9 us  [exchange(): lax.all_to_all(x, ('plane', 'half'), split_axis=0, concat_axis=0, tiled=T...]
    all_to_all x1 -> x0, blocking collectives: 190 us -> none  [body(): lax.all_to_all(pack(tokens), 'expert', split_axis=0, concat_axis=0, tiled...]
    psum x1 -> x0, waiting for transfers between devices: 71.2 us -> none  [body(): grad_router = lax.psum(router_term, ('expert', 'tensor'))]
    reduce_scatter x1 -> x0, waiting for transfers between devices: 71 us -> none  [body(): lax.psum_scatter(jnp.dot(w_in, pre_grad.T, preferred_element_type=jnp.flo...]
    gather x8 -> x0, local copies, waits for them, and re-layouts: 57.7 us -> none  [the longest x2 24.7 us: pack(): source[send_rows]]
    ppermute x0 -> x29, waiting for transfers between devices: none -> 51.8 us  [the longest x20 31.1 us: flip(): return lax.ppermute(x, 'tensor', [(i, i ^ bit >> 1) for i in range(n)])]
    pallas_call x0 -> x13, Pallas kernels: none -> 39.6 us  [the longest x12 39.1 us: call(): pl.pallas_call(run, in_specs=[pl.BlockSpec(memory_space=pltpu.SMEM)] * le...]
    dot_general x7 -> x0, matrix products: 35.8 us -> none  [the longest x1 6.76 us: body(): jnp.dot(x_rows.T, pre_grad, preferred_element_type=jnp.float32)]
  transfers between devices with their start and end apart: 4 -> 32, of which waited for: 4 -> 19; matrix products, arithmetic and copies ran while one was open for 8% -> 2% of each run, Pallas kernels for 0% -> 16%
where the time goes in v2:
time: 177 us; the launch traced here: 176 us
  waiting for transfers between devices  69.7 us (39%)
  Pallas kernels  39.6 us (22%)
  starting transfers between devices  38.3 us (22%)
  local copies, waits for them, and re-layouts  24.5 us (14%)
  other arithmetic  2.92 us (2%)
    pallas_call x12, Pallas kernels, call(): pl.pallas_call(run, in_specs=[pl.BlockSpec(memory_space=pltpu.SMEM)] * le...  39.1 us
    ppermute x20, waiting for transfers between devices, flip(): return lax.ppermute(x, 'tensor', [(i, i ^ bit >> 1) for i in range(n)])  31.1 us
    unnamed x60, local copies, waits for them, and re-layouts  22.1 us
    ppermute x7, waiting for transfers between devices, flip(): return lax.ppermute(x, 'half', [(0, 1), (1, 0)])  20 us
    all_to_all x3, waiting for transfers between devices, exchange(): lax.all_to_all(x, ('plane', 'half'), split_axis=0, concat_axis=0, tiled=T...  17.9 us
    all_to_all x3, starting transfers between devices, exchange(): lax.all_to_all(x, ('plane', 'half'), split_axis=0, concat_axis=0, tiled=T...  15.3 us
    ppermute x20, starting transfers between devices, flip(): return lax.ppermute(x, 'tensor', [(i, i ^ bit >> 1) for i in range(n)])  10.8 us
    ppermute x7, starting transfers between devices, flip(): return lax.ppermute(x, 'half', [(0, 1), (1, 0)])  7.74 us
  transfers between devices with their start and end apart: 32, of which 19 were waited for; matrix products, arithmetic and copies ran while one was open for 2% of the time, Pallas kernels for 16%

profile of v2, /device:TPU:0, one launch (start us, length us, event | category | flops | bytes accessed | tf_op | source)
XLA Modules:
  0.0 176.1 jit_solution(10238165379974776389)
XLA Ops:
  6.5 7.2 %all-to-all-start = ((bf16[8,128,512]{2,1,0:T(8,128)(2,1)}), bf16[8,128,512]{2,1,0:T(8,128)(2,1)S(1)}, u32[]{:S(2)}, u32[]{:S(2)}) async-start(bf16[8,128,512]{2,1,0:T(8,128)(2,1)} %get-tuple-element.61), calls=%async_computation | async-start | bytes 2097152 | tf_op jit(solution)/shard_map/all_to_all | solution.py:418
  15.9 2.2 %copy-done.7 = bf16[512,4096]{1,0:T(8,128)(2,1)S(1)} copy-done((bf16[512,4096]{1,0:T(8,128)(2,1)S(1)}, bf16[512,4096]{1,0:T(8,128)(2,1)}, u32[]{:S(2)}) %copy-start.7) | copy-done | bytes 4194328
  24.8 14.7 %all-to-all-done.refs_1_ = bf16[8,128,512]{2,1,0:T(8,128)(2,1)S(1)} async-done(((bf16[8,128,512]{2,1,0:T(8,128)(2,1)}), bf16[8,128,512]{2,1,0:T(8,128)(2,1)S(1)}, u32[]{:S(2)}, u32[]{:S(2)}) %all-to-all-start) | async-done | bytes 1048608 | tf_op jit(solution)/shard_map/all_to_all | solution.py:418
  39.5 3.7 %all-to-all-start.1 = ((bf16[8,128,512]{2,1,0:T(8,128)(2,1)}), bf16[8,128,512]{2,1,0:T(8,128)(2,1)S(1)}, u32[]{:S(2)}, u32[]{:S(2)}) async-start(bf16[8,128,512]{2,1,0:T(8,128)(2,1)} %get-tuple-element.67), calls=%async_computation.1 | async-start | bytes 2097152 | tf_op jit(solution)/shard_map/all_to_all | solution.py:418
  49.5 10.0 %collective-permute-done.1.refs_4_.refs_3_ = bf16[512,512]{1,0:T(8,128)(2,1)S(1)} collective-permute-done((bf16[512,512]{1,0:T(8,128)(2,1)S(1)}, bf16[512,512]{1,0:T(8,128)(2,1)S(1)}, u32[]{:S(2)}, u32[]{:S(2)}) %collective-permute-start.1) | collective-permute-done | bytes 524320 | tf_op jit(solution)/shard_map/ppermute | solution.py:26
  61.3 7.4 %collective-permute-done.refs_3_.refs_2_ = bf16[512,512]{1,0:T(8,128)(2,1)S(1)} collective-permute-done((bf16[512,512]{1,0:T(8,128)(2,1)S(1)}, bf16[512,512]{1,0:T(8,128)(2,1)S(1)}, u32[]{:S(2)}, u32[]{:S(2)}) %collective-permute-start) | collective-permute-done | bytes 524320 | tf_op jit(solution)/shard_map/ppermute | solution.py:24
  71.1 2.7 %collective-permute-done.2.refs_8_.refs_7_ = bf16[256,512]{1,0:T(8,128)(2,1)S(1)} collective-permute-done((bf16[256,512]{1,0:T(8,128)(2,1)S(1)}, bf16[256,512]{1,0:T(8,128)(2,1)S(1)}, u32[]{:S(2)}, u32[]{:S(2)}) %collective-permute-start.2) | collective-permute-done | bytes 262176 | tf_op jit(solution)/shard_map/ppermute | solution.py:24
  73.8 2.3 %collective-permute-done.3.refs_9_.refs_8_ = bf16[256,512]{1,0:T(8,128)(2,1)S(1)} collective-permute-done((bf16[256,512]{1,0:T(8,128)(2,1)S(1)}, bf16[256,512]{1,0:T(8,128)(2,1)S(1)}, u32[]{:S(2)}, u32[]{:S(2)}) %collective-permute-start.3) | collective-permute-done | bytes 262176 | tf_op jit(solution)/shard_map/ppermute | solution.py:26
  85.1 5.6 %project_in.1 = (f32[512,512]{1,0:T(8,128)S(1)}, f32[512,1]{1,0:T(8,128)S(1)}) custom-call(s32[8]{0:T(128)S(1)} %stack.58.refs_0_, s32[1]{0:T(128)} %bitcast.11.refs_1_, bf16[512,512]{1,0:T(8,128)(2,1)} %copy-done.5, bf16[512,512]{1,0:T(8,128)(2,1)} %copy-done.21, bf16[512,512]{1,0:T(8,128)(2,1)} %copy-done.20, bf16[512,512]{1,0:T(8,128)(2,1)} %copy-done.22, ...), custom_call_target="tpu_custom_call" | custom-call | flops 2147483648 | bytes 9472036 | tf_op jit(solution)/shard_map/project_in/pallas_call | solution.py:99
  91.4 3.5 %collective-permute-done.11.refs_2_ = bf16[512,512]{1,0:T(8,128)(2,1)S(1)} collective-permute-done((bf16[512,512]{1,0:T(8,128)(2,1)S(1)}, bf16[512,512]{1,0:T(8,128)(2,1)S(1)}, u32[]{:S(2)}, u32[]{:S(2)}) %collective-permute-start.11) | collective-permute-done | bytes 524320 | tf_op jit(solution)/shard_map/ppermute | solution.py:24
  97.3 5.3 %collective-permute-done.12.refs_2_.refs_8_ = bf16[256,512]{1,0:T(8,128)(2,1)S(1)} collective-permute-done((bf16[256,512]{1,0:T(8,128)(2,1)S(1)}, bf16[256,512]{1,0:T(8,128)(2,1)S(1)}, u32[]{:S(2)}, u32[]{:S(2)}) %collective-permute-start.12) | collective-permute-done | bytes 262176 | tf_op jit(solution)/shard_map/ppermute | solution.py:26
  104.0 2.4 %copy-done.4 = bf16[512,4096]{1,0:T(8,128)(2,1)S(1)} copy-done((bf16[512,4096]{1,0:T(8,128)(2,1)S(1)}, bf16[512,4096]{1,0:T(8,128)(2,1)}, u32[]{:S(2)}) %copy-start.4) | copy-done | bytes 4194328
  106.4 2.4 %project_out.1.refs_8_ = f32[512,512]{1,0:T(8,128)S(1)} custom-call(s32[6]{0:T(128)S(1)} %stack.59.refs_0_, bf16[512,512]{1,0:T(8,128)(2,1)S(1)} %compact_rows.3.refs_1_, bf16[512,512]{1,0:T(8,128)(2,1)S(1)} %collective-permute-done.11.refs_2_, bf16[512,512]{1,0:T(8,128)(2,1)S(1)} %collective-permute-done.9.refs_3_, ...), custom_call_target="tpu_custom_call" | custom-call | flops 1610612736 | bytes 8388632 | tf_op jit(solution)/shard_map/project_out/pallas_call | solution.py:99
  108.8 4.5 %activation.1 = (bf16[512,512]{1,0:T(8,128)(2,1)S(1)}, bf16[512,512]{1,0:T(8,128)(2,1)S(1)}, f32[512,1]{1,0:T(8,128)S(1)}, bf16[1,512,512]{2,1,0:T(8,128)(2,1)S(...) custom-call(s32[10]{0:T(128)S(1)} %stack.57.refs_0_, ...), custom_call_target="tpu_custom_call" | custom-call | flops 2684354560 | bytes 22040616 | tf_op jit(solution)/shard_map/activation/pallas_call | solution.py:99
  114.6 3.1 %router_column.1 = f32[1,4096]{1,0:T(1,128)S(1)} custom-call(s32[8]{0:T(128)S(1)} %stack.58.refs_0_, bf16[512,512]{1,0:T(8,128)(2,1)} %copy-done.5, bf16[512,512]{1,0:T(8,128)(2,1)} %copy-done.21, bf16[512,512]{1,0:T(8,128)(2,1)} %copy-done.20, bf16[512,512]{1,0:T(8,128)(2,1)} %copy-done.22, bf16[512,512]{1,0:T(8,128)(2,1)} %collective-permute-done.5.refs_6_.refs_5_, ...), custom_call_target="tpu_custom_call" | custom-call | flops 4194304 | bytes 4212768 | tf_op jit(solution)/shard_map/router_column/pallas_call | solution.py:99
  123.2 5.3 %collective-permute-done.21 = bf16[256,512]{1,0:T(8,128)(2,1)S(1)} collective-permute-done((bf16[256,512]{1,0:T(8,128)(2,1)S(1)}, bf16[256,512]{1,0:T(8,128)(2,1)S(1)}, u32[]{:S(2)}, u32[]{:S(2)}) %collective-permute-start.21) | collective-permute-done | bytes 262176 | tf_op jit(solution)/shard_map/ppermute | solution.py:26
  131.0 2.9 %collective-permute-start.25 = (f32[4,4096]{1,0:T(4,128)S(1)}, f32[4,4096]{1,0:T(4,128)S(1)}, u32[]{:S(2)}, u32[]{:S(2)}) collective-permute-start(f32[4,4096]{1,0:T(4,128)S(1)} %fusion), channel_id=1, source_target_pairs={{0,16},{8,24},{16,0},{24,8},{1,17},{9,25},{17,1},{25,9},{2,18},{10... | collective-permute-start | bytes 196616 | tf_op jit(solution)/shard_map/ppermute | solution.py:461
  133.9 6.6 %grads_in.1 = bf16[4096,512]{1,0:T(8,128)(2,1)} custom-call(s32[8]{0:T(128)S(1)} %stack.58.refs_0_, bf16[512,512]{1,0:T(8,128)(2,1)} %copy-done.5, bf16[512,512]{1,0:T(8,128)(2,1)} %copy-done.21, bf16[512,512]{1,0:T(8,128)(2,1)} %copy-done.20, bf16[512,512]{1,0:T(8,128)(2,1)} %copy-done.22, bf16[512,512]{1,0:T(8,128)(2,1)} %collective-permute-done.5.refs_6_.refs_5_, ...), custom_call_target="tpu_custom_call" | custom-call | flops 2147483648 | bytes 13107232 | tf_op jit(solution)/shard_map/grads_in/pallas_call | solution.py:99
  143.1 2.3 %place_rows.1 = bf16[8,128,512]{2,1,0:T(8,128)(2,1)} custom-call(s32[8]{0:T(128)S(1)} %convert_reduce_fusion.refs_0_, f32[512,512]{1,0:T(8,128)S(1)} %get-tuple-element.105.refs_1_, bf16[512,512]{1,0:T(8,128)(2,1)S(1)} %collective-permute-done.23.refs_2_, bf16[512,512]{1,0:T(8,128)(2,1)S(1)} %collective-permute-done.24.refs_3_), custom_call_target="tpu_custom_call" | custom-call | flops 536870912 | bytes 4194336 | tf_op jit(solution)/shard_map/place_rows/pallas_call | solution.py:99
  145.4 4.3 %all-to-all-start.2 = ((bf16[8,128,512]{2,1,0:T(8,128)(2,1)}), bf16[8,128,512]{2,1,0:T(8,128)(2,1)S(1)}, u32[]{:S(2)}, u32[]{:S(2)}) async-start(bf16[8,128,512]{2,1,0:T(8,128)(2,1)} %place_rows.1), calls=%async_computation.2 | async-start | bytes 2097152 | tf_op jit(solution)/shard_map/all_to_all | solution.py:418
  152.9 5.5 %grads_out.1 = bf16[512,4096]{1,0:T(8,128)(2,1)} custom-call(s32[8]{0:T(128)S(1)} %stack.58.refs_0_, bf16[512,512]{1,0:T(8,128)(2,1)S(1)} %compact_rows.3.refs_1_, bf16[512,512]{1,0:T(8,128)(2,1)S(1)} %collective-permute-done.11.refs_2_, bf16[512,512]{1,0:T(8,128)(2,1)S(1)} %collective-permute-done.9.refs_3_, ...), custom_call_target="tpu_custom_call" | custom-call | flops 2147483648 | bytes 13107232 | tf_op jit(solution)/shard_map/grads_out/pallas_call | solution.py:99
  159.4 3.3 %collective-permute-done.26 = f32[4,4096]{1,0:T(4,128)S(1)} collective-permute-done((f32[4,4096]{1,0:T(4,128)S(1)}, f32[4,4096]{1,0:T(4,128)S(1)}, u32[]{:S(2)}, u32[]{:S(2)}) %collective-permute-start.26) | collective-permute-done | bytes 65568 | tf_op jit(solution)/shard_map/ppermute | solution.py:26
  166.1 3.7 %collective-permute-done.28 = f32[4,4096]{1,0:T(4,128)S(1)} collective-permute-done((f32[4,4096]{1,0:T(4,128)S(1)}, f32[4,4096]{1,0:T(4,128)S(1)}, u32[]{:S(2)}, u32[]{:S(2)}) %collective-permute-start.28) | collective-permute-done | bytes 65568 | tf_op jit(solution)/shard_map/ppermute | solution.py:24
  170.4 3.2 %all-to-all-done.2.refs_1_ = bf16[8,128,512]{2,1,0:T(8,128)(2,1)S(1)} async-done(((bf16[8,128,512]{2,1,0:T(8,128)(2,1)}), bf16[8,128,512]{2,1,0:T(8,128)(2,1)S(1)}, u32[]{:S(2)}, u32[]{:S(2)}) %all-to-all-start.2) | async-done | bytes 1048608 | tf_op jit(solution)/shard_map/all_to_all | solution.py:418
  (140 shorter events, 61.0 us)
Async XLA Ops:
  6.5 33.0 %all-to-all-start = ((bf16[8,128,512]{2,1,0:T(8,128)(2,1)}), bf16[8,128,512]{2,1,0:T(8,128)(2,1)S(1)}, u32[]{:S(2)}, u32[]{:S(2)}) async-start(bf16[8,128,512]{2,1,0:T(8,128)(2,1)} %get-tuple-element.61), calls=%async_computation | async-start | bytes 2097152 | tf_op jit(solution)/shard_map/all_to_all | solution.py:418
  39.5 39.6 %all-to-all-start.1 = ((bf16[8,128,512]{2,1,0:T(8,128)(2,1)}), bf16[8,128,512]{2,1,0:T(8,128)(2,1)S(1)}, u32[]{:S(2)}, u32[]{:S(2)}) async-start(bf16[8,128,512]{2,1,0:T(8,128)(2,1)} %get-tuple-element.67), calls=%async_computation.1 | async-start | bytes 2097152 | tf_op jit(solution)/shard_map/all_to_all | solution.py:418
  45.9 13.6 %collective-permute-start.1 = (bf16[512,512]{1,0:T(8,128)(2,1)S(1)}, bf16[512,512]{1,0:T(8,128)(2,1)S(1)}, u32[]{:S(2)}, u32[]{:S(2)}) collective-permute-start(bf16[512,512]{1,0:T(8,128)(2,1)S(1)} %compact_rows.2.refs_2_.refs_1_), channel_id=1, source_target_pairs={{0,2},{1,3},{2,0},{3,1},{4,6},{5,7},{6,4},{7,5},{8,10},{9,11},{10,... | collective-permute-start | bytes 1572872 | tf_op jit(solution)/shard_map/ppermute | solution.py:26
  47.5 21.3 %collective-permute-start = (bf16[512,512]{1,0:T(8,128)(2,1)S(1)}, bf16[512,512]{1,0:T(8,128)(2,1)S(1)}, u32[]{:S(2)}, u32[]{:S(2)}) collective-permute-start(bf16[512,512]{1,0:T(8,128)(2,1)S(1)} %compact_rows.2.refs_2_.refs_1_), channel_id=1, source_target_pairs={{0,4},{4,0},{1,5},{5,1},{2,6},{6,2},{3,7},{7,3},{8,12},{12,8},{9,1... | collective-permute-start | bytes 1572872 | tf_op jit(solution)/shard_map/ppermute | solution.py:24
  49.5 26.6 %collective-permute-start.4 = (bf16[512,512]{1,0:T(8,128)(2,1)S(1)}, bf16[512,512]{1,0:T(8,128)(2,1)S(1)}, u32[]{:S(2)}, u32[]{:S(2)}) collective-permute-start(bf16[512,512]{1,0:T(8,128)(2,1)S(1)} %compact_rows.2.refs_2_.refs_1_), channel_id=1, source_target_pairs={{0,1},{1,0},{2,3},{3,2},{4,5},{5,4},{6,7},{7,6},{8,9},{9,8},{10,11... | collective-permute-start | bytes 1572872 | tf_op jit(solution)/shard_map/ppermute | solution.py:26
  59.5 14.3 %collective-permute-start.2 = (bf16[256,512]{1,0:T(8,128)(2,1)S(1)}, bf16[256,512]{1,0:T(8,128)(2,1)S(1)}, u32[]{:S(2)}, u32[]{:S(2)}) collective-permute-start(bf16[256,512]{1,0:T(8,128)(2,1)S(1)} %slice.52), channel_id=1, source_target_pairs={{0,4},{4,0},{1,5},{5,1},{2,6},{6,2},{3,7},{7,3},{8,12},{12,8},{9,1... | collective-permute-start | bytes 786440 | tf_op jit(solution)/shard_map/ppermute | solution.py:24
  68.8 7.3 %collective-permute-start.3 = (bf16[256,512]{1,0:T(8,128)(2,1)S(1)}, bf16[256,512]{1,0:T(8,128)(2,1)S(1)}, u32[]{:S(2)}, u32[]{:S(2)}) collective-permute-start(bf16[256,512]{1,0:T(8,128)(2,1)S(1)} %slice.53), channel_id=1, source_target_pairs={{0,2},{1,3},{2,0},{3,1},{4,6},{5,7},{6,4},{7,5},{8,10},{9,11},{10,... | collective-permute-start | bytes 786440 | tf_op jit(solution)/shard_map/ppermute | solution.py:26
  70.6 7.0 %collective-permute-start.6 = (bf16[512,512]{1,0:T(8,128)(2,1)S(1)}, bf16[512,512]{1,0:T(8,128)(2,1)S(1)}, u32[]{:S(2)}, u32[]{:S(2)}) collective-permute-start(bf16[512,512]{1,0:T(8,128)(2,1)S(1)} %collective-permute-done.1.refs_4_.refs_3_), channel_id=1, source_target_pairs={{0,1},{1,0},{2,3},{3,2},{4,5},{5,4},{6,7},{7,6},{8,9},{9,8},{10,11... | collective-permute-start | bytes 1572872 | tf_op jit(solution)/shard_map/ppermute | solution.py:26
  70.6 8.5 %collective-permute-start.5 = (bf16[512,512]{1,0:T(8,128)(2,1)S(1)}, bf16[512,512]{1,0:T(8,128)(2,1)}, u32[]{:S(2)}, u32[]{:S(2)}) collective-permute-start(bf16[512,512]{1,0:T(8,128)(2,1)S(1)} %collective-permute-done.refs_3_.refs_2_), channel_id=1, source_target_pairs={{0,1},{1,0},{2,3},{3,2},{4,5},{5,4},{6,7},{7,6},{8,9},{9,8},{10,11... | collective-permute-start | bytes 1572872 | tf_op jit(solution)/shard_map/ppermute | solution.py:26
  80.9 14.0 %collective-permute-start.11 = (bf16[512,512]{1,0:T(8,128)(2,1)S(1)}, bf16[512,512]{1,0:T(8,128)(2,1)S(1)}, u32[]{:S(2)}, u32[]{:S(2)}) collective-permute-start(bf16[512,512]{1,0:T(8,128)(2,1)S(1)} %compact_rows.3.refs_1_), channel_id=1, source_target_pairs={{0,4},{4,0},{1,5},{5,1},{2,6},{6,2},{3,7},{7,3},{8,12},{12,8},{9,1... | collective-permute-start | bytes 1572872 | tf_op jit(solution)/shard_map/ppermute | solution.py:24
  81.0 15.3 %collective-permute-start.9 = (bf16[512,512]{1,0:T(8,128)(2,1)S(1)}, bf16[512,512]{1,0:T(8,128)(2,1)S(1)}, u32[]{:S(2)}, u32[]{:S(2)}) collective-permute-start(bf16[512,512]{1,0:T(8,128)(2,1)S(1)} %compact_rows.3.refs_1_), channel_id=1, source_target_pairs={{0,2},{1,3},{2,0},{3,1},{4,6},{5,7},{6,4},{7,5},{8,10},{9,11},{10,... | collective-permute-start | bytes 1572872 | tf_op jit(solution)/shard_map/ppermute | solution.py:26
  95.0 7.6 %collective-permute-start.12 = (bf16[256,512]{1,0:T(8,128)(2,1)S(1)}, bf16[256,512]{1,0:T(8,128)(2,1)S(1)}, u32[]{:S(2)}, u32[]{:S(2)}) collective-permute-start(bf16[256,512]{1,0:T(8,128)(2,1)S(1)} %slice.55), channel_id=1, source_target_pairs={{0,2},{1,3},{2,0},{3,1},{4,6},{5,7},{6,4},{7,5},{8,10},{9,11},{10,... | collective-permute-start | bytes 786440 | tf_op jit(solution)/shard_map/ppermute | solution.py:26
  96.3 7.4 %collective-permute-start.10 = (bf16[256,512]{1,0:T(8,128)(2,1)S(1)}, bf16[256,512]{1,0:T(8,128)(2,1)}, u32[]{:S(2)}, u32[]{:S(2)}) collective-permute-start(bf16[256,512]{1,0:T(8,128)(2,1)S(1)} %slice.54), channel_id=1, source_target_pairs={{0,4},{4,0},{1,5},{5,1},{2,6},{6,2},{3,7},{7,3},{8,12},{12,8},{9,1... | collective-permute-start | bytes 786440 | tf_op jit(solution)/shard_map/ppermute | solution.py:24
  96.8 7.2 %collective-permute-start.15 = (bf16[512,512]{1,0:T(8,128)(2,1)S(1)}, bf16[512,512]{1,0:T(8,128)(2,1)S(1)}, u32[]{:S(2)}, u32[]{:S(2)}) collective-permute-start(bf16[512,512]{1,0:T(8,128)(2,1)S(1)} %compact_rows.3.refs_1_), channel_id=1, source_target_pairs={{0,1},{1,0},{2,3},{3,2},{4,5},{5,4},{6,7},{7,6},{8,9},{9,8},{10,11... | collective-permute-start | bytes 1572872 | tf_op jit(solution)/shard_map/ppermute | solution.py:26
  96.8 7.2 %collective-permute-start.16 = (bf16[512,512]{1,0:T(8,128)(2,1)S(1)}, bf16[512,512]{1,0:T(8,128)(2,1)S(1)}, u32[]{:S(2)}, u32[]{:S(2)}) collective-permute-start(bf16[512,512]{1,0:T(8,128)(2,1)S(1)} %collective-permute-done.11.refs_2_), channel_id=1, source_target_pairs={{0,1},{1,0},{2,3},{3,2},{4,5},{5,4},{6,7},{7,6},{8,9},{9,8},{10,11... | collective-permute-start | bytes 1572872 | tf_op jit(solution)/shard_map/ppermute | solution.py:26
  97.3 6.7 %collective-permute-start.17 = (bf16[512,512]{1,0:T(8,128)(2,1)S(1)}, bf16[512,512]{1,0:T(8,128)(2,1)S(1)}, u32[]{:S(2)}, u32[]{:S(2)}) collective-permute-start(bf16[512,512]{1,0:T(8,128)(2,1)S(1)} %collective-permute-done.9.refs_3_), channel_id=1, source_target_pairs={{0,1},{1,0},{2,3},{3,2},{4,5},{5,4},{6,7},{7,6},{8,9},{9,8},{10,11... | collective-permute-start | bytes 1572872 | tf_op jit(solution)/shard_map/ppermute | solution.py:26
  102.5 6.2 %collective-permute-start.14 = (bf16[256,512]{1,0:T(8,128)(2,1)S(1)}, bf16[256,512]{1,0:T(8,128)(2,1)}, u32[]{:S(2)}, u32[]{:S(2)}) collective-permute-start(bf16[256,512]{1,0:T(8,128)(2,1)S(1)} %collective-permute-done.12.refs_2_.refs_8_), channel_id=1, source_target_pairs={{0,1},{1,0},{2,3},{3,2},{4,5},{5,4},{6,7},{7,6},{8,9},{9,8},{10,11... | collective-permute-start | bytes 786440 | tf_op jit(solution)/shard_map/ppermute | solution.py:26
  120.3 8.3 %collective-permute-start.21 = (bf16[256,512]{1,0:T(8,128)(2,1)S(1)}, bf16[256,512]{1,0:T(8,128)(2,1)S(1)}, u32[]{:S(2)}, u32[]{:S(2)}) collective-permute-start(bf16[256,512]{1,0:T(8,128)(2,1)S(1)} %get-tuple-element.119), channel_id=1, source_target_pairs={{0,2},{1,3},{2,0},{3,1},{4,6},{5,7},{6,4},{7,5},{8,10},{9,11},{10,... | collective-permute-start | bytes 786440 | tf_op jit(solution)/shard_map/ppermute | solution.py:26
  121.0 8.0 %collective-permute-start.20 = (bf16[256,512]{1,0:T(8,128)(2,1)S(1)}, bf16[256,512]{1,0:T(8,128)(2,1)S(1)}, u32[]{:S(2)}, u32[]{:S(2)}) collective-permute-start(bf16[256,512]{1,0:T(8,128)(2,1)S(1)} %get-tuple-element.120), channel_id=1, source_target_pairs={{0,4},{4,0},{1,5},{5,1},{2,6},{6,2},{3,7},{7,3},{8,12},{12,8},{9,1... | collective-permute-start | bytes 786440 | tf_op jit(solution)/shard_map/ppermute | solution.py:24
  129.2 12.8 %collective-permute-start.23 = (bf16[512,512]{1,0:T(8,128)(2,1)S(1)}, bf16[512,512]{1,0:T(8,128)(2,1)S(1)}, u32[]{:S(2)}, u32[]{:S(2)}) collective-permute-start(bf16[512,512]{1,0:T(8,128)(2,1)S(1)} %add_convert_fusion.1), channel_id=1, source_target_pairs={{0,2},{1,3},{2,0},{3,1},{4,6},{5,7},{6,4},{7,5},{8,10},{9,11},{10,... | collective-permute-start | bytes 1572872 | tf_op jit(solution)/shard_map/ppermute | solution.py:26
  130.6 12.5 %collective-permute-start.24 = (bf16[512,512]{1,0:T(8,128)(2,1)S(1)}, bf16[512,512]{1,0:T(8,128)(2,1)S(1)}, u32[]{:S(2)}, u32[]{:S(2)}) collective-permute-start(bf16[512,512]{1,0:T(8,128)(2,1)S(1)} %add_convert_fusion), channel_id=1, source_target_pairs={{0,4},{4,0},{1,5},{5,1},{2,6},{6,2},{3,7},{7,3},{8,12},{12,8},{9,1... | collective-permute-start | bytes 1572872 | tf_op jit(solution)/shard_map/ppermute | solution.py:24
  131.0 9.5 %collective-permute-start.25 = (f32[4,4096]{1,0:T(4,128)S(1)}, f32[4,4096]{1,0:T(4,128)S(1)}, u32[]{:S(2)}, u32[]{:S(2)}) collective-permute-start(f32[4,4096]{1,0:T(4,128)S(1)} %fusion), channel_id=1, source_target_pairs={{0,16},{8,24},{16,0},{24,8},{1,17},{9,25},{17,1},{25,9},{2,18},{10... | collective-permute-start | bytes 196616 | tf_op jit(solution)/shard_map/ppermute | solution.py:461
  145.4 28.2 %all-to-all-start.2 = ((bf16[8,128,512]{2,1,0:T(8,128)(2,1)}), bf16[8,128,512]{2,1,0:T(8,128)(2,1)S(1)}, u32[]{:S(2)}, u32[]{:S(2)}) async-start(bf16[8,128,512]{2,1,0:T(8,128)(2,1)} %place_rows.1), calls=%async_computation.2 | async-start | bytes 2097152 | tf_op jit(solution)/shard_map/all_to_all | solution.py:418
  164.0 5.8 %collective-permute-start.28 = (f32[4,4096]{1,0:T(4,128)S(1)}, f32[4,4096]{1,0:T(4,128)S(1)}, u32[]{:S(2)}, u32[]{:S(2)}) collective-permute-start(f32[4,4096]{1,0:T(4,128)S(1)} %add.80), channel_id=1, source_target_pairs={{0,4},{4,0},{1,5},{5,1},{2,6},{6,2},{3,7},{7,3},{8,12},{12,8},{9,1... | collective-permute-start | bytes 196616 | tf_op jit(solution)/shard_map/ppermute | solution.py:24
  (37 other events, 196.9 us)

commit v3 on v2

--- a/solution.py
+++ b/solution.py
@@ -47,9 +47,12 @@
             if before:
                 first, second = after(first, *before), after(second, *before)
             blocks[m] = [(0, flip(first, low)), (half, flip(second, high))]
-    for m in chip_masks(slots):
+    return blocks
+
+
+def add_core(blocks, masks):
+    for m in masks:
         blocks[m | CORE] = [(at, flip(x, CORE)) for at, x in blocks[m]]
-    return blocks
 
 
 def rows_of(pieces, start, count):
@@ -116,51 +119,36 @@
     return pl.ds(pl.multiple_of(start * size, size), size)
 
 
-def stage(*arrays):
-    def kernel(*refs):
-        sources, results, ready = refs[: len(arrays)], refs[len(arrays) : -1], refs[-1]
-        copies = [
-            pltpu.make_async_copy(x, y, ready.at[i]) for i, (x, y) in enumerate(zip(sources, results))
-        ]
-        for copy in copies:
-            copy.start()
-        for copy in copies:
-            copy.wait()
-
-    return pl.pallas_call(
-        kernel,
-        in_specs=[pl.BlockSpec(memory_space=pltpu.HBM)] * len(arrays),
-        out_specs=[pl.BlockSpec(memory_space=pltpu.VMEM)] * len(arrays),
-        out_shape=[pltpu.VMEM(x.shape, x.dtype) for x in arrays],
-        scratch_shapes=[pltpu.SemaphoreType.DMA((len(arrays),))],
-        compiler_params=pltpu.CompilerParams(vmem_limit_bytes=VMEM_LIMIT),
-        cost_estimate=pl.CostEstimate(
-            flops=0, bytes_accessed=sum(2 * x.size * x.dtype.itemsize for x in arrays), transcendentals=0
-        ),
-        name="stage_weights",
-    )(*arrays)
-
-
-def pack(firsts, chosen_cols, source, bucket):
-    experts = chosen_cols.shape[1]
-    rows, features = source.shape
-    width = features // 2
-
-    def kernel(firsts_ref, chosen_ref, source_ref, out, hot_out):
+def pack(firsts, chosen, sources, bucket, halves):
+    experts, cap = chosen.shape
+    rows, width = sources[0].shape
+
+    def kernel(firsts_ref, chosen_ref, *refs):
+        ins, (out, hot_out) = refs[: len(sources)], refs[len(sources) :]
         for e in range(experts):
-            picked = chosen_ref[pl.ds(firsts_ref[e + 1], bucket), :][:, e : e + 1] - firsts_ref[0]
-            hot = lax.broadcasted_iota(jnp.int32, (bucket, rows), 1) == picked
-            hot = hot.astype(F32).astype(BF)
-            hot_out[e] = hot
-            got = dot(hot, source_ref[...], 1, 0).astype(BF)
-            out[2 * e], out[2 * e + 1] = got[:, :width], got[:, width:]
-
-    flops = 2 * experts * bucket * rows * features
+            line = chosen_ref[e : e + 1, :]
+            start = jnp.sum((line < firsts_ref[0]).astype(jnp.int32))
+            line = pltpu.roll(jnp.broadcast_to(line, (8, cap)), cap - start, 1)[:1, :bucket]
+            got = None
+            for i, x in enumerate(ins):
+                hot = lax.broadcasted_iota(jnp.int32, (rows, bucket), 0) == line - firsts_ref[i + 1]
+                hot = hot.astype(F32).astype(BF)
+                hot_out[e] = hot
+                term = dot(hot, x[...], 0, 0)
+                got = term if got is None else got + term
+            got = got.astype(BF)
+            if halves:
+                out[2 * e], out[2 * e + 1] = got[:, : width // 2], got[:, width // 2 :]
+            else:
+                out[e] = got
+
+    flops = 2 * experts * bucket * rows * width * len(sources)
+    cut = 2 if halves else 1
     outs = [
-        shaped(2 * experts, bucket, width, dtype=BF),
-        shaped(experts, bucket, rows, dtype=BF),
+        shaped(experts * cut, bucket, width // cut, dtype=BF),
+        pltpu.HBM((experts, rows, bucket), BF),
     ]
-    return call(kernel, "pack_rows", flops, outs, [firsts], chosen_cols, source)
+    return call(kernel, "pack_rows", flops, outs, [firsts], chosen, *sources)
 
 
 def compact(reach, buckets, cap):
@@ -199,14 +187,14 @@
 
 
 def combine(hots, returned):
-    experts, bucket, rows = hots.shape
+    experts, rows, bucket = hots.shape
     width = returned.shape[2]
 
     def kernel(hots_ref, returned_ref, out):
         for h in range(2):
             acc = None
             for e in range(experts):
-                term = dot(hots_ref[e], returned_ref[2 * e + h], 0, 0)
+                term = dot(hots_ref[e], returned_ref[2 * e + h], 1, 0)
                 acc = term if acc is None else acc + term
             out[:, h * width : (h + 1) * width] = acc.astype(BF)
 
@@ -247,13 +235,13 @@
     spots, xs = flat(blocks, keys)
     cap, width = blocks[0][0][1].shape
     hidden = w_in.shape[1]
-    experts = router.shape[1]
+    experts = router.shape[0]
 
     def kernel(order_ref, expert_ref, *refs):
         ins, (tiles, r_ref, a_ref, gate_ref) = refs[: len(xs)], refs[len(xs) :]
         scores = None
         for (j, at, rows), x in zip(spots, ins):
-            s = dot(x[...], r_ref[block_at(order_ref[j], width), :], 1, 0)
+            s = dot(x[...], r_ref[:, block_at(order_ref[j], width)], 1, 1)
             scores = [(at, s)] if scores is None else add_rows(scores, at, rows, s)
             a = dot(x[...], tiles[j][...], 1, 0)
             if j == 0:
@@ -277,20 +265,19 @@
     hidden = w_out.shape[0]
 
     def kernel(order_ref, *refs):
-        ins, (tiles, up) = refs[: len(ys)], refs[len(ys) :]
+        ins, (w_ref, up) = refs[: len(ys)], refs[len(ys) :]
         for (j, at, rows), y in zip(spots, ins):
-            u = dot(y[...], tiles[j][...], 1, 1)
+            u = dot(y[...], w_ref[:, block_at(order_ref[j], width)], 1, 1)
             if j == 0:
                 up[at : at + rows, :] = u
             else:
                 up[at : at + rows, :] += u
 
     flops = 2 * cap * width * len(keys) * hidden
-    tiles = Tiles(w_out, 1, len(keys))
-    return call(kernel, "project_out", flops, [shaped(cap, hidden)], [order], *ys, tiles)[0]
-
-
-def activation(order, blocks, keys, far, near, w_out, w_in, router_row, upstream, pre_act, gate):
+    return call(kernel, "project_out", flops, [shaped(cap, hidden)], [order], *ys, [w_out])[0]
+
+
+def activation(order, blocks, keys, far, near, tiles, w_in, router_row, upstream, pre_act, gate):
     spots, ys = flat(blocks, keys)
     width = blocks[0][0][1].shape[1]
     cap, hidden = pre_act.shape
@@ -298,10 +285,11 @@
 
     def kernel(order_ref, *refs):
         ins, refs = refs[: len(ys)], refs[len(ys) :]
-        tiles, back, r_ref, u_ref, a_ref, gate_ref, hg_ref, da_ref, ds_ref, *outs = refs
+        late, refs = refs[: len(tiles)], refs[len(tiles) :]
+        back, r_ref, u_ref, a_ref, gate_ref, hg_ref, da_ref, ds_ref, *outs = refs
         up = [(0, u_ref[...])]
         for (j, at, rows), y in zip(spots, ins):
-            up = add_rows(up, at, rows, dot(y[...], tiles[j][...], 1, 1))
+            up = add_rows(up, at, rows, dot(y[...], late[j][...], 1, 1))
         for at, u in up:
             place = slice(at, at + u.shape[0])
             a = a_ref[place, :]
@@ -314,16 +302,15 @@
             da_ref[place, :] = (gate * u * sig * (1.0 + a * (1.0 - sig))).astype(BF)
         places = [(out, k) for out, n in zip(outs, far + near) for k in range(n)]
         for k, (out, spot) in enumerate(places):
-            here = block_at(order_ref[len(keys) + k], width)
+            here = block_at(order_ref[k], width)
             block = dot(da_ref[...], back[k][...], 1, 1) + ds_ref[...] * r_ref[:, here]
             out[spot] = block.astype(out.dtype)
 
     flops = 2 * cap * width * (len(keys) + count) * hidden
     outs = [shaped(cap, hidden, dtype=BF), shaped(cap, hidden, dtype=BF), shaped(cap, 1)]
     outs += [shaped(n, cap, width, dtype=BF) for n in far] + [shaped(n, cap, width) for n in near]
-    tiles, back = Tiles(w_out, 1, len(keys)), Tiles(w_in, 0, count, len(keys))
-    more = (tiles, back, router_row, upstream, pre_act, gate)
-    return call(kernel, "activation", flops, outs, [order], *ys, *more)
+    more = (Tiles(w_in, 0, count), router_row, upstream, pre_act, gate)
+    return call(kernel, "activation", flops, outs, [order], *ys, *tiles, *more)
 
 
 def router_column(order, blocks, keys, score_grad):
@@ -382,7 +369,7 @@
 
     flops = 2 * cap * width * len(keys) * hidden
     outs = [shaped(hidden, width * len(keys), dtype=BF)]
-    return call(kernel, "grads_out", flops, outs, [order], *ys, gated)[0]
+    return call(kernel, "grads_out", flops, outs, [order], *[[y] for y in ys], gated)[0]
 
 
 def numbers(values):
@@ -403,54 +390,63 @@
     expert = plane.astype(jnp.int32)[None]
     router_row = lax.dynamic_slice_in_dim(router.T, plane, 1, 0).astype(F32)
     masks = chip_masks(slots)
-    first = ((plane * 2 + half) * tok_dev).astype(jnp.int32)
-    before_me = jnp.sum((chosen < first).astype(jnp.int32), axis=1)
-    firsts = jnp.concatenate([first[None], before_me])
-    chosen_cols = jnp.pad(chosen.T, ((0, bucket), (0, 0)), constant_values=-1)
+    firsts = numbers([(plane * 2 + half) * tok_dev] * 2)
+    plane_firsts = numbers([(plane * 2 + part) * tok_dev for part in (0, half, 1 - half)])
     mine = lax.dynamic_slice_in_dim(chosen, plane, 1, 0)
     edges = jnp.arange(homes, dtype=jnp.int32)[:, None] * tok_dev
     reach = jnp.sum((mine < edges).astype(jnp.int32), axis=1)
 
-    def tensor_slice(source):
-        return lax.dynamic_slice_in_dim(source, (slot // 2) * 2 * width, 2 * width, 1)
-
-    def exchange(x):
-        return lax.all_to_all(x, ("plane", "half"), split_axis=0, concat_axis=0, tiled=True)
+    def columns(source, start, count):
+        return lax.dynamic_slice_in_dim(source, start * width, count * width, 1)
+
+    def exchange(x, axes):
+        return lax.all_to_all(x, axes, split_axis=0, concat_axis=0, tiled=True)
 
     def order_of(*keys):
         return numbers([slot ^ m for m in keys])
 
-    x_sent, hots = pack(firsts, chosen_cols, tensor_slice(tokens), bucket)
-    x_got = exchange(x_sent)
-    w_in, w_out, _ = join(w_in, w_out, x_sent)
-    w_in, w_out = stage(w_in, w_out)
-    y_sent, _ = pack(firsts, chosen_cols, tensor_slice(cotangent), bucket)
-    x_got, y_sent, w_in, w_out = join(x_got, y_sent, w_in, w_out)
-    y_got = exchange(y_sent)
+    late = [m for m in masks if m.bit_count() > 1]
+    early = [m for m in masks if m not in late]
+    late_keys = late + [m | CORE for m in late]
+    early_keys = early + [m | CORE for m in early]
+    keys = early_keys + late_keys
+    order = order_of(*keys)
+
+    x_sent, hots = pack(firsts, chosen, [columns(tokens, slot // 2 * 2, 2)], bucket, True)
+    x_got = exchange(x_sent, ("plane", "half"))
+    cotangent, w_out, _ = join(cotangent, w_out, x_sent)
+    y_own, y_away = columns(cotangent, slot, 1), flip(columns(cotangent, slot ^ 1, 1), 1)
+    y_sent, _ = pack(plane_firsts, chosen, [y_own, y_away], 2 * bucket, False)
+    tiles = [columns(w_out, slot ^ m, 1) for m in late_keys]
+    x_got, y_sent, *tiles = join(x_got, y_sent, *tiles)
+
+    y_got = exchange(y_sent, "plane")
     xs = plane_gather(compact(reach, x_got, cap), slots)
+    add_core(xs, masks)
     pieces = [x for m in xs for _, x in xs[m]]
     y_got, *pieces = join(y_got, *pieces)
     xs = {m: [(at, pieces.pop(0)) for at, _ in xs[m]] for m in xs}
-    late = [m for m in masks if m.bit_count() > 1]
-    late += [m | CORE for m in late]
-    early = [m for m in xs if m not in late]
-    keys = early + late
-    order = order_of(*keys)
-    pre_act, gate = project_in(order, expert, xs, keys, w_in, router)
-    ys = plane_gather(compact(reach, y_got, cap), slots, pre_act)
-    upstream = project_out(order_of(*early), ys, early, w_out)
-
-    groups = [[m for m in masks if m.bit_count() > 1], [m for m in masks if m.bit_count() <= 1]]
-    groups = [g[::-1] for g in groups]
+
+    pre_act, gate = project_in(order, expert, xs, keys, w_in, router.T)
+    ys = plane_gather(compact(reach[::2], y_got, cap), slots, pre_act)
+    tied = {m: [(at, after(x, pre_act)) for at, x in ys[m]] for m in early}
+    add_core(tied, early)
+    ys.update({m: tied[m] for m in tied if m & CORE})
+    upstream = project_out(order_of(*early_keys), ys, early_keys, w_out)
+    for m in late:
+        ys[m] = [(at, after(x, upstream)) for at, x in ys[m]]
+    add_core(ys, late)
+
+    groups = [late[::-1], early[::-1]]
     sizes = [len(g) for g in groups]
     near = [m for g in groups for m in g]
     gated, pre_grad, score_grad, far1, far2, near1, near2 = activation(
-        order_of(*late, *[m | CORE for m in near], *near),
+        order_of(*[m | CORE for m in near], *near),
         ys,
-        late,
+        late_keys,
         sizes,
         sizes,
-        w_out,
+        tiles,
         w_in,
         router_row,
         upstream,
@@ -490,7 +486,7 @@
     *terms, grad_in, total = join(sums[0], *came, grad_in, total)
 
     back = place(reach, homes, bucket, terms)
-    returned = exchange(back)
+    returned = exchange(back, ("plane", "half"))
     grad_out = grads_out(order, ys, keys, after(gated, back))
     total = after(total, grad_out)
     while hops:

time: 177 us -> 169 us (0.955)
  waiting for transfers between devices: 69.7 us -> 60.8 us
  local copies, waits for them, and re-layouts: 24.5 us -> 18.1 us
  starting transfers between devices: 38.3 us -> 42.4 us
  Pallas kernels: 39.6 us -> 43.3 us
    unnamed x60 -> x56, local copies, waits for them, and re-layouts: 22.1 us -> 10.3 us
    all_to_all x3, waiting for transfers between devices: 17.9 us -> 7.93 us  [exchange(): return lax.all_to_all(x, axes, split_axis=0, concat_axis=0, tiled=True)]
    pallas_call x12, Pallas kernels: 39.1 us -> 43.3 us  [call(): pl.pallas_call(run, in_specs=[pl.BlockSpec(memory_space=pltpu.SMEM)] * le...]
    ppermute x7 -> x8, starting transfers between devices: 7.74 us -> 11.7 us  [flip(): return lax.ppermute(x, 'half', [(0, 1), (1, 0)])]
    slice x4, local copies, waits for them, and re-layouts: 0.07 us -> 3.37 us  [rows_of(): return x[start - at:start - at + count]]
    dynamic_slice x1 -> x3, local copies, waits for them, and re-layouts: 1.27 us -> 4.05 us  [columns(): return lax.dynamic_slice_in_dim(source, start * width, count * width, 1)]
    ppermute x7 -> x8, waiting for transfers between devices: 20 us -> 20.8 us  [flip(): return lax.ppermute(x, 'half', [(0, 1), (1, 0)])]
  transfers between devices with their start and end apart: 32 -> 33, of which waited for: 19 -> 20; matrix products, arithmetic and copies ran while one was open for 2% -> 6% of each run, Pallas kernels for 16% -> 19%
where the time goes in v3:
time: 169 us; the launch traced here: 168 us
  waiting for transfers between devices  60.8 us (36%)
  Pallas kernels  43.3 us (26%)
  starting transfers between devices  42.4 us (25%)
  local copies, waits for them, and re-layouts  18.1 us (11%)
  other arithmetic  2.24 us (1%)
    pallas_call x12, Pallas kernels, call(): pl.pallas_call(run, in_specs=[pl.BlockSpec(memory_space=pltpu.SMEM)] * le...  43.3 us
    ppermute x20, waiting for transfers between devices, flip(): return lax.ppermute(x, 'tensor', [(i, i ^ bit >> 1) for i in range(n)])  32.1 us
    ppermute x8, waiting for transfers between devices, flip(): return lax.ppermute(x, 'half', [(0, 1), (1, 0)])  20.8 us
    all_to_all x3, starting transfers between devices, exchange(): return lax.all_to_all(x, axes, split_axis=0, concat_axis=0, tiled=True)  16.4 us
    ppermute x8, starting transfers between devices, flip(): return lax.ppermute(x, 'half', [(0, 1), (1, 0)])  11.7 us
    unnamed x56, local copies, waits for them, and re-layouts  10.3 us
    ppermute x20, starting transfers between devices, flip(): return lax.ppermute(x, 'tensor', [(i, i ^ bit >> 1) for i in range(n)])  10.1 us
    all_to_all x3, waiting for transfers between devices, exchange(): return lax.all_to_all(x, axes, split_axis=0, concat_axis=0, tiled=True)  7.93 us
  transfers between devices with their start and end apart: 33, of which 20 were waited for; matrix products, arithmetic and copies ran while one was open for 6% of the time, Pallas kernels for 19%

profile of v3, /device:TPU:0, one launch (start us, length us, event | category | flops | bytes accessed | tf_op | source)
XLA Modules:
  0.0 167.9 jit_solution(15053043508063310077)
XLA Ops:
  5.8 7.3 %all-to-all-start = ((bf16[8,128,512]{2,1,0:T(8,128)(2,1)}), bf16[8,128,512]{2,1,0:T(8,128)(2,1)S(1)}, u32[]{:S(2)}, u32[]{:S(2)}) async-start(bf16[8,128,512]{2,1,0:T(8,128)(2,1)} %copy-done.10), calls=%async_computation | async-start | bytes 2097152 | tf_op jit(solution)/shard_map/all_to_all | solution.py:403
  16.9 2.2 %constant_dynamic-slice_fusion = (bf16[512,512]{1,0:T(8,128)(2,1)}, bf16[512,512]{1,0:T(8,128)(2,1)}) fusion(bf16[512,4096]{1,0:T(8,128)(2,1)} %refs_7_.1, s32[]{:T(128)S(6)} %select_n.34, s32[]{:T(128)S(6)} %select_n.33), kind=kLoop, calls=%fused_computation.11 | loop fusion | bytes 2097160 | tf_op jit(solution)/shard_map/dynamic_slice | solution.py:400
  19.2 11.9 %collective-permute-done.refs_3_ = bf16[256,512]{1,0:T(8,128)(2,1)} collective-permute-done((bf16[256,512]{1,0:T(8,128)(2,1)}, bf16[256,512]{1,0:T(8,128)(2,1)}, u32[]{:S(2)}, u32[]{:S(2)}) %collective-permute-start) | collective-permute-done | bytes 262176 | tf_op jit(solution)/shard_map/ppermute | solution.py:24
  31.0 2.7 %pack_rows.3 = (bf16[4,256,512]{2,1,0:T(8,128)(2,1)S(1)}, bf16[4,256,256]{2,1,0:T(8,128)(2,1)}) custom-call(s32[3]{0:T(128)S(1)} %pad_add_fusion.1.refs_0_, s32[4,512]{1,0:T(4,128)S(1)} %copy-done.21, bf16[256,512]{1,0:T(8,128)(2,1)S(1)} %get-tuple-element.128.refs_2_, bf16[256,512]{1,0:T(8,128)(2,1)} %collective-permute-done.refs_3_), custom_call_target="tpu_custom_call" | custom-call | flops 536870912 | bytes 3678220 | tf_op jit(solution)/shard_map/pack_rows/pallas_call | solution.py:102
  34.8 4.1 %all-to-all-done.refs_1_ = bf16[8,128,512]{2,1,0:T(8,128)(2,1)S(1)} async-done(((bf16[8,128,512]{2,1,0:T(8,128)(2,1)}), bf16[8,128,512]{2,1,0:T(8,128)(2,1)S(1)}, u32[]{:S(2)}, u32[]{:S(2)}) %all-to-all-start) | async-done | bytes 1048608 | tf_op jit(solution)/shard_map/all_to_all | solution.py:403
  38.9 4.4 %all-to-all-start.1 = ((bf16[4,256,512]{2,1,0:T(8,128)(2,1)}), bf16[4,256,512]{2,1,0:T(8,128)(2,1)}, u32[]{:S(2)}, u32[]{:S(2)}) async-start(bf16[4,256,512]{2,1,0:T(8,128)(2,1)} %copy-done.9), calls=%async_computation.1 | async-start | bytes 2097152 | tf_op jit(solution)/shard_map/all_to_all | solution.py:403
  49.5 9.3 %collective-permute-done.2.refs_4_.refs_3_ = bf16[512,512]{1,0:T(8,128)(2,1)S(1)} collective-permute-done((bf16[512,512]{1,0:T(8,128)(2,1)S(1)}, bf16[512,512]{1,0:T(8,128)(2,1)S(1)}, u32[]{:S(2)}, u32[]{:S(2)}) %collective-permute-start.2) | collective-permute-done | bytes 524320 | tf_op jit(solution)/shard_map/ppermute | solution.py:26
  58.8 2.1 %collective-permute-start.3 = (bf16[256,512]{1,0:T(8,128)(2,1)S(1)}, bf16[256,512]{1,0:T(8,128)(2,1)S(1)}, u32[]{:S(2)}, u32[]{:S(2)}) collective-permute-start(bf16[256,512]{1,0:T(8,128)(2,1)S(1)} %slice.56), channel_id=1, source_target_pairs={{0,4},{4,0},{1,5},{5,1},{2,6},{6,2},{3,7},{7,3},{8,12},{12,8},{9,1... | collective-permute-start | bytes 786440 | tf_op jit(solution)/shard_map/ppermute | solution.py:24
  66.0 2.5 %collective-permute-done.4.refs_9_.refs_8_ = bf16[256,512]{1,0:T(8,128)(2,1)} collective-permute-done((bf16[256,512]{1,0:T(8,128)(2,1)S(1)}, bf16[256,512]{1,0:T(8,128)(2,1)}, u32[]{:S(2)}, u32[]{:S(2)}) %collective-permute-start.4) | collective-permute-done | bytes 262176 | tf_op jit(solution)/shard_map/ppermute | solution.py:26
  70.4 2.7 %compact_rows.3.refs_1_ = bf16[512,512]{1,0:T(8,128)(2,1)} custom-call(s32[4]{0:T(128)S(1)} %slice.43.refs_0_, bf16[4,256,512]{2,1,0:T(8,128)(2,1)} %all-to-all-done.1.refs_1_), custom_call_target="tpu_custom_call" | custom-call | flops 536870912 | bytes 2097168 | tf_op jit(solution)/shard_map/compact_rows/pallas_call | solution.py:102
  75.0 2.2 %copy-done.2 = bf16[4096,512]{1,0:T(8,128)(2,1)S(1)} copy-done((bf16[4096,512]{1,0:T(8,128)(2,1)S(1)}, bf16[4096,512]{1,0:T(8,128)(2,1)}, u32[]{:S(2)}) %copy-start.2) | copy-done | bytes 4194328
  77.2 5.5 %project_in.1 = (f32[512,512]{1,0:T(8,128)S(1)}, f32[512,1]{1,0:T(8,128)S(1)}) custom-call(s32[8]{0:T(128)S(1)} %stack.78.refs_0_, s32[1]{0:T(128)} %bitcast.12.refs_1_, bf16[512,512]{1,0:T(8,128)(2,1)} %copy-done.1, bf16[512,512]{1,0:T(8,128)(2,1)} %collective-permute-done.1.refs_3_.refs_2_, bf16[512,512]{1,0:T(8,128)(2,1)} %copy-done.26, ...), custom_call_target="tpu_custom_call" | custom-call | flops 2147483648 | bytes 9472036 | tf_op jit(solution)/shard_map/project_in/pallas_call | solution.py:102
  83.4 3.9 %collective-permute-done.10.refs_3_ = bf16[512,512]{1,0:T(8,128)(2,1)S(1)} collective-permute-done((bf16[512,512]{1,0:T(8,128)(2,1)}, bf16[512,512]{1,0:T(8,128)(2,1)S(1)}, u32[]{:S(2)}, u32[]{:S(2)}) %collective-permute-start.10) | collective-permute-done | bytes 524320 | tf_op jit(solution)/shard_map/ppermute | solution.py:26
  93.8 4.9 %project_out.1.refs_9_ = f32[512,512]{1,0:T(8,128)S(1)} custom-call(s32[6]{0:T(128)S(1)} %stack.79.refs_0_, bf16[512,512]{1,0:T(8,128)(2,1)} %compact_rows.3.refs_1_, bf16[512,512]{1,0:T(8,128)(2,1)} %collective-permute-done.12.refs_2_, bf16[512,512]{1,0:T(8,128)(2,1)S(1)} %collective-permute-done.10.refs_3_, ...), custom_call_target="tpu_custom_call" | custom-call | flops 1610612736 | bytes 8388632 | tf_op jit(solution)/shard_map/project_out/pallas_call | solution.py:102
  102.4 4.4 %activation.1 = (bf16[512,512]{1,0:T(8,128)(2,1)S(1)}, bf16[512,512]{1,0:T(8,128)(2,1)S(1)}, f32[512,1]{1,0:T(8,128)S(1)}, bf16[1,512,512]{2,1,0:T(8,128)(2,1)S(...) custom-call(s32[8]{0:T(128)S(1)} %stack.74.refs_0_, ...), custom_call_target="tpu_custom_call" | custom-call | flops 2684354560 | bytes 18894880 | tf_op jit(solution)/shard_map/activation/pallas_call | solution.py:102
  107.5 3.1 %router_column.1 = f32[1,4096]{1,0:T(1,128)S(1)} custom-call(s32[8]{0:T(128)S(1)} %stack.78.refs_0_, bf16[512,512]{1,0:T(8,128)(2,1)} %copy-done.1, bf16[512,512]{1,0:T(8,128)(2,1)} %collective-permute-done.1.refs_3_.refs_2_, bf16[512,512]{1,0:T(8,128)(2,1)} %copy-done.26, bf16[512,512]{1,0:T(8,128)(2,1)} %collective-permute-done.5.refs_5_.refs_4_, ...), custom_call_target="tpu_custom_call" | custom-call | flops 4194304 | bytes 4212768 | tf_op jit(solution)/shard_map/router_column/pallas_call | solution.py:102
  116.0 5.4 %collective-permute-done.22 = bf16[256,512]{1,0:T(8,128)(2,1)S(1)} collective-permute-done((bf16[256,512]{1,0:T(8,128)(2,1)S(1)}, bf16[256,512]{1,0:T(8,128)(2,1)S(1)}, u32[]{:S(2)}, u32[]{:S(2)}) %collective-permute-start.22) | collective-permute-done | bytes 262176 | tf_op jit(solution)/shard_map/ppermute | solution.py:26
  125.1 2.4 %collective-permute-start.26 = (f32[4,4096]{1,0:T(4,128)S(1)}, f32[4,4096]{1,0:T(4,128)S(1)}, u32[]{:S(2)}, u32[]{:S(2)}) collective-permute-start(f32[4,4096]{1,0:T(4,128)S(1)} %fusion), channel_id=1, source_target_pairs={{0,16},{8,24},{16,0},{24,8},{1,17},{9,25},{17,1},{25,9},{2,18},{10... | collective-permute-start | bytes 196616 | tf_op jit(solution)/shard_map/ppermute | solution.py:457
  127.5 6.8 %grads_in.1 = bf16[4096,512]{1,0:T(8,128)(2,1)} custom-call(s32[8]{0:T(128)S(1)} %stack.78.refs_0_, bf16[512,512]{1,0:T(8,128)(2,1)} %copy-done.1, bf16[512,512]{1,0:T(8,128)(2,1)} %collective-permute-done.1.refs_3_.refs_2_, bf16[512,512]{1,0:T(8,128)(2,1)} %copy-done.26, bf16[512,512]{1,0:T(8,128)(2,1)} %collective-permute-done.5.refs_5_.refs_4_, ...), custom_call_target="tpu_custom_call" | custom-call | flops 2147483648 | bytes 13107232 | tf_op jit(solution)/shard_map/grads_in/pallas_call | solution.py:102
  138.0 4.8 %all-to-all-start.2 = ((bf16[8,128,512]{2,1,0:T(8,128)(2,1)}), bf16[8,128,512]{2,1,0:T(8,128)(2,1)S(1)}, u32[]{:S(2)}, u32[]{:S(2)}) async-start(bf16[8,128,512]{2,1,0:T(8,128)(2,1)} %copy-done.4), calls=%async_computation.2 | async-start | bytes 2097152 | tf_op jit(solution)/shard_map/all_to_all | solution.py:403
  143.8 6.6 %grads_out.1 = bf16[512,4096]{1,0:T(8,128)(2,1)} custom-call(s32[8]{0:T(128)S(1)} %stack.78.refs_0_, bf16[512,512]{1,0:T(8,128)(2,1)} %compact_rows.3.refs_1_, bf16[512,512]{1,0:T(8,128)(2,1)} %collective-permute-done.12.refs_2_, bf16[512,512]{1,0:T(8,128)(2,1)} %copy-done.5, bf16[512,512]{1,0:T(8,128)(2,1)} %copy-done.6, ...), custom_call_target="tpu_custom_call" | custom-call | flops 2147483648 | bytes 13107232 | tf_op jit(solution)/shard_map/grads_out/pallas_call | solution.py:102
  151.0 3.7 %collective-permute-done.27 = f32[4,4096]{1,0:T(4,128)S(1)} collective-permute-done((f32[4,4096]{1,0:T(4,128)S(1)}, f32[4,4096]{1,0:T(4,128)S(1)}, u32[]{:S(2)}, u32[]{:S(2)}) %collective-permute-start.27) | collective-permute-done | bytes 65568 | tf_op jit(solution)/shard_map/ppermute | solution.py:26
  158.1 3.8 %collective-permute-done.29 = f32[4,4096]{1,0:T(4,128)S(1)} collective-permute-done((f32[4,4096]{1,0:T(4,128)S(1)}, f32[4,4096]{1,0:T(4,128)S(1)}, u32[]{:S(2)}, u32[]{:S(2)}) %collective-permute-start.29) | collective-permute-done | bytes 65568 | tf_op jit(solution)/shard_map/ppermute | solution.py:24
  162.5 3.8 %all-to-all-done.2.refs_1_ = bf16[8,128,512]{2,1,0:T(8,128)(2,1)S(1)} async-done(((bf16[8,128,512]{2,1,0:T(8,128)(2,1)}), bf16[8,128,512]{2,1,0:T(8,128)(2,1)S(1)}, u32[]{:S(2)}, u32[]{:S(2)}) %all-to-all-start.2) | async-done | bytes 1048608 | tf_op jit(solution)/shard_map/all_to_all | solution.py:403
  (138 shorter events, 56.4 us)
Async XLA Ops:
  5.8 33.0 %all-to-all-start = ((bf16[8,128,512]{2,1,0:T(8,128)(2,1)}), bf16[8,128,512]{2,1,0:T(8,128)(2,1)S(1)}, u32[]{:S(2)}, u32[]{:S(2)}) async-start(bf16[8,128,512]{2,1,0:T(8,128)(2,1)} %copy-done.10), calls=%async_computation | async-start | bytes 2097152 | tf_op jit(solution)/shard_map/all_to_all | solution.py:403
  14.8 16.2 %collective-permute-start = (bf16[256,512]{1,0:T(8,128)(2,1)}, bf16[256,512]{1,0:T(8,128)(2,1)}, u32[]{:S(2)}, u32[]{:S(2)}) collective-permute-start(bf16[256,512]{1,0:T(8,128)(2,1)} %get-tuple-element.127), channel_id=1, source_target_pairs={{0,4},{4,0},{1,5},{5,1},{2,6},{6,2},{3,7},{7,3},{8,12},{12,8},{9,1... | collective-permute-start | bytes 786440 | tf_op jit(solution)/shard_map/ppermute | solution.py:24
  38.9 31.5 %all-to-all-start.1 = ((bf16[4,256,512]{2,1,0:T(8,128)(2,1)}), bf16[4,256,512]{2,1,0:T(8,128)(2,1)}, u32[]{:S(2)}, u32[]{:S(2)}) async-start(bf16[4,256,512]{2,1,0:T(8,128)(2,1)} %copy-done.9), calls=%async_computation.1 | async-start | bytes 2097152 | tf_op jit(solution)/shard_map/all_to_all | solution.py:403
  46.5 12.3 %collective-permute-start.2 = (bf16[512,512]{1,0:T(8,128)(2,1)S(1)}, bf16[512,512]{1,0:T(8,128)(2,1)S(1)}, u32[]{:S(2)}, u32[]{:S(2)}) collective-permute-start(bf16[512,512]{1,0:T(8,128)(2,1)S(1)} %compact_rows.2.refs_2_.refs_1_), channel_id=1, source_target_pairs={{0,2},{1,3},{2,0},{3,1},{4,6},{5,7},{6,4},{7,5},{8,10},{9,11},{10,... | collective-permute-start | bytes 1572872 | tf_op jit(solution)/shard_map/ppermute | solution.py:26
  48.1 12.9 %collective-permute-start.1 = (bf16[512,512]{1,0:T(8,128)(2,1)S(1)}, bf16[512,512]{1,0:T(8,128)(2,1)}, u32[]{:S(2)}, u32[]{:S(2)}) collective-permute-start(bf16[512,512]{1,0:T(8,128)(2,1)S(1)} %compact_rows.2.refs_2_.refs_1_), channel_id=1, source_target_pairs={{0,4},{4,0},{1,5},{5,1},{2,6},{6,2},{3,7},{7,3},{8,12},{12,8},{9,1... | collective-permute-start | bytes 1572872 | tf_op jit(solution)/shard_map/ppermute | solution.py:24
  49.5 19.1 %collective-permute-start.5 = (bf16[512,512]{1,0:T(8,128)(2,1)S(1)}, bf16[512,512]{1,0:T(8,128)(2,1)}, u32[]{:S(2)}, u32[]{:S(2)}) collective-permute-start(bf16[512,512]{1,0:T(8,128)(2,1)S(1)} %compact_rows.2.refs_2_.refs_1_), channel_id=1, source_target_pairs={{0,1},{1,0},{2,3},{3,2},{4,5},{5,4},{6,7},{7,6},{8,9},{9,8},{10,11... | collective-permute-start | bytes 1572872 | tf_op jit(solution)/shard_map/ppermute | solution.py:26
  58.8 7.2 %collective-permute-start.3 = (bf16[256,512]{1,0:T(8,128)(2,1)S(1)}, bf16[256,512]{1,0:T(8,128)(2,1)S(1)}, u32[]{:S(2)}, u32[]{:S(2)}) collective-permute-start(bf16[256,512]{1,0:T(8,128)(2,1)S(1)} %slice.56), channel_id=1, source_target_pairs={{0,4},{4,0},{1,5},{5,1},{2,6},{6,2},{3,7},{7,3},{8,12},{12,8},{9,1... | collective-permute-start | bytes 786440 | tf_op jit(solution)/shard_map/ppermute | solution.py:24
  61.9 6.5 %collective-permute-start.4 = (bf16[256,512]{1,0:T(8,128)(2,1)S(1)}, bf16[256,512]{1,0:T(8,128)(2,1)}, u32[]{:S(2)}, u32[]{:S(2)}) collective-permute-start(bf16[256,512]{1,0:T(8,128)(2,1)S(1)} %slice.57), channel_id=1, source_target_pairs={{0,2},{1,3},{2,0},{3,1},{4,6},{5,7},{6,4},{7,5},{8,10},{9,11},{10,... | collective-permute-start | bytes 786440 | tf_op jit(solution)/shard_map/ppermute | solution.py:26
  63.5 6.8 %collective-permute-start.7 = (bf16[512,512]{1,0:T(8,128)(2,1)S(1)}, bf16[512,512]{1,0:T(8,128)(2,1)}, u32[]{:S(2)}, u32[]{:S(2)}) collective-permute-start(bf16[512,512]{1,0:T(8,128)(2,1)S(1)} %collective-permute-done.2.refs_4_.refs_3_), channel_id=1, source_target_pairs={{0,1},{1,0},{2,3},{3,2},{4,5},{5,4},{6,7},{7,6},{8,9},{9,8},{10,11... | collective-permute-start | bytes 1572872 | tf_op jit(solution)/shard_map/ppermute | solution.py:26
  63.5 6.8 %collective-permute-start.6 = (bf16[512,512]{1,0:T(8,128)(2,1)}, bf16[512,512]{1,0:T(8,128)(2,1)}, u32[]{:S(2)}, u32[]{:S(2)}) collective-permute-start(bf16[512,512]{1,0:T(8,128)(2,1)} %collective-permute-done.1.refs_3_.refs_2_), channel_id=1, source_target_pairs={{0,1},{1,0},{2,3},{3,2},{4,5},{5,4},{6,7},{7,6},{8,9},{9,8},{10,11... | collective-permute-start | bytes 1572872 | tf_op jit(solution)/shard_map/ppermute | solution.py:26
  73.1 14.2 %collective-permute-start.10 = (bf16[512,512]{1,0:T(8,128)(2,1)}, bf16[512,512]{1,0:T(8,128)(2,1)S(1)}, u32[]{:S(2)}, u32[]{:S(2)}) collective-permute-start(bf16[512,512]{1,0:T(8,128)(2,1)} %compact_rows.3.refs_1_), channel_id=1, source_target_pairs={{0,2},{1,3},{2,0},{3,1},{4,6},{5,7},{6,4},{7,5},{8,10},{9,11},{10,... | collective-permute-start | bytes 1572872 | tf_op jit(solution)/shard_map/ppermute | solution.py:26
  74.6 14.0 %collective-permute-start.12 = (bf16[512,512]{1,0:T(8,128)(2,1)}, bf16[512,512]{1,0:T(8,128)(2,1)}, u32[]{:S(2)}, u32[]{:S(2)}) collective-permute-start(bf16[512,512]{1,0:T(8,128)(2,1)} %compact_rows.3.refs_1_), channel_id=1, source_target_pairs={{0,4},{4,0},{1,5},{5,1},{2,6},{6,2},{3,7},{7,3},{8,12},{12,8},{9,1... | collective-permute-start | bytes 1572872 | tf_op jit(solution)/shard_map/ppermute | solution.py:24
  83.4 10.3 %collective-permute-start.13 = (bf16[512,512]{1,0:T(8,128)(2,1)}, bf16[512,512]{1,0:T(8,128)(2,1)S(1)}, u32[]{:S(2)}, u32[]{:S(2)}) collective-permute-start(bf16[512,512]{1,0:T(8,128)(2,1)} %compact_rows.3.refs_1_), channel_id=1, source_target_pairs={{0,1},{1,0},{2,3},{3,2},{4,5},{5,4},{6,7},{7,6},{8,9},{9,8},{10,11... | collective-permute-start | bytes 1572872 | tf_op jit(solution)/shard_map/ppermute | solution.py:26
  88.6 5.1 %collective-permute-start.14 = (bf16[512,512]{1,0:T(8,128)(2,1)}, bf16[512,512]{1,0:T(8,128)(2,1)}, u32[]{:S(2)}, u32[]{:S(2)}) collective-permute-start(bf16[512,512]{1,0:T(8,128)(2,1)} %collective-permute-done.12.refs_2_), channel_id=1, source_target_pairs={{0,1},{1,0},{2,3},{3,2},{4,5},{5,4},{6,7},{7,6},{8,9},{9,8},{10,11... | collective-permute-start | bytes 1572872 | tf_op jit(solution)/shard_map/ppermute | solution.py:26
  88.6 5.1 %collective-permute-start.15 = (bf16[512,512]{1,0:T(8,128)(2,1)S(1)}, bf16[512,512]{1,0:T(8,128)(2,1)}, u32[]{:S(2)}, u32[]{:S(2)}) collective-permute-start(bf16[512,512]{1,0:T(8,128)(2,1)S(1)} %collective-permute-done.10.refs_3_), channel_id=1, source_target_pairs={{0,1},{1,0},{2,3},{3,2},{4,5},{5,4},{6,7},{7,6},{8,9},{9,8},{10,11... | collective-permute-start | bytes 1572872 | tf_op jit(solution)/shard_map/ppermute | solution.py:26
  91.5 8.4 %collective-permute-start.16 = (bf16[256,512]{1,0:T(8,128)(2,1)}, bf16[256,512]{1,0:T(8,128)(2,1)S(1)}, u32[]{:S(2)}, u32[]{:S(2)}) collective-permute-start(bf16[256,512]{1,0:T(8,128)(2,1)} %slice.59), channel_id=1, source_target_pairs={{0,2},{1,3},{2,0},{3,1},{4,6},{5,7},{6,4},{7,5},{8,10},{9,11},{10,... | collective-permute-start | bytes 786440 | tf_op jit(solution)/shard_map/ppermute | solution.py:26
  92.0 8.2 %collective-permute-start.11 = (bf16[256,512]{1,0:T(8,128)(2,1)}, bf16[256,512]{1,0:T(8,128)(2,1)}, u32[]{:S(2)}, u32[]{:S(2)}) collective-permute-start(bf16[256,512]{1,0:T(8,128)(2,1)} %slice.58), channel_id=1, source_target_pairs={{0,4},{4,0},{1,5},{5,1},{2,6},{6,2},{3,7},{7,3},{8,12},{12,8},{9,1... | collective-permute-start | bytes 786440 | tf_op jit(solution)/shard_map/ppermute | solution.py:24
  113.3 8.1 %collective-permute-start.22 = (bf16[256,512]{1,0:T(8,128)(2,1)S(1)}, bf16[256,512]{1,0:T(8,128)(2,1)S(1)}, u32[]{:S(2)}, u32[]{:S(2)}) collective-permute-start(bf16[256,512]{1,0:T(8,128)(2,1)S(1)} %get-tuple-element.129), channel_id=1, source_target_pairs={{0,2},{1,3},{2,0},{3,1},{4,6},{5,7},{6,4},{7,5},{8,10},{9,11},{10,... | collective-permute-start | bytes 786440 | tf_op jit(solution)/shard_map/ppermute | solution.py:26
  114.7 7.8 %collective-permute-start.21 = (bf16[256,512]{1,0:T(8,128)(2,1)S(1)}, bf16[256,512]{1,0:T(8,128)(2,1)S(1)}, u32[]{:S(2)}, u32[]{:S(2)}) collective-permute-start(bf16[256,512]{1,0:T(8,128)(2,1)S(1)} %get-tuple-element.130), channel_id=1, source_target_pairs={{0,4},{4,0},{1,5},{5,1},{2,6},{6,2},{3,7},{7,3},{8,12},{12,8},{9,1... | collective-permute-start | bytes 786440 | tf_op jit(solution)/shard_map/ppermute | solution.py:24
  122.7 12.6 %collective-permute-start.24 = (bf16[512,512]{1,0:T(8,128)(2,1)S(1)}, bf16[512,512]{1,0:T(8,128)(2,1)S(1)}, u32[]{:S(2)}, u32[]{:S(2)}) collective-permute-start(bf16[512,512]{1,0:T(8,128)(2,1)S(1)} %get-tuple-element.107), channel_id=1, source_target_pairs={{0,2},{1,3},{2,0},{3,1},{4,6},{5,7},{6,4},{7,5},{8,10},{9,11},{10,... | collective-permute-start | bytes 1572872 | tf_op jit(solution)/shard_map/ppermute | solution.py:26
  123.4 12.2 %collective-permute-start.25 = (bf16[512,512]{1,0:T(8,128)(2,1)S(1)}, bf16[512,512]{1,0:T(8,128)(2,1)S(1)}, u32[]{:S(2)}, u32[]{:S(2)}) collective-permute-start(bf16[512,512]{1,0:T(8,128)(2,1)S(1)} %get-tuple-element.108), channel_id=1, source_target_pairs={{0,4},{4,0},{1,5},{5,1},{2,6},{6,2},{3,7},{7,3},{8,12},{12,8},{9,1... | collective-permute-start | bytes 1572872 | tf_op jit(solution)/shard_map/ppermute | solution.py:24
  125.1 9.1 %collective-permute-start.26 = (f32[4,4096]{1,0:T(4,128)S(1)}, f32[4,4096]{1,0:T(4,128)S(1)}, u32[]{:S(2)}, u32[]{:S(2)}) collective-permute-start(f32[4,4096]{1,0:T(4,128)S(1)} %fusion), channel_id=1, source_target_pairs={{0,16},{8,24},{16,0},{24,8},{1,17},{9,25},{17,1},{25,9},{2,18},{10... | collective-permute-start | bytes 196616 | tf_op jit(solution)/shard_map/ppermute | solution.py:457
  138.0 28.4 %all-to-all-start.2 = ((bf16[8,128,512]{2,1,0:T(8,128)(2,1)}), bf16[8,128,512]{2,1,0:T(8,128)(2,1)S(1)}, u32[]{:S(2)}, u32[]{:S(2)}) async-start(bf16[8,128,512]{2,1,0:T(8,128)(2,1)} %copy-done.4), calls=%async_computation.2 | async-start | bytes 2097152 | tf_op jit(solution)/shard_map/all_to_all | solution.py:403
  156.0 5.9 %collective-permute-start.29 = (f32[4,4096]{1,0:T(4,128)S(1)}, f32[4,4096]{1,0:T(4,128)S(1)}, u32[]{:S(2)}, u32[]{:S(2)}) collective-permute-start(f32[4,4096]{1,0:T(4,128)S(1)} %add.98), channel_id=1, source_target_pairs={{0,4},{4,0},{1,5},{5,1},{2,6},{6,2},{3,7},{7,3},{8,12},{12,8},{9,1... | collective-permute-start | bytes 196616 | tf_op jit(solution)/shard_map/ppermute | solution.py:24
  (37 other events, 266.2 us)

commit v4 on v3

--- a/solution.py
+++ b/solution.py
@@ -34,19 +34,13 @@
     return 1 << (m.bit_length() - 1)
 
 
-def plane_gather(own, slots, *before):
-    half = own.shape[0] // 2
-    blocks = {0: [(0, own)]}
+def plane_gather(top, bottom, slots):
+    half = top.shape[0]
+    blocks = {0: [(0, top), (half, bottom)]}
     for m in chip_masks(slots)[1:]:
         low, high = m & -m, top_bit(m)
-        if low == high:
-            blocks[m] = [(0, flip(own, m))]
-        else:
-            first = rows_of(blocks[m ^ low], 0, half)
-            second = rows_of(blocks[m ^ high], half, half)
-            if before:
-                first, second = after(first, *before), after(second, *before)
-            blocks[m] = [(0, flip(first, low)), (half, flip(second, high))]
+        first, second = (blocks[0], blocks[0]) if low == high else (blocks[m ^ low], blocks[m ^ high])
+        blocks[m] = [(0, flip(first[0][1], low)), (half, flip(second[1][1], high))]
     return blocks
 
 
@@ -55,15 +49,6 @@
         blocks[m | CORE] = [(at, flip(x, CORE)) for at, x in blocks[m]]
 
 
-def rows_of(pieces, start, count):
-    for at, x in pieces:
-        if at == start and x.shape[0] == count:
-            return x
-        if at <= start and start + count <= at + x.shape[0]:
-            return x[start - at : start - at + count]
-    raise ValueError("rows split")
-
-
 def after(x, *others):
     return lax.optimization_barrier((x, *others))[0]
 
@@ -72,13 +57,19 @@
     return lax.optimization_barrier(arrays)
 
 
+def in_hbm(x):
+    return pltpu.with_memory_space_constraint(x, pltpu.HBM)
+
+
 class Tiles:
-    def __init__(self, x, axis, count, first=0):
-        self.x, self.axis, self.count, self.first = x, axis, count, first
+    def __init__(self, x, axis, count, hbm=False):
+        self.x, self.axis, self.count = x, axis, count
+        if hbm:
+            self.x = in_hbm(x)
         self.size = x.shape[axis] // (2 * lax.axis_size("tensor"))
 
     def at(self, ref, order_ref, j):
-        here = block_at(order_ref[self.first + j], self.size)
+        here = block_at(order_ref[j], self.size)
         return ref.at[here, :] if self.axis == 0 else ref.at[:, here]
 
 
@@ -88,7 +79,7 @@
         if isinstance(x, Tiles):
             x = x.x
         elif isinstance(x, list):
-            x = pltpu.with_memory_space_constraint(x[0], pltpu.HBM)
+            x = in_hbm(x[0])
         flat_args.append(x)
 
     def run(*refs):
@@ -143,9 +134,9 @@
                 out[e] = got
 
     flops = 2 * experts * bucket * rows * width * len(sources)
-    cut = 2 if halves else 1
+    parts = 2 if halves else 1
     outs = [
-        shaped(experts * cut, bucket, width // cut, dtype=BF),
+        pltpu.HBM((experts * parts, bucket, width // parts), BF),
         pltpu.HBM((experts, rows, bucket), BF),
     ]
     return call(kernel, "pack_rows", flops, outs, [firsts], chosen, *sources)
@@ -154,18 +145,18 @@
 def compact(reach, buckets, cap):
     homes, bucket, width = buckets.shape
 
-    def kernel(reach_ref, buckets_ref, out):
+    def kernel(reach_ref, buckets_ref, top, bottom):
         acc = None
         for s in range(homes):
             at = lax.broadcasted_iota(jnp.int32, (cap, bucket), 0) - reach_ref[s]
             hot = lax.broadcasted_iota(jnp.int32, (cap, bucket), 1) == at
             term = dot(hot.astype(F32).astype(BF), buckets_ref[s], 1, 0)
             acc = term if acc is None else acc + term
-        out[...] = acc.astype(BF)
+        top[...], bottom[...] = acc[: cap // 2].astype(BF), acc[cap // 2 :].astype(BF)
 
     flops = 2 * cap * homes * bucket * width
-    outs = [shaped(cap, width, dtype=BF)]
-    return call(kernel, "compact_rows", flops, outs, [reach], buckets)[0]
+    outs = [shaped(cap // 2, width, dtype=BF)] * 2
+    return call(kernel, "compact_rows", flops, outs, [reach], buckets)
 
 
 def place(reach, homes, bucket, terms):
@@ -233,35 +224,35 @@
 
 def project_in(order, expert, blocks, keys, w_in, router):
     spots, xs = flat(blocks, keys)
-    cap, width = blocks[0][0][1].shape
+    cap, width = 2 * blocks[0][0][1].shape[0], blocks[0][0][1].shape[1]
     hidden = w_in.shape[1]
     experts = router.shape[0]
 
     def kernel(order_ref, expert_ref, *refs):
         ins, (tiles, r_ref, a_ref, gate_ref) = refs[: len(xs)], refs[len(xs) :]
-        scores = None
+        scores = {}
         for (j, at, rows), x in zip(spots, ins):
             s = dot(x[...], r_ref[:, block_at(order_ref[j], width)], 1, 1)
-            scores = [(at, s)] if scores is None else add_rows(scores, at, rows, s)
+            scores[at] = scores[at] + s if at in scores else s
             a = dot(x[...], tiles[j][...], 1, 0)
             if j == 0:
                 a_ref[at : at + rows, :] = a
             else:
                 a_ref[at : at + rows, :] += a
-        for at, s in scores:
+        for at, s in scores.items():
             mine = lax.broadcasted_iota(jnp.int32, s.shape, 1) == expert_ref[0]
             picked = jnp.sum(jnp.where(mine, s, 0.0), axis=1, keepdims=True)
             gate_ref[at : at + s.shape[0], :] = jax.nn.sigmoid(picked)
 
     flops = 2 * cap * width * len(keys) * hidden
     outs = [shaped(cap, hidden), shaped(cap, 1)]
-    tiles = Tiles(w_in, 0, len(keys))
+    tiles = Tiles(w_in, 0, len(keys), hbm=True)
     return call(kernel, "project_in", flops, outs, [order, expert], *[[x] for x in xs], tiles, router)
 
 
 def project_out(order, blocks, keys, w_out):
     spots, ys = flat(blocks, keys)
-    cap, width = blocks[0][0][1].shape
+    cap, width = 2 * blocks[0][0][1].shape[0], blocks[0][0][1].shape[1]
     hidden = w_out.shape[0]
 
     def kernel(order_ref, *refs):
@@ -334,7 +325,7 @@
 
 def grads_in(order, blocks, keys, pre_grad):
     spots, xs = flat(blocks, keys)
-    cap, width = blocks[0][0][1].shape
+    cap, width = 2 * blocks[0][0][1].shape[0], blocks[0][0][1].shape[1]
     hidden = pre_grad.shape[1]
 
     def kernel(order_ref, *refs):
@@ -354,7 +345,7 @@
 
 def grads_out(order, blocks, keys, gated):
     spots, ys = flat(blocks, keys)
-    cap, width = blocks[0][0][1].shape
+    cap, width = 2 * blocks[0][0][1].shape[0], blocks[0][0][1].shape[1]
     hidden = gated.shape[1]
 
     def kernel(order_ref, *refs):
@@ -421,14 +412,15 @@
     x_got, y_sent, *tiles = join(x_got, y_sent, *tiles)
 
     y_got = exchange(y_sent, "plane")
-    xs = plane_gather(compact(reach, x_got, cap), slots)
-    add_core(xs, masks)
+    xs = plane_gather(*compact(reach, x_got, cap), slots)
+    add_core(xs, early)
     pieces = [x for m in xs for _, x in xs[m]]
     y_got, *pieces = join(y_got, *pieces)
     xs = {m: [(at, pieces.pop(0)) for at, _ in xs[m]] for m in xs}
+    add_core(xs, late)
 
     pre_act, gate = project_in(order, expert, xs, keys, w_in, router.T)
-    ys = plane_gather(compact(reach[::2], y_got, cap), slots, pre_act)
+    ys = plane_gather(*compact(reach[::2], y_got, cap), slots)
     tied = {m: [(at, after(x, pre_act)) for at, x in ys[m]] for m in early}
     add_core(tied, early)
     ys.update({m: tied[m] for m in tied if m & CORE})
@@ -463,24 +455,25 @@
         return total + hops.pop(0)(total) if hops else total
 
     mid = cap // 2
-    got1, got2 = flip(far1, CORE), flip(far2, CORE)
+    got1 = flip(far1, CORE)
+    got1, near1, score_grad, far2 = join(got1, near1, score_grad, far2)
+    got2 = flip(far2, CORE)
+    sums = {m: near1[k] + got1[k].astype(F32) for k, m in enumerate(groups[0])}
     column = router_column(order, xs, keys, score_grad)
-    got1, got2, column = join(got1, got2, column)
-    total = jnp.where(jnp.arange(planes)[:, None] == plane, column, 0.0)
-    sums = {m: near1[k] + got1[k].astype(F32) for k, m in enumerate(groups[0])}
     sums.update({m: near2[k] + got2[k].astype(F32) for k, m in enumerate(groups[1])})
-    total = hop(total)
     for m in groups[0]:
         low, high = m & -m, top_bit(m)
         a, b = flip(sums[m][:mid].astype(BF), low), flip(sums[m][mid:].astype(BF), high)
-        a, b, total, *rest = join(a, b, total, *[sums[k] for k in groups[1]])
+        a, b, column, *rest = join(a, b, column, *[sums[k] for k in groups[1]])
         sums.update(zip(groups[1], rest))
         pad = jnp.zeros((cap - mid, width), F32)
         sums[m ^ low] = sums[m ^ low] + jnp.concatenate([a.astype(F32), pad])
         sums[m ^ high] = sums[m ^ high] + jnp.concatenate([pad, b.astype(F32)])
     sent = [sums[m].astype(BF) for m in groups[1] if m]
-    *sent, total, pre_grad = join(*sent, total, pre_grad)
+    *sent, column, pre_grad = join(*sent, column, pre_grad)
     came = [flip(x, m) for x, m in zip(sent, groups[1])]
+    total = jnp.where(jnp.arange(planes)[:, None] == plane, column, 0.0)
+    total = hop(total)
     grad_in = grads_in(order, xs, keys, pre_grad)
     total = hop(total)
     *terms, grad_in, total = join(sums[0], *came, grad_in, total)

time: 169 us -> 166 us (0.982)
  local copies, waits for them, and re-layouts: 18.1 us -> 14.9 us
    ppermute x20 -> x28, waiting for transfers between devices: 32.1 us -> 23.6 us  [flip(): return lax.ppermute(x, 'tensor', [(i, i ^ bit >> 1) for i in range(n)])]
    ppermute x8 -> x10, waiting for transfers between devices: 20.8 us -> 26.3 us  [flip(): return lax.ppermute(x, 'half', [(0, 1), (1, 0)])]
    slice x5 -> x1, local copies, waits for them, and re-layouts: 3.46 us -> 0.09 us  [body(): ys = plane_gather(*compact(reach[::2], y_got, cap), slots)]
    ppermute x20 -> x28, starting transfers between devices: 10.1 us -> 11.6 us  [flip(): return lax.ppermute(x, 'tensor', [(i, i ^ bit >> 1) for i in range(n)])]
    ppermute x8 -> x10, starting transfers between devices: 11.7 us -> 11.5 us  [flip(): return lax.ppermute(x, 'half', [(0, 1), (1, 0)])]
    unnamed x56 -> x76, local copies, waits for them, and re-layouts: 10.3 us -> 10.5 us
  transfers between devices with their start and end apart: 33 -> 43, of which waited for: 20 -> 23; matrix products, arithmetic and copies ran while one was open for 6% -> 4% of each run, Pallas kernels for 19% -> 21%
where the time goes in v4:
time: 166 us
  waiting for transfers between devices  59.5 us (36%)
  Pallas kernels  44.4 us (27%)
  starting transfers between devices  43.1 us (26%)
  local copies, waits for them, and re-layouts  14.9 us (9%)
  other arithmetic  2.42 us (1%)
    pallas_call x12, Pallas kernels, call(): pl.pallas_call(run, in_specs=[pl.BlockSpec(memory_space=pltpu.SMEM)] * le...  44.4 us
    ppermute x10, waiting for transfers between devices, flip(): return lax.ppermute(x, 'half', [(0, 1), (1, 0)])  26.3 us
    ppermute x28, waiting for transfers between devices, flip(): return lax.ppermute(x, 'tensor', [(i, i ^ bit >> 1) for i in range(n)])  23.6 us
    all_to_all x3, starting transfers between devices, exchange(): return lax.all_to_all(x, axes, split_axis=0, concat_axis=0, tiled=True)  15.2 us
    ppermute x28, starting transfers between devices, flip(): return lax.ppermute(x, 'tensor', [(i, i ^ bit >> 1) for i in range(n)])  11.6 us
    ppermute x10, starting transfers between devices, flip(): return lax.ppermute(x, 'half', [(0, 1), (1, 0)])  11.5 us
    unnamed x76, local copies, waits for them, and re-layouts  10.5 us
    all_to_all x3, waiting for transfers between devices, exchange(): return lax.all_to_all(x, axes, split_axis=0, concat_axis=0, tiled=True)  8.7 us
  transfers between devices with their start and end apart: 43, of which 23 were waited for; matrix products, arithmetic and copies ran while one was open for 4% of the time, Pallas kernels for 21%

profile of v4, /device:TPU:0, one launch (start us, length us, event | category | flops | bytes accessed | tf_op | source)
XLA Modules:
  0.0 165.6 jit_solution(18073640128873859559)
XLA Ops:
  3.0 2.4 %pack_rows.2 = (bf16[8,128,512]{2,1,0:T(8,128)(2,1)}, bf16[4,256,128]{2,1,0:T(8,128)(2,1)}) custom-call(s32[2]{0:T(128)S(1)} %pad_add_fusion.refs_0_, s32[4,512]{1,0:T(4,128)S(1)} %copy-done.22, bf16[256,1024]{1,0:T(8,128)(2,1)S(1)} %constant_dynamic-slice_fusion.5.refs_2_), custom_call_target="tpu_custom_call" | custom-call | flops 268435456 | bytes 3153928 | tf_op jit(solution)/shard_map/pack_rows/pallas_call | solution.py:93
  5.4 7.3 %all-to-all-start = ((bf16[8,128,512]{2,1,0:T(8,128)(2,1)}), bf16[8,128,512]{2,1,0:T(8,128)(2,1)S(1)}, u32[]{:S(2)}, u32[]{:S(2)}) async-start(bf16[8,128,512]{2,1,0:T(8,128)(2,1)} %get-tuple-element.74), calls=%async_computation | async-start | bytes 2097152 | tf_op jit(solution)/shard_map/all_to_all | solution.py:394
  16.5 2.2 %constant_dynamic-slice_fusion = (bf16[512,512]{1,0:T(8,128)(2,1)}, bf16[512,512]{1,0:T(8,128)(2,1)}) fusion(bf16[512,4096]{1,0:T(8,128)(2,1)} %refs_13_, s32[]{:T(128)S(6)} %select_n.34, s32[]{:T(128)S(6)} %select_n.33), kind=kLoop, calls=%fused_computation.11 | loop fusion | bytes 2097160 | tf_op jit(solution)/shard_map/dynamic_slice | solution.py:391
  18.7 11.8 %collective-permute-done.refs_3_ = bf16[256,512]{1,0:T(8,128)(2,1)} collective-permute-done((bf16[256,512]{1,0:T(8,128)(2,1)}, bf16[256,512]{1,0:T(8,128)(2,1)}, u32[]{:S(2)}, u32[]{:S(2)}) %collective-permute-start) | collective-permute-done | bytes 262176 | tf_op jit(solution)/shard_map/ppermute | solution.py:24
  30.6 3.2 %pack_rows.3 = (bf16[4,256,512]{2,1,0:T(8,128)(2,1)}, bf16[4,256,256]{2,1,0:T(8,128)(2,1)}) custom-call(s32[3]{0:T(128)S(1)} %pad_add_fusion.1.refs_0_, s32[4,512]{1,0:T(4,128)S(1)} %copy-done.23, bf16[256,512]{1,0:T(8,128)(2,1)S(1)} %get-tuple-element.148.refs_2_, bf16[256,512]{1,0:T(8,128)(2,1)} %collective-permute-done.refs_3_), custom_call_target="tpu_custom_call" | custom-call | flops 536870912 | bytes 3678220 | tf_op jit(solution)/shard_map/pack_rows/pallas_call | solution.py:93
  33.8 4.6 %all-to-all-done.refs_1_ = bf16[8,128,512]{2,1,0:T(8,128)(2,1)S(1)} async-done(((bf16[8,128,512]{2,1,0:T(8,128)(2,1)}), bf16[8,128,512]{2,1,0:T(8,128)(2,1)S(1)}, u32[]{:S(2)}, u32[]{:S(2)}) %all-to-all-start) | async-done | bytes 1048608 | tf_op jit(solution)/shard_map/all_to_all | solution.py:394
  38.4 4.3 %all-to-all-start.1 = ((bf16[4,256,512]{2,1,0:T(8,128)(2,1)}), bf16[4,256,512]{2,1,0:T(8,128)(2,1)}, u32[]{:S(2)}, u32[]{:S(2)}) async-start(bf16[4,256,512]{2,1,0:T(8,128)(2,1)} %get-tuple-element.78), calls=%async_computation.1 | async-start | bytes 2097152 | tf_op jit(solution)/shard_map/all_to_all | solution.py:394
  50.1 5.0 %collective-permute-done.3.refs_6_.refs_5_ = bf16[256,512]{1,0:T(8,128)(2,1)S(1)} collective-permute-done((bf16[256,512]{1,0:T(8,128)(2,1)S(1)}, bf16[256,512]{1,0:T(8,128)(2,1)S(1)}, u32[]{:S(2)}, u32[]{:S(2)}) %collective-permute-start.3) | collective-permute-done | bytes 262176 | tf_op jit(solution)/shard_map/ppermute | solution.py:26
  58.1 2.2 %collective-permute-done.4.refs_7_.refs_6_ = bf16[256,512]{1,0:T(8,128)(2,1)S(1)} collective-permute-done((bf16[256,512]{1,0:T(8,128)(2,1)S(1)}, bf16[256,512]{1,0:T(8,128)(2,1)S(1)}, u32[]{:S(2)}, u32[]{:S(2)}) %collective-permute-start.4) | collective-permute-done | bytes 262176 | tf_op jit(solution)/shard_map/ppermute | solution.py:26
  62.9 4.3 %collective-permute-done.5.refs_14_.refs_13_ = bf16[256,512]{1,0:T(8,128)(2,1)} collective-permute-done((bf16[256,512]{1,0:T(8,128)(2,1)S(1)}, bf16[256,512]{1,0:T(8,128)(2,1)}, u32[]{:S(2)}, u32[]{:S(2)}) %collective-permute-start.5) | collective-permute-done | bytes 262176 | tf_op jit(solution)/shard_map/ppermute | solution.py:24
  68.8 2.4 %collective-permute-done.6.refs_15_.refs_14_ = bf16[256,512]{1,0:T(8,128)(2,1)} collective-permute-done((bf16[256,512]{1,0:T(8,128)(2,1)S(1)}, bf16[256,512]{1,0:T(8,128)(2,1)}, u32[]{:S(2)}, u32[]{:S(2)}) %collective-permute-start.6) | collective-permute-done | bytes 262176 | tf_op jit(solution)/shard_map/ppermute | solution.py:26
  78.0 7.0 %project_in.1 = (f32[512,512]{1,0:T(8,128)S(1)}, f32[512,1]{1,0:T(8,128)S(1)}) custom-call(s32[8]{0:T(128)S(1)} %stack.79.refs_0_, s32[1]{0:T(128)} %bitcast.12.refs_1_, bf16[256,512]{1,0:T(8,128)(2,1)} %copy-done.3, bf16[256,512]{1,0:T(8,128)(2,1)} %copy-done.4, bf16[256,512]{1,0:T(8,128)(2,1)} %copy-done.30, bf16[256,512]{1,0:T(8,128)(2,1)} %copy-done.33, ...), custom_call_target="tpu_custom_call" | custom-call | flops 2147483648 | bytes 9472036 | tf_op jit(solution)/shard_map/project_in/pallas_call | solution.py:93
  93.2 4.7 %project_out.1.refs_9_ = f32[512,512]{1,0:T(8,128)S(1)} custom-call(s32[6]{0:T(128)S(1)} %stack.78.refs_0_, bf16[256,512]{1,0:T(8,128)(2,1)S(1)} %get-tuple-element.100.refs_1_, bf16[256,512]{1,0:T(8,128)(2,1)S(1)} %get-tuple-element.101.refs_2_, bf16[256,512]{1,0:T(8,128)(2,1)S(1)} %collective-permute-done.15.refs_3_, ...), custom_call_target="tpu_custom_call" | custom-call | flops 1610612736 | bytes 8388632 | tf_op jit(solution)/shard_map/project_out/pallas_call | solution.py:93
  102.1 4.4 %activation.1 = (bf16[512,512]{1,0:T(8,128)(2,1)S(1)}, bf16[512,512]{1,0:T(8,128)(2,1)S(1)}, f32[512,1]{1,0:T(8,128)S(1)}, bf16[1,512,512]{2,1,0:T(8,128)(2,1)S(...) custom-call(s32[8]{0:T(128)S(1)} %stack.74.refs_0_, ...), custom_call_target="tpu_custom_call" | custom-call | flops 2684354560 | bytes 18894880 | tf_op jit(solution)/shard_map/activation/pallas_call | solution.py:93
  110.8 3.1 %router_column.1 = f32[1,4096]{1,0:T(1,128)S(1)} custom-call(s32[8]{0:T(128)S(1)} %stack.79.refs_0_, bf16[256,512]{1,0:T(8,128)(2,1)} %copy-done.3, bf16[256,512]{1,0:T(8,128)(2,1)} %copy-done.4, bf16[256,512]{1,0:T(8,128)(2,1)} %copy-done.30, bf16[256,512]{1,0:T(8,128)(2,1)} %copy-done.33, bf16[256,512]{1,0:T(8,128)(2,1)} %copy-done.29, ...), custom_call_target="tpu_custom_call" | custom-call | flops 4194304 | bytes 4212768 | tf_op jit(solution)/shard_map/router_column/pallas_call | solution.py:93
  114.6 2.9 %collective-permute-done.31 = bf16[256,512]{1,0:T(8,128)(2,1)S(1)} collective-permute-done((bf16[256,512]{1,0:T(8,128)(2,1)S(1)}, bf16[256,512]{1,0:T(8,128)(2,1)S(1)}, u32[]{:S(2)}, u32[]{:S(2)}) %collective-permute-start.31) | collective-permute-done | bytes 262176 | tf_op jit(solution)/shard_map/ppermute | solution.py:26
  123.2 2.9 %collective-permute-start.36 = (f32[4,4096]{1,0:T(4,128)S(1)}, f32[4,4096]{1,0:T(4,128)S(1)}, u32[]{:S(2)}, u32[]{:S(2)}) collective-permute-start(f32[4,4096]{1,0:T(4,128)S(1)} %fusion), channel_id=1, source_target_pairs={{0,16},{8,24},{16,0},{24,8},{1,17},{9,25},{17,1},{25,9},{2,18},{10... | collective-permute-start | bytes 196616 | tf_op jit(solution)/shard_map/ppermute | solution.py:449
  126.1 6.5 %grads_in.1 = bf16[4096,512]{1,0:T(8,128)(2,1)} custom-call(s32[8]{0:T(128)S(1)} %stack.79.refs_0_, bf16[256,512]{1,0:T(8,128)(2,1)} %copy-done.3, bf16[256,512]{1,0:T(8,128)(2,1)} %copy-done.4, bf16[256,512]{1,0:T(8,128)(2,1)} %copy-done.30, bf16[256,512]{1,0:T(8,128)(2,1)} %copy-done.33, bf16[256,512]{1,0:T(8,128)(2,1)} %copy-done.29, ...), custom_call_target="tpu_custom_call" | custom-call | flops 2147483648 | bytes 13107232 | tf_op jit(solution)/shard_map/grads_in/pallas_call | solution.py:93
  136.5 3.7 %all-to-all-start.2 = ((bf16[8,128,512]{2,1,0:T(8,128)(2,1)}), bf16[8,128,512]{2,1,0:T(8,128)(2,1)S(1)}, u32[]{:S(2)}, u32[]{:S(2)}) async-start(bf16[8,128,512]{2,1,0:T(8,128)(2,1)} %copy-done.2), calls=%async_computation.2 | async-start | bytes 2097152 | tf_op jit(solution)/shard_map/all_to_all | solution.py:394
  141.2 6.6 %grads_out.1 = bf16[512,4096]{1,0:T(8,128)(2,1)} custom-call(s32[8]{0:T(128)S(1)} %stack.79.refs_0_, bf16[256,512]{1,0:T(8,128)(2,1)} %copy-done.5, bf16[256,512]{1,0:T(8,128)(2,1)} %copy-done.6, bf16[256,512]{1,0:T(8,128)(2,1)} %copy-done.7, bf16[256,512]{1,0:T(8,128)(2,1)} %collective-permute-done.16.refs_4_, ...), custom_call_target="tpu_custom_call" | custom-call | flops 2147483648 | bytes 13107232 | tf_op jit(solution)/shard_map/grads_out/pallas_call | solution.py:93
  149.0 3.1 %collective-permute-done.37 = f32[4,4096]{1,0:T(4,128)S(1)} collective-permute-done((f32[4,4096]{1,0:T(4,128)S(1)}, f32[4,4096]{1,0:T(4,128)S(1)}, u32[]{:S(2)}, u32[]{:S(2)}) %collective-permute-start.37) | collective-permute-done | bytes 65568 | tf_op jit(solution)/shard_map/ppermute | solution.py:26
  153.4 2.1 %collective-permute-start.39 = (f32[4,4096]{1,0:T(4,128)S(1)}, f32[4,4096]{1,0:T(4,128)S(1)}, u32[]{:S(2)}, u32[]{:S(2)}) collective-permute-start(f32[4,4096]{1,0:T(4,128)S(1)} %add.98), channel_id=1, source_target_pairs={{0,4},{4,0},{1,5},{5,1},{2,6},{6,2},{3,7},{7,3},{8,12},{12,8},{9,1... | collective-permute-start | bytes 196616 | tf_op jit(solution)/shard_map/ppermute | solution.py:24
  155.5 3.8 %collective-permute-done.39 = f32[4,4096]{1,0:T(4,128)S(1)} collective-permute-done((f32[4,4096]{1,0:T(4,128)S(1)}, f32[4,4096]{1,0:T(4,128)S(1)}, u32[]{:S(2)}, u32[]{:S(2)}) %collective-permute-start.39) | collective-permute-done | bytes 65568 | tf_op jit(solution)/shard_map/ppermute | solution.py:24
  160.0 4.1 %all-to-all-done.2.refs_1_ = bf16[8,128,512]{2,1,0:T(8,128)(2,1)S(1)} async-done(((bf16[8,128,512]{2,1,0:T(8,128)(2,1)}), bf16[8,128,512]{2,1,0:T(8,128)(2,1)S(1)}, u32[]{:S(2)}, u32[]{:S(2)}) %all-to-all-start.2) | async-done | bytes 1048608 | tf_op jit(solution)/shard_map/all_to_all | solution.py:394
  (174 shorter events, 59.8 us)
Async XLA Ops:
  5.4 33.0 %all-to-all-start = ((bf16[8,128,512]{2,1,0:T(8,128)(2,1)}), bf16[8,128,512]{2,1,0:T(8,128)(2,1)S(1)}, u32[]{:S(2)}, u32[]{:S(2)}) async-start(bf16[8,128,512]{2,1,0:T(8,128)(2,1)} %get-tuple-element.74), calls=%async_computation | async-start | bytes 2097152 | tf_op jit(solution)/shard_map/all_to_all | solution.py:394
  14.4 16.2 %collective-permute-start = (bf16[256,512]{1,0:T(8,128)(2,1)}, bf16[256,512]{1,0:T(8,128)(2,1)}, u32[]{:S(2)}, u32[]{:S(2)}) collective-permute-start(bf16[256,512]{1,0:T(8,128)(2,1)} %get-tuple-element.147), channel_id=1, source_target_pairs={{0,4},{4,0},{1,5},{5,1},{2,6},{6,2},{3,7},{7,3},{8,12},{12,8},{9,1... | collective-permute-start | bytes 786440 | tf_op jit(solution)/shard_map/ppermute | solution.py:24
  38.4 32.8 %all-to-all-start.1 = ((bf16[4,256,512]{2,1,0:T(8,128)(2,1)}), bf16[4,256,512]{2,1,0:T(8,128)(2,1)}, u32[]{:S(2)}, u32[]{:S(2)}) async-start(bf16[4,256,512]{2,1,0:T(8,128)(2,1)} %get-tuple-element.78), calls=%async_computation.1 | async-start | bytes 2097152 | tf_op jit(solution)/shard_map/all_to_all | solution.py:394
  46.0 9.2 %collective-permute-start.3 = (bf16[256,512]{1,0:T(8,128)(2,1)S(1)}, bf16[256,512]{1,0:T(8,128)(2,1)S(1)}, u32[]{:S(2)}, u32[]{:S(2)}) collective-permute-start(bf16[256,512]{1,0:T(8,128)(2,1)S(1)} %get-tuple-element.85.refs_2_.refs_1_), channel_id=1, source_target_pairs={{0,2},{1,3},{2,0},{3,1},{4,6},{5,7},{6,4},{7,5},{8,10},{9,11},{10,... | collective-permute-start | bytes 786440 | tf_op jit(solution)/shard_map/ppermute | solution.py:26
  47.5 9.2 %collective-permute-start.1 = (bf16[256,512]{1,0:T(8,128)(2,1)S(1)}, bf16[256,512]{1,0:T(8,128)(2,1)S(1)}, u32[]{:S(2)}, u32[]{:S(2)}) collective-permute-start(bf16[256,512]{1,0:T(8,128)(2,1)S(1)} %get-tuple-element.85.refs_2_.refs_1_), channel_id=1, source_target_pairs={{0,4},{4,0},{1,5},{5,1},{2,6},{6,2},{3,7},{7,3},{8,12},{12,8},{9,1... | collective-permute-start | bytes 786440 | tf_op jit(solution)/shard_map/ppermute | solution.py:24
  49.0 9.2 %collective-permute-start.8 = (bf16[256,512]{1,0:T(8,128)(2,1)S(1)}, bf16[256,512]{1,0:T(8,128)(2,1)S(1)}, u32[]{:S(2)}, u32[]{:S(2)}) collective-permute-start(bf16[256,512]{1,0:T(8,128)(2,1)S(1)} %get-tuple-element.86.refs_3_.refs_2_), channel_id=1, source_target_pairs={{0,1},{1,0},{2,3},{3,2},{4,5},{5,4},{6,7},{7,6},{8,9},{9,8},{10,11... | collective-permute-start | bytes 786440 | tf_op jit(solution)/shard_map/ppermute | solution.py:26
  49.0 11.3 %collective-permute-start.4 = (bf16[256,512]{1,0:T(8,128)(2,1)S(1)}, bf16[256,512]{1,0:T(8,128)(2,1)S(1)}, u32[]{:S(2)}, u32[]{:S(2)}) collective-permute-start(bf16[256,512]{1,0:T(8,128)(2,1)S(1)} %get-tuple-element.86.refs_3_.refs_2_), channel_id=1, source_target_pairs={{0,2},{1,3},{2,0},{3,1},{4,6},{5,7},{6,4},{7,5},{8,10},{9,11},{10,... | collective-permute-start | bytes 786440 | tf_op jit(solution)/shard_map/ppermute | solution.py:26
  49.5 12.8 %collective-permute-start.2 = (bf16[256,512]{1,0:T(8,128)(2,1)S(1)}, bf16[256,512]{1,0:T(8,128)(2,1)S(1)}, u32[]{:S(2)}, u32[]{:S(2)}) collective-permute-start(bf16[256,512]{1,0:T(8,128)(2,1)S(1)} %get-tuple-element.86.refs_3_.refs_2_), channel_id=1, source_target_pairs={{0,4},{4,0},{1,5},{5,1},{2,6},{6,2},{3,7},{7,3},{8,12},{12,8},{9,1... | collective-permute-start | bytes 786440 | tf_op jit(solution)/shard_map/ppermute | solution.py:24
  55.1 7.2 %collective-permute-start.11 = (bf16[256,512]{1,0:T(8,128)(2,1)S(1)}, bf16[256,512]{1,0:T(8,128)(2,1)S(1)}, u32[]{:S(2)}, u32[]{:S(2)}) collective-permute-start(bf16[256,512]{1,0:T(8,128)(2,1)S(1)} %collective-permute-done.3.refs_6_.refs_5_), channel_id=1, source_target_pairs={{0,1},{1,0},{2,3},{3,2},{4,5},{5,4},{6,7},{7,6},{8,9},{9,8},{10,11... | collective-permute-start | bytes 786440 | tf_op jit(solution)/shard_map/ppermute | solution.py:26
  56.7 10.6 %collective-permute-start.5 = (bf16[256,512]{1,0:T(8,128)(2,1)S(1)}, bf16[256,512]{1,0:T(8,128)(2,1)}, u32[]{:S(2)}, u32[]{:S(2)}) collective-permute-start(bf16[256,512]{1,0:T(8,128)(2,1)S(1)} %collective-permute-done.3.refs_6_.refs_5_), channel_id=1, source_target_pairs={{0,4},{4,0},{1,5},{5,1},{2,6},{6,2},{3,7},{7,3},{8,12},{12,8},{9,1... | collective-permute-start | bytes 786440 | tf_op jit(solution)/shard_map/ppermute | solution.py:24
  58.1 9.1 %collective-permute-start.9 = (bf16[256,512]{1,0:T(8,128)(2,1)S(1)}, bf16[256,512]{1,0:T(8,128)(2,1)S(1)}, u32[]{:S(2)}, u32[]{:S(2)}) collective-permute-start(bf16[256,512]{1,0:T(8,128)(2,1)S(1)} %collective-permute-done.1.refs_4_.refs_3_), channel_id=1, source_target_pairs={{0,1},{1,0},{2,3},{3,2},{4,5},{5,4},{6,7},{7,6},{8,9},{9,8},{10,11... | collective-permute-start | bytes 786440 | tf_op jit(solution)/shard_map/ppermute | solution.py:26
  62.4 8.9 %collective-permute-start.6 = (bf16[256,512]{1,0:T(8,128)(2,1)S(1)}, bf16[256,512]{1,0:T(8,128)(2,1)}, u32[]{:S(2)}, u32[]{:S(2)}) collective-permute-start(bf16[256,512]{1,0:T(8,128)(2,1)S(1)} %collective-permute-done.2.refs_5_.refs_4_), channel_id=1, source_target_pairs={{0,2},{1,3},{2,0},{3,1},{4,6},{5,7},{6,4},{7,5},{8,10},{9,11},{10,... | collective-permute-start | bytes 786440 | tf_op jit(solution)/shard_map/ppermute | solution.py:26
  73.9 12.8 %collective-permute-start.15 = (bf16[256,512]{1,0:T(8,128)(2,1)S(1)}, bf16[256,512]{1,0:T(8,128)(2,1)S(1)}, u32[]{:S(2)}, u32[]{:S(2)}) collective-permute-start(bf16[256,512]{1,0:T(8,128)(2,1)S(1)} %get-tuple-element.100.refs_1_), channel_id=1, source_target_pairs={{0,4},{4,0},{1,5},{5,1},{2,6},{6,2},{3,7},{7,3},{8,12},{12,8},{9,1... | collective-permute-start | bytes 786440 | tf_op jit(solution)/shard_map/ppermute | solution.py:24
  75.4 13.7 %collective-permute-start.13 = (bf16[256,512]{1,0:T(8,128)(2,1)S(1)}, bf16[256,512]{1,0:T(8,128)(2,1)}, u32[]{:S(2)}, u32[]{:S(2)}) collective-permute-start(bf16[256,512]{1,0:T(8,128)(2,1)S(1)} %get-tuple-element.100.refs_1_), channel_id=1, source_target_pairs={{0,2},{1,3},{2,0},{3,1},{4,6},{5,7},{6,4},{7,5},{8,10},{9,11},{10,... | collective-permute-start | bytes 786440 | tf_op jit(solution)/shard_map/ppermute | solution.py:26
  75.9 13.1 %collective-permute-start.17 = (bf16[256,512]{1,0:T(8,128)(2,1)S(1)}, bf16[256,512]{1,0:T(8,128)(2,1)}, u32[]{:S(2)}, u32[]{:S(2)}) collective-permute-start(bf16[256,512]{1,0:T(8,128)(2,1)S(1)} %get-tuple-element.101.refs_2_), channel_id=1, source_target_pairs={{0,2},{1,3},{2,0},{3,1},{4,6},{5,7},{6,4},{7,5},{8,10},{9,11},{10,... | collective-permute-start | bytes 786440 | tf_op jit(solution)/shard_map/ppermute | solution.py:26
  77.4 11.6 %collective-permute-start.16 = (bf16[256,512]{1,0:T(8,128)(2,1)S(1)}, bf16[256,512]{1,0:T(8,128)(2,1)}, u32[]{:S(2)}, u32[]{:S(2)}) collective-permute-start(bf16[256,512]{1,0:T(8,128)(2,1)S(1)} %get-tuple-element.101.refs_2_), channel_id=1, source_target_pairs={{0,4},{4,0},{1,5},{5,1},{2,6},{6,2},{3,7},{7,3},{8,12},{12,8},{9,1... | collective-permute-start | bytes 786440 | tf_op jit(solution)/shard_map/ppermute | solution.py:24
  90.1 8.6 %collective-permute-start.26 = (bf16[256,512]{1,0:T(8,128)(2,1)}, bf16[256,512]{1,0:T(8,128)(2,1)}, u32[]{:S(2)}, u32[]{:S(2)}) collective-permute-start(bf16[256,512]{1,0:T(8,128)(2,1)} %collective-permute-done.16.refs_4_), channel_id=1, source_target_pairs={{0,2},{1,3},{2,0},{3,1},{4,6},{5,7},{6,4},{7,5},{8,10},{9,11},{10,... | collective-permute-start | bytes 786440 | tf_op jit(solution)/shard_map/ppermute | solution.py:26
  91.3 8.6 %collective-permute-start.14 = (bf16[256,512]{1,0:T(8,128)(2,1)}, bf16[256,512]{1,0:T(8,128)(2,1)}, u32[]{:S(2)}, u32[]{:S(2)}) collective-permute-start(bf16[256,512]{1,0:T(8,128)(2,1)} %collective-permute-done.13.refs_5_), channel_id=1, source_target_pairs={{0,4},{4,0},{1,5},{5,1},{2,6},{6,2},{3,7},{7,3},{8,12},{12,8},{9,1... | collective-permute-start | bytes 786440 | tf_op jit(solution)/shard_map/ppermute | solution.py:24
  108.9 8.6 %collective-permute-start.31 = (bf16[256,512]{1,0:T(8,128)(2,1)S(1)}, bf16[256,512]{1,0:T(8,128)(2,1)S(1)}, u32[]{:S(2)}, u32[]{:S(2)}) collective-permute-start(bf16[256,512]{1,0:T(8,128)(2,1)S(1)} %get-tuple-element.149), channel_id=1, source_target_pairs={{0,2},{1,3},{2,0},{3,1},{4,6},{5,7},{6,4},{7,5},{8,10},{9,11},{10,... | collective-permute-start | bytes 786440 | tf_op jit(solution)/shard_map/ppermute | solution.py:26
  110.2 8.3 %collective-permute-start.30 = (bf16[256,512]{1,0:T(8,128)(2,1)S(1)}, bf16[256,512]{1,0:T(8,128)(2,1)S(1)}, u32[]{:S(2)}, u32[]{:S(2)}) collective-permute-start(bf16[256,512]{1,0:T(8,128)(2,1)S(1)} %get-tuple-element.150), channel_id=1, source_target_pairs={{0,4},{4,0},{1,5},{5,1},{2,6},{6,2},{3,7},{7,3},{8,12},{12,8},{9,1... | collective-permute-start | bytes 786440 | tf_op jit(solution)/shard_map/ppermute | solution.py:24
  120.8 12.8 %collective-permute-start.33 = (bf16[512,512]{1,0:T(8,128)(2,1)S(1)}, bf16[512,512]{1,0:T(8,128)(2,1)S(1)}, u32[]{:S(2)}, u32[]{:S(2)}) collective-permute-start(bf16[512,512]{1,0:T(8,128)(2,1)S(1)} %get-tuple-element.127), channel_id=1, source_target_pairs={{0,2},{1,3},{2,0},{3,1},{4,6},{5,7},{6,4},{7,5},{8,10},{9,11},{10,... | collective-permute-start | bytes 1572872 | tf_op jit(solution)/shard_map/ppermute | solution.py:26
  121.7 12.5 %collective-permute-start.34 = (bf16[512,512]{1,0:T(8,128)(2,1)S(1)}, bf16[512,512]{1,0:T(8,128)(2,1)S(1)}, u32[]{:S(2)}, u32[]{:S(2)}) collective-permute-start(bf16[512,512]{1,0:T(8,128)(2,1)S(1)} %get-tuple-element.128), channel_id=1, source_target_pairs={{0,4},{4,0},{1,5},{5,1},{2,6},{6,2},{3,7},{7,3},{8,12},{12,8},{9,1... | collective-permute-start | bytes 1572872 | tf_op jit(solution)/shard_map/ppermute | solution.py:24
  123.2 9.4 %collective-permute-start.36 = (f32[4,4096]{1,0:T(4,128)S(1)}, f32[4,4096]{1,0:T(4,128)S(1)}, u32[]{:S(2)}, u32[]{:S(2)}) collective-permute-start(f32[4,4096]{1,0:T(4,128)S(1)} %fusion), channel_id=1, source_target_pairs={{0,16},{8,24},{16,0},{24,8},{1,17},{9,25},{17,1},{25,9},{2,18},{10... | collective-permute-start | bytes 196616 | tf_op jit(solution)/shard_map/ppermute | solution.py:449
  136.5 27.6 %all-to-all-start.2 = ((bf16[8,128,512]{2,1,0:T(8,128)(2,1)}), bf16[8,128,512]{2,1,0:T(8,128)(2,1)S(1)}, u32[]{:S(2)}, u32[]{:S(2)}) async-start(bf16[8,128,512]{2,1,0:T(8,128)(2,1)} %copy-done.2), calls=%async_computation.2 | async-start | bytes 2097152 | tf_op jit(solution)/shard_map/all_to_all | solution.py:394
  (57 other events, 429.1 us)

commit v5 on v4

--- a/solution.py
+++ b/solution.py
@@ -265,7 +265,7 @@
                 up[at : at + rows, :] += u
 
     flops = 2 * cap * width * len(keys) * hidden
-    return call(kernel, "project_out", flops, [shaped(cap, hidden)], [order], *ys, [w_out])[0]
+    return call(kernel, "project_out", flops, [shaped(cap, hidden)], [order], *[[y] for y in ys], [w_out])[0]
 
 
 def activation(order, blocks, keys, far, near, tiles, w_in, router_row, upstream, pre_act, gate):
@@ -413,11 +413,11 @@
 
     y_got = exchange(y_sent, "plane")
     xs = plane_gather(*compact(reach, x_got, cap), slots)
-    add_core(xs, early)
-    pieces = [x for m in xs for _, x in xs[m]]
+    ready = [m for m in early if m]
+    pieces = [x for m in ready for _, x in xs[m]]
     y_got, *pieces = join(y_got, *pieces)
-    xs = {m: [(at, pieces.pop(0)) for at, _ in xs[m]] for m in xs}
-    add_core(xs, late)
+    xs.update({m: [(at, pieces.pop(0)) for at, _ in xs[m]] for m in ready})
+    add_core(xs, masks)
 
     pre_act, gate = project_in(order, expert, xs, keys, w_in, router.T)
     ys = plane_gather(*compact(reach[::2], y_got, cap), slots)

time: 166 us -> 161 us (0.970)
  local copies, waits for them, and re-layouts: 14.9 us -> 10.9 us
    unnamed x76 -> x58, local copies, waits for them, and re-layouts: 10.5 us -> 6.46 us
    ppermute x28, waiting for transfers between devices: 23.6 us -> 19.8 us  [flip(): return lax.ppermute(x, 'tensor', [(i, i ^ bit >> 1) for i in range(n)])]
    ppermute x2, starting transfers between devices: 4.93 us -> 1.79 us  [body(): lax.ppermute(x, 'plane', [(e, e ^ step) for e in range(planes)])]
    ppermute x28, starting transfers between devices: 11.6 us -> 14.2 us  [flip(): return lax.ppermute(x, 'tensor', [(i, i ^ bit >> 1) for i in range(n)])]
    ppermute x2, waiting for transfers between devices: 0.89 us -> 2.56 us  [body(): lax.ppermute(x, 'plane', [(e, e ^ step) for e in range(planes)])]
  transfers between devices with their start and end apart: 43 -> 43, of which waited for: 23 -> 23; matrix products, arithmetic and copies ran while one was open for 4% -> 4% of each run, Pallas kernels for 21% -> 22%
where the time goes in v5:
time: 161 us
  waiting for transfers between devices  59.2 us (37%)
  Pallas kernels  44.3 us (28%)
  starting transfers between devices  42.6 us (26%)
  local copies, waits for them, and re-layouts  10.9 us (7%)
  other arithmetic  2.4 us (1%)
    pallas_call x12, Pallas kernels, call(): pl.pallas_call(run, in_specs=[pl.BlockSpec(memory_space=pltpu.SMEM)] * le...  44.3 us
    ppermute x10, waiting for transfers between devices, flip(): return lax.ppermute(x, 'half', [(0, 1), (1, 0)])  27.2 us
    ppermute x28, waiting for transfers between devices, flip(): return lax.ppermute(x, 'tensor', [(i, i ^ bit >> 1) for i in range(n)])  19.8 us
    all_to_all x3, starting transfers between devices, exchange(): return lax.all_to_all(x, axes, split_axis=0, concat_axis=0, tiled=True)  15.1 us
    ppermute x28, starting transfers between devices, flip(): return lax.ppermute(x, 'tensor', [(i, i ^ bit >> 1) for i in range(n)])  14.2 us
    ppermute x10, starting transfers between devices, flip(): return lax.ppermute(x, 'half', [(0, 1), (1, 0)])  11.5 us
    all_to_all x3, waiting for transfers between devices, exchange(): return lax.all_to_all(x, axes, split_axis=0, concat_axis=0, tiled=True)  9.67 us
    unnamed x58, local copies, waits for them, and re-layouts  6.46 us
  transfers between devices with their start and end apart: 43, of which 23 were waited for; matrix products, arithmetic and copies ran while one was open for 4% of the time, Pallas kernels for 22%

profile of v5, /device:TPU:0, one launch (start us, length us, event | category | flops | bytes accessed | tf_op | source)
XLA Modules:
  0.0 160.5 jit_solution(12730122521367116642)
XLA Ops:
  3.0 2.4 %pack_rows.2 = (bf16[8,128,512]{2,1,0:T(8,128)(2,1)}, bf16[4,256,128]{2,1,0:T(8,128)(2,1)}) custom-call(s32[2]{0:T(128)S(1)} %pad_add_fusion.refs_0_, s32[4,512]{1,0:T(4,128)S(1)} %copy-done.19, bf16[256,1024]{1,0:T(8,128)(2,1)S(1)} %constant_dynamic-slice_fusion.5.refs_2_), custom_call_target="tpu_custom_call" | custom-call | flops 268435456 | bytes 3153928 | tf_op jit(solution)/shard_map/pack_rows/pallas_call | solution.py:93
  5.4 7.3 %all-to-all-start = ((bf16[8,128,512]{2,1,0:T(8,128)(2,1)}), bf16[8,128,512]{2,1,0:T(8,128)(2,1)S(1)}, u32[]{:S(2)}, u32[]{:S(2)}) async-start(bf16[8,128,512]{2,1,0:T(8,128)(2,1)} %get-tuple-element.64), calls=%async_computation | async-start | bytes 2097152 | tf_op jit(solution)/shard_map/all_to_all | solution.py:394
  16.5 2.2 %constant_dynamic-slice_fusion = (bf16[512,512]{1,0:T(8,128)(2,1)}, bf16[512,512]{1,0:T(8,128)(2,1)}) fusion(bf16[512,4096]{1,0:T(8,128)(2,1)} %refs_13_, s32[]{:T(128)S(6)} %select_n.34, s32[]{:T(128)S(6)} %select_n.33), kind=kLoop, calls=%fused_computation.11 | loop fusion | bytes 2097160 | tf_op jit(solution)/shard_map/dynamic_slice | solution.py:391
  18.7 11.9 %collective-permute-done.refs_3_ = bf16[256,512]{1,0:T(8,128)(2,1)} collective-permute-done((bf16[256,512]{1,0:T(8,128)(2,1)}, bf16[256,512]{1,0:T(8,128)(2,1)}, u32[]{:S(2)}, u32[]{:S(2)}) %collective-permute-start) | collective-permute-done | bytes 262176 | tf_op jit(solution)/shard_map/ppermute | solution.py:24
  30.6 3.2 %pack_rows.3 = (bf16[4,256,512]{2,1,0:T(8,128)(2,1)}, bf16[4,256,256]{2,1,0:T(8,128)(2,1)}) custom-call(s32[3]{0:T(128)S(1)} %pad_add_fusion.1.refs_0_, s32[4,512]{1,0:T(4,128)S(1)} %copy-done.20, bf16[256,512]{1,0:T(8,128)(2,1)S(1)} %get-tuple-element.128.refs_2_, bf16[256,512]{1,0:T(8,128)(2,1)} %collective-permute-done.refs_3_), custom_call_target="tpu_custom_call" | custom-call | flops 536870912 | bytes 3678220 | tf_op jit(solution)/shard_map/pack_rows/pallas_call | solution.py:93
  33.8 4.6 %all-to-all-done.refs_1_ = bf16[8,128,512]{2,1,0:T(8,128)(2,1)S(1)} async-done(((bf16[8,128,512]{2,1,0:T(8,128)(2,1)}), bf16[8,128,512]{2,1,0:T(8,128)(2,1)S(1)}, u32[]{:S(2)}, u32[]{:S(2)}) %all-to-all-start) | async-done | bytes 1048608 | tf_op jit(solution)/shard_map/all_to_all | solution.py:394
  38.4 4.2 %all-to-all-start.1 = ((bf16[4,256,512]{2,1,0:T(8,128)(2,1)}), bf16[4,256,512]{2,1,0:T(8,128)(2,1)}, u32[]{:S(2)}, u32[]{:S(2)}) async-start(bf16[4,256,512]{2,1,0:T(8,128)(2,1)} %get-tuple-element.68), calls=%async_computation.1 | async-start | bytes 2097152 | tf_op jit(solution)/shard_map/all_to_all | solution.py:394
  49.5 3.1 %collective-permute-done.3.refs_6_.refs_5_ = bf16[256,512]{1,0:T(8,128)(2,1)S(1)} collective-permute-done((bf16[256,512]{1,0:T(8,128)(2,1)S(1)}, bf16[256,512]{1,0:T(8,128)(2,1)S(1)}, u32[]{:S(2)}, u32[]{:S(2)}) %collective-permute-start.3) | collective-permute-done | bytes 262176 | tf_op jit(solution)/shard_map/ppermute | solution.py:26
  58.7 3.6 %collective-permute-done.1.refs_4_.refs_3_ = bf16[256,512]{1,0:T(8,128)(2,1)S(1)} collective-permute-done((bf16[256,512]{1,0:T(8,128)(2,1)S(1)}, bf16[256,512]{1,0:T(8,128)(2,1)S(1)}, u32[]{:S(2)}, u32[]{:S(2)}) %collective-permute-start.1) | collective-permute-done | bytes 262176 | tf_op jit(solution)/shard_map/ppermute | solution.py:24
  62.3 3.1 %collective-permute-done.16.refs_14_.refs_13_ = bf16[256,512]{1,0:T(8,128)(2,1)} collective-permute-done((bf16[256,512]{1,0:T(8,128)(2,1)S(1)}, bf16[256,512]{1,0:T(8,128)(2,1)}, u32[]{:S(2)}, u32[]{:S(2)}) %collective-permute-start.16) | collective-permute-done | bytes 262176 | tf_op jit(solution)/shard_map/ppermute | solution.py:24
  70.5 2.1 %collective-permute-start.7 = (bf16[256,512]{1,0:T(8,128)(2,1)S(1)}, bf16[256,512]{1,0:T(8,128)(2,1)S(1)}, u32[]{:S(2)}, u32[]{:S(2)}) collective-permute-start(bf16[256,512]{1,0:T(8,128)(2,1)S(1)} %get-tuple-element.80.refs_1_), channel_id=1, source_target_pairs={{0,4},{4,0},{1,5},{5,1},{2,6},{6,2},{3,7},{7,3},{8,12},{12,8},{9,1... | collective-permute-start | bytes 786440 | tf_op jit(solution)/shard_map/ppermute | solution.py:24
  74.8 7.0 %project_in.1 = (f32[512,512]{1,0:T(8,128)S(1)}, f32[512,1]{1,0:T(8,128)S(1)}) custom-call(s32[8]{0:T(128)S(1)} %stack.79.refs_0_, s32[1]{0:T(128)} %bitcast.12.refs_1_, bf16[256,512]{1,0:T(8,128)(2,1)} %copy-done.3, bf16[256,512]{1,0:T(8,128)(2,1)} %copy-done.4, bf16[256,512]{1,0:T(8,128)(2,1)} %copy-done.25, bf16[256,512]{1,0:T(8,128)(2,1)} %copy-done.24, ...), custom_call_target="tpu_custom_call" | custom-call | flops 2147483648 | bytes 9472036 | tf_op jit(solution)/shard_map/project_in/pallas_call | solution.py:93
  83.3 3.0 %collective-permute-done.9.refs_6_ = bf16[256,512]{1,0:T(8,128)(2,1)} collective-permute-done((bf16[256,512]{1,0:T(8,128)(2,1)S(1)}, bf16[256,512]{1,0:T(8,128)(2,1)}, u32[]{:S(2)}, u32[]{:S(2)}) %collective-permute-start.9) | collective-permute-done | bytes 262176 | tf_op jit(solution)/shard_map/ppermute | solution.py:26
  89.5 5.1 %project_out.1.refs_9_ = f32[512,512]{1,0:T(8,128)S(1)} custom-call(s32[6]{0:T(128)S(1)} %stack.78.refs_0_, bf16[256,512]{1,0:T(8,128)(2,1)} %copy-done.5, bf16[256,512]{1,0:T(8,128)(2,1)} %copy-done.6, bf16[256,512]{1,0:T(8,128)(2,1)} %copy-done.26, bf16[256,512]{1,0:T(8,128)(2,1)} %collective-permute-done.8.refs_4_, ...), custom_call_target="tpu_custom_call" | custom-call | flops 1610612736 | bytes 8388632 | tf_op jit(solution)/shard_map/project_out/pallas_call | solution.py:93
  99.1 3.9 %activation.1 = (bf16[512,512]{1,0:T(8,128)(2,1)S(1)}, bf16[512,512]{1,0:T(8,128)(2,1)S(1)}, f32[512,1]{1,0:T(8,128)S(1)}, bf16[1,512,512]{2,1,0:T(8,128)(2,1)S(...) custom-call(s32[8]{0:T(128)S(1)} %stack.74.refs_0_, ...), custom_call_target="tpu_custom_call" | custom-call | flops 2684354560 | bytes 18894880 | tf_op jit(solution)/shard_map/activation/pallas_call | solution.py:93
  106.7 3.1 %router_column.1 = f32[1,4096]{1,0:T(1,128)S(1)} custom-call(s32[8]{0:T(128)S(1)} %stack.79.refs_0_, bf16[256,512]{1,0:T(8,128)(2,1)} %copy-done.3, bf16[256,512]{1,0:T(8,128)(2,1)} %copy-done.4, bf16[256,512]{1,0:T(8,128)(2,1)} %copy-done.25, bf16[256,512]{1,0:T(8,128)(2,1)} %copy-done.24, bf16[256,512]{1,0:T(8,128)(2,1)} %copy-done.23, ...), custom_call_target="tpu_custom_call" | custom-call | flops 4194304 | bytes 4212768 | tf_op jit(solution)/shard_map/router_column/pallas_call | solution.py:93
  110.5 3.4 %collective-permute-done.31 = bf16[256,512]{1,0:T(8,128)(2,1)S(1)} collective-permute-done((bf16[256,512]{1,0:T(8,128)(2,1)S(1)}, bf16[256,512]{1,0:T(8,128)(2,1)S(1)}, u32[]{:S(2)}, u32[]{:S(2)}) %collective-permute-start.31) | collective-permute-done | bytes 262176 | tf_op jit(solution)/shard_map/ppermute | solution.py:26
  116.7 2.6 %collective-permute-done.35 = f32[4,4096]{1,0:T(4,128)S(1)} collective-permute-done((f32[4,4096]{1,0:T(4,128)S(1)}, f32[4,4096]{1,0:T(4,128)S(1)}, u32[]{:S(2)}, u32[]{:S(2)}) %collective-permute-start.35) | collective-permute-done | bytes 65568 | tf_op jit(solution)/shard_map/ppermute | solution.py:449
  120.7 6.5 %grads_in.1 = bf16[4096,512]{1,0:T(8,128)(2,1)} custom-call(s32[8]{0:T(128)S(1)} %stack.79.refs_0_, bf16[256,512]{1,0:T(8,128)(2,1)} %copy-done.3, bf16[256,512]{1,0:T(8,128)(2,1)} %copy-done.4, bf16[256,512]{1,0:T(8,128)(2,1)} %copy-done.25, bf16[256,512]{1,0:T(8,128)(2,1)} %copy-done.24, bf16[256,512]{1,0:T(8,128)(2,1)} %copy-done.23, ...), custom_call_target="tpu_custom_call" | custom-call | flops 2147483648 | bytes 13107232 | tf_op jit(solution)/shard_map/grads_in/pallas_call | solution.py:93
  131.3 3.6 %all-to-all-start.2 = ((bf16[8,128,512]{2,1,0:T(8,128)(2,1)}), bf16[8,128,512]{2,1,0:T(8,128)(2,1)S(1)}, u32[]{:S(2)}, u32[]{:S(2)}) async-start(bf16[8,128,512]{2,1,0:T(8,128)(2,1)} %copy-done.2), calls=%async_computation.2 | async-start | bytes 2097152 | tf_op jit(solution)/shard_map/all_to_all | solution.py:394
  135.9 6.6 %grads_out.1 = bf16[512,4096]{1,0:T(8,128)(2,1)} custom-call(s32[8]{0:T(128)S(1)} %stack.79.refs_0_, bf16[256,512]{1,0:T(8,128)(2,1)} %copy-done.5, bf16[256,512]{1,0:T(8,128)(2,1)} %copy-done.6, bf16[256,512]{1,0:T(8,128)(2,1)} %copy-done.26, bf16[256,512]{1,0:T(8,128)(2,1)} %collective-permute-done.8.refs_4_, ...), custom_call_target="tpu_custom_call" | custom-call | flops 2147483648 | bytes 13107232 | tf_op jit(solution)/shard_map/grads_out/pallas_call | solution.py:93
  143.5 3.2 %collective-permute-done.37 = f32[4,4096]{1,0:T(4,128)S(1)} collective-permute-done((f32[4,4096]{1,0:T(4,128)S(1)}, f32[4,4096]{1,0:T(4,128)S(1)}, u32[]{:S(2)}, u32[]{:S(2)}) %collective-permute-start.37) | collective-permute-done | bytes 65568 | tf_op jit(solution)/shard_map/ppermute | solution.py:26
  150.2 3.8 %collective-permute-done.39 = f32[4,4096]{1,0:T(4,128)S(1)} collective-permute-done((f32[4,4096]{1,0:T(4,128)S(1)}, f32[4,4096]{1,0:T(4,128)S(1)}, u32[]{:S(2)}, u32[]{:S(2)}) %collective-permute-start.39) | collective-permute-done | bytes 65568 | tf_op jit(solution)/shard_map/ppermute | solution.py:24
  154.6 4.4 %all-to-all-done.2.refs_1_ = bf16[8,128,512]{2,1,0:T(8,128)(2,1)S(1)} async-done(((bf16[8,128,512]{2,1,0:T(8,128)(2,1)}), bf16[8,128,512]{2,1,0:T(8,128)(2,1)S(1)}, u32[]{:S(2)}, u32[]{:S(2)}) %all-to-all-start.2) | async-done | bytes 1048608 | tf_op jit(solution)/shard_map/all_to_all | solution.py:394
  (156 shorter events, 55.5 us)
Async XLA Ops:
  5.4 33.0 %all-to-all-start = ((bf16[8,128,512]{2,1,0:T(8,128)(2,1)}), bf16[8,128,512]{2,1,0:T(8,128)(2,1)S(1)}, u32[]{:S(2)}, u32[]{:S(2)}) async-start(bf16[8,128,512]{2,1,0:T(8,128)(2,1)} %get-tuple-element.64), calls=%async_computation | async-start | bytes 2097152 | tf_op jit(solution)/shard_map/all_to_all | solution.py:394
  14.4 16.2 %collective-permute-start = (bf16[256,512]{1,0:T(8,128)(2,1)}, bf16[256,512]{1,0:T(8,128)(2,1)}, u32[]{:S(2)}, u32[]{:S(2)}) collective-permute-start(bf16[256,512]{1,0:T(8,128)(2,1)} %get-tuple-element.127), channel_id=1, source_target_pairs={{0,4},{4,0},{1,5},{5,1},{2,6},{6,2},{3,7},{7,3},{8,12},{12,8},{9,1... | collective-permute-start | bytes 786440 | tf_op jit(solution)/shard_map/ppermute | solution.py:24
  38.4 28.9 %all-to-all-start.1 = ((bf16[4,256,512]{2,1,0:T(8,128)(2,1)}), bf16[4,256,512]{2,1,0:T(8,128)(2,1)}, u32[]{:S(2)}, u32[]{:S(2)}) async-start(bf16[4,256,512]{2,1,0:T(8,128)(2,1)} %get-tuple-element.68), calls=%async_computation.1 | async-start | bytes 2097152 | tf_op jit(solution)/shard_map/all_to_all | solution.py:394
  47.5 9.2 %collective-permute-start.2 = (bf16[256,512]{1,0:T(8,128)(2,1)S(1)}, bf16[256,512]{1,0:T(8,128)(2,1)S(1)}, u32[]{:S(2)}, u32[]{:S(2)}) collective-permute-start(bf16[256,512]{1,0:T(8,128)(2,1)S(1)} %get-tuple-element.71.refs_3_.refs_2_), channel_id=1, source_target_pairs={{0,4},{4,0},{1,5},{5,1},{2,6},{6,2},{3,7},{7,3},{8,12},{12,8},{9,1... | collective-permute-start | bytes 786440 | tf_op jit(solution)/shard_map/ppermute | solution.py:24
  48.9 13.4 %collective-permute-start.1 = (bf16[256,512]{1,0:T(8,128)(2,1)S(1)}, bf16[256,512]{1,0:T(8,128)(2,1)S(1)}, u32[]{:S(2)}, u32[]{:S(2)}) collective-permute-start(bf16[256,512]{1,0:T(8,128)(2,1)S(1)} %get-tuple-element.70.refs_2_.refs_1_), channel_id=1, source_target_pairs={{0,4},{4,0},{1,5},{5,1},{2,6},{6,2},{3,7},{7,3},{8,12},{12,8},{9,1... | collective-permute-start | bytes 786440 | tf_op jit(solution)/shard_map/ppermute | solution.py:24
  52.6 12.9 %collective-permute-start.16 = (bf16[256,512]{1,0:T(8,128)(2,1)S(1)}, bf16[256,512]{1,0:T(8,128)(2,1)}, u32[]{:S(2)}, u32[]{:S(2)}) collective-permute-start(bf16[256,512]{1,0:T(8,128)(2,1)S(1)} %collective-permute-done.3.refs_6_.refs_5_), channel_id=1, source_target_pairs={{0,4},{4,0},{1,5},{5,1},{2,6},{6,2},{3,7},{7,3},{8,12},{12,8},{9,1... | collective-permute-start | bytes 786440 | tf_op jit(solution)/shard_map/ppermute | solution.py:24
  56.7 8.8 %collective-permute-start.17 = (bf16[256,512]{1,0:T(8,128)(2,1)S(1)}, bf16[256,512]{1,0:T(8,128)(2,1)}, u32[]{:S(2)}, u32[]{:S(2)}) collective-permute-start(bf16[256,512]{1,0:T(8,128)(2,1)S(1)} %collective-permute-done.2.refs_5_.refs_4_), channel_id=1, source_target_pairs={{0,2},{1,3},{2,0},{3,1},{4,6},{5,7},{6,4},{7,5},{8,10},{9,11},{10,... | collective-permute-start | bytes 786440 | tf_op jit(solution)/shard_map/ppermute | solution.py:26
  57.2 9.3 %collective-permute-start.4 = (bf16[256,512]{1,0:T(8,128)(2,1)S(1)}, bf16[256,512]{1,0:T(8,128)(2,1)}, u32[]{:S(2)}, u32[]{:S(2)}) collective-permute-start(bf16[256,512]{1,0:T(8,128)(2,1)S(1)} %get-tuple-element.71.refs_3_.refs_2_), channel_id=1, source_target_pairs={{0,2},{1,3},{2,0},{3,1},{4,6},{5,7},{6,4},{7,5},{8,10},{9,11},{10,... | collective-permute-start | bytes 786440 | tf_op jit(solution)/shard_map/ppermute | solution.py:26
  58.7 8.5 %collective-permute-start.10 = (bf16[256,512]{1,0:T(8,128)(2,1)S(1)}, bf16[256,512]{1,0:T(8,128)(2,1)}, u32[]{:S(2)}, u32[]{:S(2)}) collective-permute-start(bf16[256,512]{1,0:T(8,128)(2,1)S(1)} %get-tuple-element.70.refs_2_.refs_1_), channel_id=1, source_target_pairs={{0,1},{1,0},{2,3},{3,2},{4,5},{5,4},{6,7},{7,6},{8,9},{9,8},{10,11... | collective-permute-start | bytes 786440 | tf_op jit(solution)/shard_map/ppermute | solution.py:26
  67.3 6.9 %collective-permute-start.13 = (bf16[256,512]{1,0:T(8,128)(2,1)S(1)}, bf16[256,512]{1,0:T(8,128)(2,1)}, u32[]{:S(2)}, u32[]{:S(2)}) collective-permute-start(bf16[256,512]{1,0:T(8,128)(2,1)S(1)} %collective-permute-done.2.refs_5_.refs_4_), channel_id=1, source_target_pairs={{0,1},{1,0},{2,3},{3,2},{4,5},{5,4},{6,7},{7,6},{8,9},{9,8},{10,11... | collective-permute-start | bytes 786440 | tf_op jit(solution)/shard_map/ppermute | solution.py:26
  67.8 6.9 %collective-permute-start.14 = (bf16[256,512]{1,0:T(8,128)(2,1)S(1)}, bf16[256,512]{1,0:T(8,128)(2,1)}, u32[]{:S(2)}, u32[]{:S(2)}) collective-permute-start(bf16[256,512]{1,0:T(8,128)(2,1)S(1)} %collective-permute-done.3.refs_6_.refs_5_), channel_id=1, source_target_pairs={{0,1},{1,0},{2,3},{3,2},{4,5},{5,4},{6,7},{7,6},{8,9},{9,8},{10,11... | collective-permute-start | bytes 786440 | tf_op jit(solution)/shard_map/ppermute | solution.py:26
  67.9 6.9 %collective-permute-start.15 = (bf16[256,512]{1,0:T(8,128)(2,1)}, bf16[256,512]{1,0:T(8,128)(2,1)}, u32[]{:S(2)}, u32[]{:S(2)}) collective-permute-start(bf16[256,512]{1,0:T(8,128)(2,1)} %collective-permute-done.4.refs_7_.refs_6_), channel_id=1, source_target_pairs={{0,1},{1,0},{2,3},{3,2},{4,5},{5,4},{6,7},{7,6},{8,9},{9,8},{10,11... | collective-permute-start | bytes 786440 | tf_op jit(solution)/shard_map/ppermute | solution.py:26
  70.5 12.3 %collective-permute-start.7 = (bf16[256,512]{1,0:T(8,128)(2,1)S(1)}, bf16[256,512]{1,0:T(8,128)(2,1)S(1)}, u32[]{:S(2)}, u32[]{:S(2)}) collective-permute-start(bf16[256,512]{1,0:T(8,128)(2,1)S(1)} %get-tuple-element.80.refs_1_), channel_id=1, source_target_pairs={{0,4},{4,0},{1,5},{5,1},{2,6},{6,2},{3,7},{7,3},{8,12},{12,8},{9,1... | collective-permute-start | bytes 786440 | tf_op jit(solution)/shard_map/ppermute | solution.py:24
  72.6 13.7 %collective-permute-start.5 = (bf16[256,512]{1,0:T(8,128)(2,1)S(1)}, bf16[256,512]{1,0:T(8,128)(2,1)}, u32[]{:S(2)}, u32[]{:S(2)}) collective-permute-start(bf16[256,512]{1,0:T(8,128)(2,1)S(1)} %get-tuple-element.80.refs_1_), channel_id=1, source_target_pairs={{0,2},{1,3},{2,0},{3,1},{4,6},{5,7},{6,4},{7,5},{8,10},{9,11},{10,... | collective-permute-start | bytes 786440 | tf_op jit(solution)/shard_map/ppermute | solution.py:26
  74.1 12.2 %collective-permute-start.9 = (bf16[256,512]{1,0:T(8,128)(2,1)S(1)}, bf16[256,512]{1,0:T(8,128)(2,1)}, u32[]{:S(2)}, u32[]{:S(2)}) collective-permute-start(bf16[256,512]{1,0:T(8,128)(2,1)S(1)} %get-tuple-element.81.refs_2_), channel_id=1, source_target_pairs={{0,2},{1,3},{2,0},{3,1},{4,6},{5,7},{6,4},{7,5},{8,10},{9,11},{10,... | collective-permute-start | bytes 786440 | tf_op jit(solution)/shard_map/ppermute | solution.py:26
  74.6 11.7 %collective-permute-start.8 = (bf16[256,512]{1,0:T(8,128)(2,1)S(1)}, bf16[256,512]{1,0:T(8,128)(2,1)}, u32[]{:S(2)}, u32[]{:S(2)}) collective-permute-start(bf16[256,512]{1,0:T(8,128)(2,1)S(1)} %get-tuple-element.81.refs_2_), channel_id=1, source_target_pairs={{0,4},{4,0},{1,5},{5,1},{2,6},{6,2},{3,7},{7,3},{8,12},{12,8},{9,1... | collective-permute-start | bytes 786440 | tf_op jit(solution)/shard_map/ppermute | solution.py:24
  87.4 8.5 %collective-permute-start.26 = (bf16[256,512]{1,0:T(8,128)(2,1)}, bf16[256,512]{1,0:T(8,128)(2,1)S(1)}, u32[]{:S(2)}, u32[]{:S(2)}) collective-permute-start(bf16[256,512]{1,0:T(8,128)(2,1)} %collective-permute-done.8.refs_4_), channel_id=1, source_target_pairs={{0,2},{1,3},{2,0},{3,1},{4,6},{5,7},{6,4},{7,5},{8,10},{9,11},{10,... | collective-permute-start | bytes 786440 | tf_op jit(solution)/shard_map/ppermute | solution.py:26
  88.9 8.2 %collective-permute-start.6 = (bf16[256,512]{1,0:T(8,128)(2,1)}, bf16[256,512]{1,0:T(8,128)(2,1)S(1)}, u32[]{:S(2)}, u32[]{:S(2)}) collective-permute-start(bf16[256,512]{1,0:T(8,128)(2,1)} %collective-permute-done.5.refs_5_), channel_id=1, source_target_pairs={{0,4},{4,0},{1,5},{5,1},{2,6},{6,2},{3,7},{7,3},{8,12},{12,8},{9,1... | collective-permute-start | bytes 786440 | tf_op jit(solution)/shard_map/ppermute | solution.py:24
  105.3 8.6 %collective-permute-start.31 = (bf16[256,512]{1,0:T(8,128)(2,1)S(1)}, bf16[256,512]{1,0:T(8,128)(2,1)S(1)}, u32[]{:S(2)}, u32[]{:S(2)}) collective-permute-start(bf16[256,512]{1,0:T(8,128)(2,1)S(1)} %get-tuple-element.129), channel_id=1, source_target_pairs={{0,2},{1,3},{2,0},{3,1},{4,6},{5,7},{6,4},{7,5},{8,10},{9,11},{10,... | collective-permute-start | bytes 786440 | tf_op jit(solution)/shard_map/ppermute | solution.py:26
  106.3 8.3 %collective-permute-start.30 = (bf16[256,512]{1,0:T(8,128)(2,1)S(1)}, bf16[256,512]{1,0:T(8,128)(2,1)S(1)}, u32[]{:S(2)}, u32[]{:S(2)}) collective-permute-start(bf16[256,512]{1,0:T(8,128)(2,1)S(1)} %get-tuple-element.130), channel_id=1, source_target_pairs={{0,4},{4,0},{1,5},{5,1},{2,6},{6,2},{3,7},{7,3},{8,12},{12,8},{9,1... | collective-permute-start | bytes 786440 | tf_op jit(solution)/shard_map/ppermute | solution.py:24
  115.4 12.8 %collective-permute-start.33 = (bf16[512,512]{1,0:T(8,128)(2,1)S(1)}, bf16[512,512]{1,0:T(8,128)(2,1)S(1)}, u32[]{:S(2)}, u32[]{:S(2)}) collective-permute-start(bf16[512,512]{1,0:T(8,128)(2,1)S(1)} %get-tuple-element.107), channel_id=1, source_target_pairs={{0,2},{1,3},{2,0},{3,1},{4,6},{5,7},{6,4},{7,5},{8,10},{9,11},{10,... | collective-permute-start | bytes 1572872 | tf_op jit(solution)/shard_map/ppermute | solution.py:26
  116.4 12.6 %collective-permute-start.34 = (bf16[512,512]{1,0:T(8,128)(2,1)S(1)}, bf16[512,512]{1,0:T(8,128)(2,1)S(1)}, u32[]{:S(2)}, u32[]{:S(2)}) collective-permute-start(bf16[512,512]{1,0:T(8,128)(2,1)S(1)} %get-tuple-element.108), channel_id=1, source_target_pairs={{0,4},{4,0},{1,5},{5,1},{2,6},{6,2},{3,7},{7,3},{8,12},{12,8},{9,1... | collective-permute-start | bytes 1572872 | tf_op jit(solution)/shard_map/ppermute | solution.py:24
  119.4 7.9 %collective-permute-start.36 = (f32[4,4096]{1,0:T(4,128)S(1)}, f32[4,4096]{1,0:T(4,128)S(1)}, u32[]{:S(2)}, u32[]{:S(2)}) collective-permute-start(f32[4,4096]{1,0:T(4,128)S(1)} %fusion), channel_id=1, source_target_pairs={{0,16},{8,24},{16,0},{24,8},{1,17},{9,25},{17,1},{25,9},{2,18},{10... | collective-permute-start | bytes 196616 | tf_op jit(solution)/shard_map/ppermute | solution.py:449
  131.3 27.7 %all-to-all-start.2 = ((bf16[8,128,512]{2,1,0:T(8,128)(2,1)}), bf16[8,128,512]{2,1,0:T(8,128)(2,1)S(1)}, u32[]{:S(2)}, u32[]{:S(2)}) async-start(bf16[8,128,512]{2,1,0:T(8,128)(2,1)} %copy-done.2), calls=%async_computation.2 | async-start | bytes 2097152 | tf_op jit(solution)/shard_map/all_to_all | solution.py:394
  (48 other events, 385.3 us)

commit v6 on v5

--- a/solution.py
+++ b/solution.py
@@ -173,7 +173,7 @@
             refs[-1][s] = dot(hot.astype(F32).astype(BF), rows, 1, 0).astype(BF)
 
     flops = 2 * cap * homes * bucket * width
-    outs = [shaped(homes, bucket, width, dtype=BF)]
+    outs = [pltpu.HBM((homes, bucket, width), BF)]
     return call(kernel, "place_rows", flops, outs, [reach], *terms)[0]
 
 
@@ -421,7 +421,7 @@
 
     pre_act, gate = project_in(order, expert, xs, keys, w_in, router.T)
     ys = plane_gather(*compact(reach[::2], y_got, cap), slots)
-    tied = {m: [(at, after(x, pre_act)) for at, x in ys[m]] for m in early}
+    tied = {m: [(at, after(x, pre_act)) if m else (at, x) for at, x in ys[m]] for m in early}
     add_core(tied, early)
     ys.update({m: tied[m] for m in tied if m & CORE})
     upstream = project_out(order_of(*early_keys), ys, early_keys, w_out)
@@ -470,7 +470,7 @@
         sums[m ^ low] = sums[m ^ low] + jnp.concatenate([a.astype(F32), pad])
         sums[m ^ high] = sums[m ^ high] + jnp.concatenate([pad, b.astype(F32)])
     sent = [sums[m].astype(BF) for m in groups[1] if m]
-    *sent, column, pre_grad = join(*sent, column, pre_grad)
+    *sent, pre_grad = join(*sent, pre_grad)
     came = [flip(x, m) for x, m in zip(sent, groups[1])]
     total = jnp.where(jnp.arange(planes)[:, None] == plane, column, 0.0)
     total = hop(total)

time: 161 us -> 161 us (level)
    unnamed x58 -> x54, local copies, waits for them, and re-layouts: 6.46 us -> 5.79 us
where the time goes in v6:
time: 161 us
  waiting for transfers between devices  59.5 us (37%)
  Pallas kernels  45.3 us (28%)
  starting transfers between devices  42.3 us (26%)
  local copies, waits for them, and re-layouts  10.2 us (6%)
  other arithmetic  2.4 us (1%)
    pallas_call x12, Pallas kernels, call(): pl.pallas_call(run, in_specs=[pl.BlockSpec(memory_space=pltpu.SMEM)] * le...  45.3 us
    ppermute x10, waiting for transfers between devices, flip(): return lax.ppermute(x, 'half', [(0, 1), (1, 0)])  27 us
    ppermute x28, waiting for transfers between devices, flip(): return lax.ppermute(x, 'tensor', [(i, i ^ bit >> 1) for i in range(n)])  21.2 us
    all_to_all x3, starting transfers between devices, exchange(): return lax.all_to_all(x, axes, split_axis=0, concat_axis=0, tiled=True)  15.1 us
    ppermute x28, starting transfers between devices, flip(): return lax.ppermute(x, 'tensor', [(i, i ^ bit >> 1) for i in range(n)])  13.3 us
    ppermute x10, starting transfers between devices, flip(): return lax.ppermute(x, 'half', [(0, 1), (1, 0)])  12 us
    all_to_all x3, waiting for transfers between devices, exchange(): return lax.all_to_all(x, axes, split_axis=0, concat_axis=0, tiled=True)  9.58 us
    unnamed x54, local copies, waits for them, and re-layouts  5.79 us
  transfers between devices with their start and end apart: 43, of which 23 were waited for; matrix products, arithmetic and copies ran while one was open for 4% of the time, Pallas kernels for 22%

profile of v6, /device:TPU:0, one launch (start us, length us, event | category | flops | bytes accessed | tf_op | source)
XLA Modules:
  0.0 160.7 jit_solution(17019763185028566230)
XLA Ops:
  3.0 2.4 %pack_rows.2 = (bf16[8,128,512]{2,1,0:T(8,128)(2,1)}, bf16[4,256,128]{2,1,0:T(8,128)(2,1)}) custom-call(s32[2]{0:T(128)S(1)} %pad_add_fusion.refs_0_, s32[4,512]{1,0:T(4,128)S(1)} %copy-done.18, bf16[256,1024]{1,0:T(8,128)(2,1)S(1)} %constant_dynamic-slice_fusion.5.refs_2_), custom_call_target="tpu_custom_call" | custom-call | flops 268435456 | bytes 3153928 | tf_op jit(solution)/shard_map/pack_rows/pallas_call | solution.py:93
  5.4 7.3 %all-to-all-start = ((bf16[8,128,512]{2,1,0:T(8,128)(2,1)}), bf16[8,128,512]{2,1,0:T(8,128)(2,1)S(1)}, u32[]{:S(2)}, u32[]{:S(2)}) async-start(bf16[8,128,512]{2,1,0:T(8,128)(2,1)} %get-tuple-element.61), calls=%async_computation | async-start | bytes 2097152 | tf_op jit(solution)/shard_map/all_to_all | solution.py:394
  16.5 2.2 %constant_dynamic-slice_fusion = (bf16[512,512]{1,0:T(8,128)(2,1)}, bf16[512,512]{1,0:T(8,128)(2,1)}) fusion(bf16[512,4096]{1,0:T(8,128)(2,1)} %refs_13_, s32[]{:T(128)S(6)} %select_n.34, s32[]{:T(128)S(6)} %select_n.33), kind=kLoop, calls=%fused_computation.11 | loop fusion | bytes 2097160 | tf_op jit(solution)/shard_map/dynamic_slice | solution.py:391
  18.7 11.9 %collective-permute-done.refs_3_ = bf16[256,512]{1,0:T(8,128)(2,1)} collective-permute-done((bf16[256,512]{1,0:T(8,128)(2,1)}, bf16[256,512]{1,0:T(8,128)(2,1)}, u32[]{:S(2)}, u32[]{:S(2)}) %collective-permute-start) | collective-permute-done | bytes 262176 | tf_op jit(solution)/shard_map/ppermute | solution.py:24
  30.6 3.2 %pack_rows.3 = (bf16[4,256,512]{2,1,0:T(8,128)(2,1)}, bf16[4,256,256]{2,1,0:T(8,128)(2,1)}) custom-call(s32[3]{0:T(128)S(1)} %pad_add_fusion.1.refs_0_, s32[4,512]{1,0:T(4,128)S(1)} %copy-done.19, bf16[256,512]{1,0:T(8,128)(2,1)S(1)} %get-tuple-element.122.refs_2_, bf16[256,512]{1,0:T(8,128)(2,1)} %collective-permute-done.refs_3_), custom_call_target="tpu_custom_call" | custom-call | flops 536870912 | bytes 3678220 | tf_op jit(solution)/shard_map/pack_rows/pallas_call | solution.py:93
  33.8 4.6 %all-to-all-done.refs_1_ = bf16[8,128,512]{2,1,0:T(8,128)(2,1)S(1)} async-done(((bf16[8,128,512]{2,1,0:T(8,128)(2,1)}), bf16[8,128,512]{2,1,0:T(8,128)(2,1)S(1)}, u32[]{:S(2)}, u32[]{:S(2)}) %all-to-all-start) | async-done | bytes 1048608 | tf_op jit(solution)/shard_map/all_to_all | solution.py:394
  38.4 4.2 %all-to-all-start.1 = ((bf16[4,256,512]{2,1,0:T(8,128)(2,1)}), bf16[4,256,512]{2,1,0:T(8,128)(2,1)}, u32[]{:S(2)}, u32[]{:S(2)}) async-start(bf16[4,256,512]{2,1,0:T(8,128)(2,1)} %get-tuple-element.65), calls=%async_computation.1 | async-start | bytes 2097152 | tf_op jit(solution)/shard_map/all_to_all | solution.py:394
  49.5 3.1 %collective-permute-done.3.refs_6_.refs_5_ = bf16[256,512]{1,0:T(8,128)(2,1)S(1)} collective-permute-done((bf16[256,512]{1,0:T(8,128)(2,1)S(1)}, bf16[256,512]{1,0:T(8,128)(2,1)S(1)}, u32[]{:S(2)}, u32[]{:S(2)}) %collective-permute-start.3) | collective-permute-done | bytes 262176 | tf_op jit(solution)/shard_map/ppermute | solution.py:26
  54.6 2.2 %collective-permute-done.2.refs_5_.refs_4_ = bf16[256,512]{1,0:T(8,128)(2,1)} collective-permute-done((bf16[256,512]{1,0:T(8,128)(2,1)S(1)}, bf16[256,512]{1,0:T(8,128)(2,1)}, u32[]{:S(2)}, u32[]{:S(2)}) %collective-permute-start.2) | collective-permute-done | bytes 262176 | tf_op jit(solution)/shard_map/ppermute | solution.py:24
  58.8 3.6 %collective-permute-done.1.refs_4_.refs_3_ = bf16[256,512]{1,0:T(8,128)(2,1)} collective-permute-done((bf16[256,512]{1,0:T(8,128)(2,1)S(1)}, bf16[256,512]{1,0:T(8,128)(2,1)}, u32[]{:S(2)}, u32[]{:S(2)}) %collective-permute-start.1) | collective-permute-done | bytes 262176 | tf_op jit(solution)/shard_map/ppermute | solution.py:24
  62.4 2.9 %collective-permute-done.18.refs_14_.refs_13_ = bf16[256,512]{1,0:T(8,128)(2,1)S(1)} collective-permute-done((bf16[256,512]{1,0:T(8,128)(2,1)S(1)}, bf16[256,512]{1,0:T(8,128)(2,1)S(1)}, u32[]{:S(2)}, u32[]{:S(2)}) %collective-permute-start.18) | collective-permute-done | bytes 262176 | tf_op jit(solution)/shard_map/ppermute | solution.py:24
  74.9 7.0 %project_in.1 = (f32[512,512]{1,0:T(8,128)S(1)}, f32[512,1]{1,0:T(8,128)S(1)}) custom-call(s32[8]{0:T(128)S(1)} %stack.79.refs_0_, s32[1]{0:T(128)} %bitcast.12.refs_1_, bf16[256,512]{1,0:T(8,128)(2,1)} %copy-done.2, bf16[256,512]{1,0:T(8,128)(2,1)} %copy-done.3, bf16[256,512]{1,0:T(8,128)(2,1)} %collective-permute-done.1.refs_4_.refs_3_, ...), custom_call_target="tpu_custom_call" | custom-call | flops 2147483648 | bytes 9472036 | tf_op jit(solution)/shard_map/project_in/pallas_call | solution.py:93
  83.4 3.0 %collective-permute-done.5.refs_5_ = bf16[256,512]{1,0:T(8,128)(2,1)} collective-permute-done((bf16[256,512]{1,0:T(8,128)(2,1)S(1)}, bf16[256,512]{1,0:T(8,128)(2,1)}, u32[]{:S(2)}, u32[]{:S(2)}) %collective-permute-start.5) | collective-permute-done | bytes 262176 | tf_op jit(solution)/shard_map/ppermute | solution.py:26
  89.4 5.1 %project_out.1.refs_9_ = f32[512,512]{1,0:T(8,128)S(1)} custom-call(s32[6]{0:T(128)S(1)} %stack.78.refs_0_, bf16[256,512]{1,0:T(8,128)(2,1)} %copy-done.4, bf16[256,512]{1,0:T(8,128)(2,1)} %copy-done.5, bf16[256,512]{1,0:T(8,128)(2,1)} %collective-permute-done.7.refs_3_, bf16[256,512]{1,0:T(8,128)(2,1)} %collective-permute-done.8.refs_4_, ...), custom_call_target="tpu_custom_call" | custom-call | flops 1610612736 | bytes 8388632 | tf_op jit(solution)/shard_map/project_out/pallas_call | solution.py:93
  99.1 3.9 %activation.1 = (bf16[512,512]{1,0:T(8,128)(2,1)S(1)}, bf16[512,512]{1,0:T(8,128)(2,1)S(1)}, f32[512,1]{1,0:T(8,128)S(1)}, bf16[1,512,512]{2,1,0:T(8,128)(2,1)S(...) custom-call(s32[8]{0:T(128)S(1)} %stack.74.refs_0_, ...), custom_call_target="tpu_custom_call" | custom-call | flops 2684354560 | bytes 18894880 | tf_op jit(solution)/shard_map/activation/pallas_call | solution.py:93
  106.3 3.1 %router_column.1 = f32[1,4096]{1,0:T(1,128)S(1)} custom-call(s32[8]{0:T(128)S(1)} %stack.79.refs_0_, bf16[256,512]{1,0:T(8,128)(2,1)} %copy-done.2, bf16[256,512]{1,0:T(8,128)(2,1)} %copy-done.3, bf16[256,512]{1,0:T(8,128)(2,1)} %collective-permute-done.1.refs_4_.refs_3_, bf16[256,512]{1,0:T(8,128)(2,1)} %collective-permute-done.2.refs_5_.refs_4_, ...), custom_call_target="tpu_custom_call" | custom-call | flops 4194304 | bytes 4212768 | tf_op jit(solution)/shard_map/router_column/pallas_call | solution.py:93
  110.1 3.9 %collective-permute-done.31 = bf16[256,512]{1,0:T(8,128)(2,1)S(1)} collective-permute-done((bf16[256,512]{1,0:T(8,128)(2,1)S(1)}, bf16[256,512]{1,0:T(8,128)(2,1)S(1)}, u32[]{:S(2)}, u32[]{:S(2)}) %collective-permute-start.31) | collective-permute-done | bytes 262176 | tf_op jit(solution)/shard_map/ppermute | solution.py:26
  120.1 6.5 %grads_in.1 = bf16[4096,512]{1,0:T(8,128)(2,1)} custom-call(s32[8]{0:T(128)S(1)} %stack.79.refs_0_, bf16[256,512]{1,0:T(8,128)(2,1)} %copy-done.2, bf16[256,512]{1,0:T(8,128)(2,1)} %copy-done.3, bf16[256,512]{1,0:T(8,128)(2,1)} %collective-permute-done.1.refs_4_.refs_3_, bf16[256,512]{1,0:T(8,128)(2,1)} %collective-permute-done.2.refs_5_.refs_4_, ...), custom_call_target="tpu_custom_call" | custom-call | flops 2147483648 | bytes 13107232 | tf_op jit(solution)/shard_map/grads_in/pallas_call | solution.py:93
  129.0 2.3 %place_rows.1 = bf16[8,128,512]{2,1,0:T(8,128)(2,1)} custom-call(s32[8]{0:T(128)S(1)} %convert_reduce_fusion.refs_0_, f32[512,512]{1,0:T(8,128)S(1)} %get-tuple-element.105.refs_1_, bf16[512,512]{1,0:T(8,128)(2,1)S(1)} %collective-permute-done.33.refs_2_, bf16[512,512]{1,0:T(8,128)(2,1)S(1)} %collective-permute-done.34.refs_3_), custom_call_target="tpu_custom_call" | custom-call | flops 536870912 | bytes 4194336 | tf_op jit(solution)/shard_map/place_rows/pallas_call | solution.py:93
  131.3 3.6 %all-to-all-start.2 = ((bf16[8,128,512]{2,1,0:T(8,128)(2,1)}), bf16[8,128,512]{2,1,0:T(8,128)(2,1)S(1)}, u32[]{:S(2)}, u32[]{:S(2)}) async-start(bf16[8,128,512]{2,1,0:T(8,128)(2,1)} %place_rows.1), calls=%async_computation.2 | async-start | bytes 2097152 | tf_op jit(solution)/shard_map/all_to_all | solution.py:394
  135.9 6.6 %grads_out.1 = bf16[512,4096]{1,0:T(8,128)(2,1)} custom-call(s32[8]{0:T(128)S(1)} %stack.79.refs_0_, bf16[256,512]{1,0:T(8,128)(2,1)} %copy-done.4, bf16[256,512]{1,0:T(8,128)(2,1)} %copy-done.5, bf16[256,512]{1,0:T(8,128)(2,1)} %collective-permute-done.7.refs_3_, bf16[256,512]{1,0:T(8,128)(2,1)} %collective-permute-done.8.refs_4_, ...), custom_call_target="tpu_custom_call" | custom-call | flops 2147483648 | bytes 13107232 | tf_op jit(solution)/shard_map/grads_out/pallas_call | solution.py:93
  143.2 3.6 %collective-permute-done.37 = f32[4,4096]{1,0:T(4,128)S(1)} collective-permute-done((f32[4,4096]{1,0:T(4,128)S(1)}, f32[4,4096]{1,0:T(4,128)S(1)}, u32[]{:S(2)}, u32[]{:S(2)}) %collective-permute-start.37) | collective-permute-done | bytes 65568 | tf_op jit(solution)/shard_map/ppermute | solution.py:26
  150.2 3.8 %collective-permute-done.39 = f32[4,4096]{1,0:T(4,128)S(1)} collective-permute-done((f32[4,4096]{1,0:T(4,128)S(1)}, f32[4,4096]{1,0:T(4,128)S(1)}, u32[]{:S(2)}, u32[]{:S(2)}) %collective-permute-start.39) | collective-permute-done | bytes 65568 | tf_op jit(solution)/shard_map/ppermute | solution.py:24
  154.7 4.5 %all-to-all-done.2.refs_1_ = bf16[8,128,512]{2,1,0:T(8,128)(2,1)S(1)} async-done(((bf16[8,128,512]{2,1,0:T(8,128)(2,1)}), bf16[8,128,512]{2,1,0:T(8,128)(2,1)S(1)}, u32[]{:S(2)}, u32[]{:S(2)}) %all-to-all-start.2) | async-done | bytes 1048608 | tf_op jit(solution)/shard_map/all_to_all | solution.py:394
  (152 shorter events, 55.2 us)
Async XLA Ops:
  5.4 33.0 %all-to-all-start = ((bf16[8,128,512]{2,1,0:T(8,128)(2,1)}), bf16[8,128,512]{2,1,0:T(8,128)(2,1)S(1)}, u32[]{:S(2)}, u32[]{:S(2)}) async-start(bf16[8,128,512]{2,1,0:T(8,128)(2,1)} %get-tuple-element.61), calls=%async_computation | async-start | bytes 2097152 | tf_op jit(solution)/shard_map/all_to_all | solution.py:394
  14.4 16.2 %collective-permute-start = (bf16[256,512]{1,0:T(8,128)(2,1)}, bf16[256,512]{1,0:T(8,128)(2,1)}, u32[]{:S(2)}, u32[]{:S(2)}) collective-permute-start(bf16[256,512]{1,0:T(8,128)(2,1)} %get-tuple-element.121), channel_id=1, source_target_pairs={{0,4},{4,0},{1,5},{5,1},{2,6},{6,2},{3,7},{7,3},{8,12},{12,8},{9,1... | collective-permute-start | bytes 786440 | tf_op jit(solution)/shard_map/ppermute | solution.py:24
  38.4 28.9 %all-to-all-start.1 = ((bf16[4,256,512]{2,1,0:T(8,128)(2,1)}), bf16[4,256,512]{2,1,0:T(8,128)(2,1)}, u32[]{:S(2)}, u32[]{:S(2)}) async-start(bf16[4,256,512]{2,1,0:T(8,128)(2,1)} %get-tuple-element.65), calls=%async_computation.1 | async-start | bytes 2097152 | tf_op jit(solution)/shard_map/all_to_all | solution.py:394
  47.5 9.4 %collective-permute-start.2 = (bf16[256,512]{1,0:T(8,128)(2,1)S(1)}, bf16[256,512]{1,0:T(8,128)(2,1)}, u32[]{:S(2)}, u32[]{:S(2)}) collective-permute-start(bf16[256,512]{1,0:T(8,128)(2,1)S(1)} %get-tuple-element.68.refs_3_.refs_2_), channel_id=1, source_target_pairs={{0,4},{4,0},{1,5},{5,1},{2,6},{6,2},{3,7},{7,3},{8,12},{12,8},{9,1... | collective-permute-start | bytes 786440 | tf_op jit(solution)/shard_map/ppermute | solution.py:24
  48.9 13.5 %collective-permute-start.1 = (bf16[256,512]{1,0:T(8,128)(2,1)S(1)}, bf16[256,512]{1,0:T(8,128)(2,1)}, u32[]{:S(2)}, u32[]{:S(2)}) collective-permute-start(bf16[256,512]{1,0:T(8,128)(2,1)S(1)} %get-tuple-element.67.refs_2_.refs_1_), channel_id=1, source_target_pairs={{0,4},{4,0},{1,5},{5,1},{2,6},{6,2},{3,7},{7,3},{8,12},{12,8},{9,1... | collective-permute-start | bytes 786440 | tf_op jit(solution)/shard_map/ppermute | solution.py:24
  52.5 12.8 %collective-permute-start.18 = (bf16[256,512]{1,0:T(8,128)(2,1)S(1)}, bf16[256,512]{1,0:T(8,128)(2,1)S(1)}, u32[]{:S(2)}, u32[]{:S(2)}) collective-permute-start(bf16[256,512]{1,0:T(8,128)(2,1)S(1)} %collective-permute-done.3.refs_6_.refs_5_), channel_id=1, source_target_pairs={{0,4},{4,0},{1,5},{5,1},{2,6},{6,2},{3,7},{7,3},{8,12},{12,8},{9,1... | collective-permute-start | bytes 786440 | tf_op jit(solution)/shard_map/ppermute | solution.py:24
  56.8 8.6 %collective-permute-start.19 = (bf16[256,512]{1,0:T(8,128)(2,1)}, bf16[256,512]{1,0:T(8,128)(2,1)}, u32[]{:S(2)}, u32[]{:S(2)}) collective-permute-start(bf16[256,512]{1,0:T(8,128)(2,1)} %collective-permute-done.2.refs_5_.refs_4_), channel_id=1, source_target_pairs={{0,2},{1,3},{2,0},{3,1},{4,6},{5,7},{6,4},{7,5},{8,10},{9,11},{10,... | collective-permute-start | bytes 786440 | tf_op jit(solution)/shard_map/ppermute | solution.py:26
  57.3 9.4 %collective-permute-start.4 = (bf16[256,512]{1,0:T(8,128)(2,1)S(1)}, bf16[256,512]{1,0:T(8,128)(2,1)}, u32[]{:S(2)}, u32[]{:S(2)}) collective-permute-start(bf16[256,512]{1,0:T(8,128)(2,1)S(1)} %get-tuple-element.68.refs_3_.refs_2_), channel_id=1, source_target_pairs={{0,2},{1,3},{2,0},{3,1},{4,6},{5,7},{6,4},{7,5},{8,10},{9,11},{10,... | collective-permute-start | bytes 786440 | tf_op jit(solution)/shard_map/ppermute | solution.py:26
  58.8 8.4 %collective-permute-start.12 = (bf16[256,512]{1,0:T(8,128)(2,1)S(1)}, bf16[256,512]{1,0:T(8,128)(2,1)S(1)}, u32[]{:S(2)}, u32[]{:S(2)}) collective-permute-start(bf16[256,512]{1,0:T(8,128)(2,1)S(1)} %get-tuple-element.67.refs_2_.refs_1_), channel_id=1, source_target_pairs={{0,1},{1,0},{2,3},{3,2},{4,5},{5,4},{6,7},{7,6},{8,9},{9,8},{10,11... | collective-permute-start | bytes 786440 | tf_op jit(solution)/shard_map/ppermute | solution.py:26
  67.3 6.9 %collective-permute-start.15 = (bf16[256,512]{1,0:T(8,128)(2,1)}, bf16[256,512]{1,0:T(8,128)(2,1)}, u32[]{:S(2)}, u32[]{:S(2)}) collective-permute-start(bf16[256,512]{1,0:T(8,128)(2,1)} %collective-permute-done.2.refs_5_.refs_4_), channel_id=1, source_target_pairs={{0,1},{1,0},{2,3},{3,2},{4,5},{5,4},{6,7},{7,6},{8,9},{9,8},{10,11... | collective-permute-start | bytes 786440 | tf_op jit(solution)/shard_map/ppermute | solution.py:26
  67.9 6.9 %collective-permute-start.17 = (bf16[256,512]{1,0:T(8,128)(2,1)}, bf16[256,512]{1,0:T(8,128)(2,1)}, u32[]{:S(2)}, u32[]{:S(2)}) collective-permute-start(bf16[256,512]{1,0:T(8,128)(2,1)} %collective-permute-done.4.refs_7_.refs_6_), channel_id=1, source_target_pairs={{0,1},{1,0},{2,3},{3,2},{4,5},{5,4},{6,7},{7,6},{8,9},{9,8},{10,11... | collective-permute-start | bytes 786440 | tf_op jit(solution)/shard_map/ppermute | solution.py:26
  70.4 12.5 %collective-permute-start.7 = (bf16[256,512]{1,0:T(8,128)(2,1)S(1)}, bf16[256,512]{1,0:T(8,128)(2,1)}, u32[]{:S(2)}, u32[]{:S(2)}) collective-permute-start(bf16[256,512]{1,0:T(8,128)(2,1)S(1)} %get-tuple-element.70.refs_1_), channel_id=1, source_target_pairs={{0,4},{4,0},{1,5},{5,1},{2,6},{6,2},{3,7},{7,3},{8,12},{12,8},{9,1... | collective-permute-start | bytes 786440 | tf_op jit(solution)/shard_map/ppermute | solution.py:24
  72.5 10.4 %collective-permute-start.9 = (bf16[256,512]{1,0:T(8,128)(2,1)S(1)}, bf16[256,512]{1,0:T(8,128)(2,1)}, u32[]{:S(2)}, u32[]{:S(2)}) collective-permute-start(bf16[256,512]{1,0:T(8,128)(2,1)S(1)} %get-tuple-element.71.refs_2_), channel_id=1, source_target_pairs={{0,2},{1,3},{2,0},{3,1},{4,6},{5,7},{6,4},{7,5},{8,10},{9,11},{10,... | collective-permute-start | bytes 786440 | tf_op jit(solution)/shard_map/ppermute | solution.py:26
  74.1 12.7 %collective-permute-start.10 = (bf16[256,512]{1,0:T(8,128)(2,1)S(1)}, bf16[256,512]{1,0:T(8,128)(2,1)S(1)}, u32[]{:S(2)}, u32[]{:S(2)}) collective-permute-start(bf16[256,512]{1,0:T(8,128)(2,1)S(1)} %get-tuple-element.70.refs_1_), channel_id=1, source_target_pairs={{0,1},{1,0},{2,3},{3,2},{4,5},{5,4},{6,7},{7,6},{8,9},{9,8},{10,11... | collective-permute-start | bytes 786440 | tf_op jit(solution)/shard_map/ppermute | solution.py:26
  74.2 12.1 %collective-permute-start.5 = (bf16[256,512]{1,0:T(8,128)(2,1)S(1)}, bf16[256,512]{1,0:T(8,128)(2,1)}, u32[]{:S(2)}, u32[]{:S(2)}) collective-permute-start(bf16[256,512]{1,0:T(8,128)(2,1)S(1)} %get-tuple-element.70.refs_1_), channel_id=1, source_target_pairs={{0,2},{1,3},{2,0},{3,1},{4,6},{5,7},{6,4},{7,5},{8,10},{9,11},{10,... | collective-permute-start | bytes 786440 | tf_op jit(solution)/shard_map/ppermute | solution.py:26
  74.8 11.6 %collective-permute-start.8 = (bf16[256,512]{1,0:T(8,128)(2,1)S(1)}, bf16[256,512]{1,0:T(8,128)(2,1)}, u32[]{:S(2)}, u32[]{:S(2)}) collective-permute-start(bf16[256,512]{1,0:T(8,128)(2,1)S(1)} %get-tuple-element.71.refs_2_), channel_id=1, source_target_pairs={{0,4},{4,0},{1,5},{5,1},{2,6},{6,2},{3,7},{7,3},{8,12},{12,8},{9,1... | collective-permute-start | bytes 786440 | tf_op jit(solution)/shard_map/ppermute | solution.py:24
  86.9 8.9 %collective-permute-start.26 = (bf16[256,512]{1,0:T(8,128)(2,1)}, bf16[256,512]{1,0:T(8,128)(2,1)S(1)}, u32[]{:S(2)}, u32[]{:S(2)}) collective-permute-start(bf16[256,512]{1,0:T(8,128)(2,1)} %collective-permute-done.8.refs_4_), channel_id=1, source_target_pairs={{0,2},{1,3},{2,0},{3,1},{4,6},{5,7},{6,4},{7,5},{8,10},{9,11},{10,... | collective-permute-start | bytes 786440 | tf_op jit(solution)/shard_map/ppermute | solution.py:26
  88.5 8.6 %collective-permute-start.6 = (bf16[256,512]{1,0:T(8,128)(2,1)}, bf16[256,512]{1,0:T(8,128)(2,1)S(1)}, u32[]{:S(2)}, u32[]{:S(2)}) collective-permute-start(bf16[256,512]{1,0:T(8,128)(2,1)} %collective-permute-done.5.refs_5_), channel_id=1, source_target_pairs={{0,4},{4,0},{1,5},{5,1},{2,6},{6,2},{3,7},{7,3},{8,12},{12,8},{9,1... | collective-permute-start | bytes 786440 | tf_op jit(solution)/shard_map/ppermute | solution.py:24
  105.3 8.6 %collective-permute-start.31 = (bf16[256,512]{1,0:T(8,128)(2,1)S(1)}, bf16[256,512]{1,0:T(8,128)(2,1)S(1)}, u32[]{:S(2)}, u32[]{:S(2)}) collective-permute-start(bf16[256,512]{1,0:T(8,128)(2,1)S(1)} %get-tuple-element.123), channel_id=1, source_target_pairs={{0,2},{1,3},{2,0},{3,1},{4,6},{5,7},{6,4},{7,5},{8,10},{9,11},{10,... | collective-permute-start | bytes 786440 | tf_op jit(solution)/shard_map/ppermute | solution.py:26
  105.9 8.3 %collective-permute-start.30 = (bf16[256,512]{1,0:T(8,128)(2,1)S(1)}, bf16[256,512]{1,0:T(8,128)(2,1)S(1)}, u32[]{:S(2)}, u32[]{:S(2)}) collective-permute-start(bf16[256,512]{1,0:T(8,128)(2,1)S(1)} %get-tuple-element.124), channel_id=1, source_target_pairs={{0,4},{4,0},{1,5},{5,1},{2,6},{6,2},{3,7},{7,3},{8,12},{12,8},{9,1... | collective-permute-start | bytes 786440 | tf_op jit(solution)/shard_map/ppermute | solution.py:24
  115.0 12.9 %collective-permute-start.33 = (bf16[512,512]{1,0:T(8,128)(2,1)S(1)}, bf16[512,512]{1,0:T(8,128)(2,1)S(1)}, u32[]{:S(2)}, u32[]{:S(2)}) collective-permute-start(bf16[512,512]{1,0:T(8,128)(2,1)S(1)} %get-tuple-element.101), channel_id=1, source_target_pairs={{0,2},{1,3},{2,0},{3,1},{4,6},{5,7},{6,4},{7,5},{8,10},{9,11},{10,... | collective-permute-start | bytes 1572872 | tf_op jit(solution)/shard_map/ppermute | solution.py:26
  116.2 12.8 %collective-permute-start.34 = (bf16[512,512]{1,0:T(8,128)(2,1)S(1)}, bf16[512,512]{1,0:T(8,128)(2,1)S(1)}, u32[]{:S(2)}, u32[]{:S(2)}) collective-permute-start(bf16[512,512]{1,0:T(8,128)(2,1)S(1)} %get-tuple-element.102), channel_id=1, source_target_pairs={{0,4},{4,0},{1,5},{5,1},{2,6},{6,2},{3,7},{7,3},{8,12},{12,8},{9,1... | collective-permute-start | bytes 1572872 | tf_op jit(solution)/shard_map/ppermute | solution.py:24
  118.7 7.9 %collective-permute-start.36 = (f32[4,4096]{1,0:T(4,128)S(1)}, f32[4,4096]{1,0:T(4,128)S(1)}, u32[]{:S(2)}, u32[]{:S(2)}) collective-permute-start(f32[4,4096]{1,0:T(4,128)S(1)} %fusion), channel_id=1, source_target_pairs={{0,16},{8,24},{16,0},{24,8},{1,17},{9,25},{17,1},{25,9},{2,18},{10... | collective-permute-start | bytes 196616 | tf_op jit(solution)/shard_map/ppermute | solution.py:449
  131.3 27.9 %all-to-all-start.2 = ((bf16[8,128,512]{2,1,0:T(8,128)(2,1)}), bf16[8,128,512]{2,1,0:T(8,128)(2,1)S(1)}, u32[]{:S(2)}, u32[]{:S(2)}) async-start(bf16[8,128,512]{2,1,0:T(8,128)(2,1)} %place_rows.1), calls=%async_computation.2 | async-start | bytes 2097152 | tf_op jit(solution)/shard_map/all_to_all | solution.py:394
  (46 other events, 353.9 us)
